TPU v7x, 32 devices: a whole 2x2x4 slice. The times are simulated.
32 devices in a mesh: dp: 4 (over z), sp: 8 (over y, x, core).
Axes of the slice: x: 2, y: 2, z: 4, core: 2. Of those that a mesh axis runs over, the one named last changes fastest.
Arguments:
- hidden_in: bfloat16 [4096, 2048], P(('dp', 'sp')), may hold values from -6 to 6
- teacher: bfloat16 [4096, 2048], P(('dp', 'sp')), may hold values from -13 to 13
- seq_lengths: int32 [4, 8], replicated, may hold values from 0 to 1024, as said below
- routes: int32 [4096, 4], P(('dp', 'sp')), may hold values from 0 to 7, all different within a row; in each aligned block of 128 rows (0 to 127, 128 to 255, ...) at most 72 rows name the same one
- attn_norm: bfloat16 [2048], replicated, may hold values from 0.5 to 1.5
- qkv_proj: bfloat16 [3, 2048, 2048], P(None, None, 'sp'), may hold values from -0.125 to 0.125
- qkv_bias: bfloat16 [3, 16, 128], P(None, 'sp'), may hold values from -0.75 to 0.75
- out_proj: bfloat16 [2048, 2048], P('sp'), may hold values from -1 to 1
- ffn_norm: bfloat16 [2048], replicated, may hold values from 0.5 to 1.5
- router: bfloat16 [2048, 8], replicated, may hold values from -0.125 to 0.125
- shared_gateup: bfloat16 [2048, 2, 5632], P(None, None, 'sp'), may hold values from -0.125 to 0.125
- shared_down: bfloat16 [5632, 2048], P('sp'), may hold values from -0.078125 to 0.078125
- shared_switch: bfloat16 [2048], replicated, may hold values from -0.125 to 0.125
- expert_gateup: bfloat16 [8, 2048, 2, 1408], P('sp'), may hold values from -0.125 to 0.125
- expert_down: bfloat16 [8, 1408, 2048], P('sp'), may hold values from -0.15625 to 0.15625
Outputs:
- output: float32 [4096, 2048], P(('dp', 'sp'))
- loss_value: float32 [], replicated
- hidden_grad: float32 [4096, 2048], P(('dp', 'sp'))
- attnnorm_grad: float32 [2048], P(('dp', 'sp'))
- qkvproj_grad: float32 [3, 2048, 2048], P(None, 'dp', 'sp')
- qkvbias_grad: float32 [3, 16, 128], P(None, 'sp', 'dp')
- outproj_grad: float32 [2048, 2048], P('sp', 'dp')
- ffnnorm_grad: float32 [2048], P(('dp', 'sp'))
- router_grad: float32 [2048, 8], P(('dp', 'sp'))
- sharedgu_grad: float32 [2048, 2, 5632], P('dp', None, 'sp')
- shareddown_grad: float32 [5632, 2048], P('sp', 'dp')
- switch_grad: float32 [2048], P(('dp', 'sp'))
- expertgu_grad: float32 [8, 2048, 2, 1408], P('sp', 'dp')
- expertdown_grad: float32 [8, 1408, 2048], P('sp', None, 'dp')
Inputs may be any that keep to these rules, and one draw needn't show every extreme that they name: `seq_lengths`: entries of a row past its last sequence are 0. Each row's sequences take ceil(len / 128) blocks of 128 slots and together exactly 1024 slots; some row holds one sequence of 1024 tokens. `routes`: within the 128 rows of one device, no expert is named by more than 72 rows.
All inputs are finite; a program needn't handle non-finite values.
Results may differ from a plain program's by a relative error of at most 0.012.
The roundings to bfloat16 on the way count: a program that leaves them out, or rounds other values in their place, can miss the bound.
Values may be sent and summed in bfloat16 or wider, within the bound.
No kernel may reach another device: no remote copies, remote signals or barrier semaphores. Data moves between devices by JAX's collectives and lax.ppermute only.
A program may use at most 320 MiB of HBM per device.

v0:
```python
import jax
import jax.numpy as jnp
from jax import lax
from jax.sharding import PartitionSpec as P

D = 2048
HD = 128
BLK = 128
PACK = 1024
MAXSEQ = 8


EPS = 1e-06
THETA = 1000000.0
FLOOR = -1e30
HIGH = lax.Precision.HIGHEST


def layout(length_row):
    blocks = (length_row + BLK - 1) // BLK
    ends = jnp.cumsum(blocks)
    starts = ends - blocks
    place = jnp.arange(PACK, dtype=jnp.int32)
    which = jnp.sum((place[:, None] // BLK >= ends[None, :]).astype(jnp.int32), axis=1)
    member = which[:, None] == jnp.arange(MAXSEQ, dtype=jnp.int32)[None, :]
    opening = jnp.sum(jnp.where(member, starts[None, :], 0), axis=1)
    seq_len = jnp.sum(jnp.where(member, length_row[None, :], 0), axis=1)
    position = place - opening * BLK
    return (which, position, position < seq_len)


def rope_tables(position):
    half_dim = HD // 2
    freq = THETA ** (-2.0 * jnp.arange(half_dim, dtype=jnp.float32) / HD)
    angle = position.astype(jnp.float32)[:, None] * freq[None, :]
    return (
        jnp.concatenate([jnp.cos(angle), jnp.cos(angle)], -1),
        jnp.concatenate([jnp.sin(angle), jnp.sin(angle)], -1),
    )


def rotate(flat_rows, cosine, sine_table):
    count = flat_rows.shape[0]
    shaped = flat_rows.reshape(count, -1, HD)
    half_dim = HD // 2
    turned = jnp.concatenate([-shaped[..., half_dim:], shaped[..., :half_dim]], -1)
    return (shaped * cosine[:, None, :] + turned * sine_table[:, None, :]).reshape(count, -1)


def rotate_back(flat_rows, cosine, sine_table):
    count = flat_rows.shape[0]
    shaped = flat_rows.reshape(count, -1, HD)
    half_dim = HD // 2
    sined = shaped * sine_table[:, None, :]
    turned = jnp.concatenate([sined[..., half_dim:], -sined[..., :half_dim]], -1)
    return (shaped * cosine[:, None, :] + turned).reshape(count, -1)


def normalize(values, gain_vec):
    inverse = lax.rsqrt(jnp.mean(values * values, axis=-1, keepdims=True) + EPS)
    return (values * inverse * gain_vec, inverse)


def norm_back(values, inverse, gain_vec, gradient):
    scaled = values * inverse
    gain_term = jnp.sum(gradient * scaled, axis=0)
    grad_scaled = gradient * gain_vec
    back = inverse * (grad_scaled - scaled * jnp.mean(grad_scaled * scaled, axis=-1, keepdims=True))
    return (back, gain_term)


def silu_slope(values):
    sig = jax.nn.sigmoid(values)
    return sig * (1.0 + values * (1.0 - sig))


def scores_block(queries, key_rows, segment, position, is_valid, start_row, count):
    heads = queries.shape[1] // HD
    end_row = start_row + count
    block_q = queries[start_row:end_row].reshape(count, heads, HD)
    block_k = key_rows[:end_row].reshape(end_row, heads, HD)
    scores = jnp.einsum(
        "qhd,khd->hqk", block_q, block_k, preferred_element_type=jnp.float32
    ) * HD ** (-0.5)
    allowed = (
        (segment[start_row:end_row, None] == segment[None, :end_row])
        & (position[None, :end_row] <= position[start_row:end_row, None])
        & is_valid[None, :end_row]
    )
    return jnp.where(allowed[None], scores, FLOOR)


def attend_forward(queries, key_rows, values, segment, position, is_valid):
    total_rows, width = queries.shape
    heads = width // HD
    block = min(512, total_rows)
    pieces = []
    totals = []
    for start_row in range(0, total_rows, block):
        scores = scores_block(queries, key_rows, segment, position, is_valid, start_row, block)
        peak = jnp.max(scores, axis=-1, keepdims=True)
        expon = jnp.exp(scores - peak)
        summed = jnp.sum(expon, axis=-1, keepdims=True)
        weights = (expon / summed).astype(jnp.bfloat16)
        block_v = values[: start_row + block].reshape(start_row + block, heads, HD)
        mixed = jnp.einsum("hqk,khd->qhd", weights, block_v, preferred_element_type=jnp.float32)
        pieces.append(mixed.reshape(block, width))
        totals.append(peak[..., 0] + jnp.log(summed[..., 0]))
    return (jnp.concatenate(pieces, 0), jnp.concatenate(totals, 1))


def attend_back(queries, key_rows, values, segment, position, is_valid, log_total, grad_mixed):
    total_rows, width = queries.shape
    heads = width // HD
    block = min(512, total_rows)
    scale = HD ** (-0.5)
    grad_q = []
    grad_k = jnp.zeros((total_rows, heads, HD), jnp.float32)
    grad_v = jnp.zeros((total_rows, heads, HD), jnp.float32)
    for start_row in range(0, total_rows, block):
        end_row = start_row + block
        scores = scores_block(queries, key_rows, segment, position, is_valid, start_row, block)
        probs = jnp.exp(scores - log_total[:, start_row:end_row, None])
        block_g = grad_mixed[start_row:end_row].reshape(block, heads, HD)
        block_q = queries[start_row:end_row].reshape(block, heads, HD)
        block_k = key_rows[:end_row].reshape(end_row, heads, HD)
        block_v = values[:end_row].reshape(end_row, heads, HD)
        grad_p = jnp.einsum("qhd,khd->hqk", block_g, block_v, preferred_element_type=jnp.float32)
        grad_s = (probs * (grad_p - jnp.sum(probs * grad_p, axis=-1, keepdims=True))).astype(
            jnp.bfloat16
        )
        grad_q.append(
            (
                jnp.einsum("hqk,khd->qhd", grad_s, block_k, preferred_element_type=jnp.float32)
                * scale
            ).reshape(block, width)
        )
        grad_k = grad_k.at[:end_row].add(
            jnp.einsum("hqk,qhd->khd", grad_s, block_q, preferred_element_type=jnp.float32) * scale
        )
        grad_v = grad_v.at[:end_row].add(
            jnp.einsum(
                "hqk,qhd->khd",
                probs.astype(jnp.bfloat16),
                block_g,
                preferred_element_type=jnp.float32,
            )
        )
    return (
        jnp.concatenate(grad_q, 0),
        grad_k.reshape(total_rows, width),
        grad_v.reshape(total_rows, width),
    )


def pack_rows(values):
    return lax.all_gather(values, "sp", axis=0, tiled=True)


def row_sums(values):
    return lax.psum_scatter(values, "sp", scatter_dimension=0, tiled=True)


def to_experts(buffer_rows):
    return lax.all_to_all(buffer_rows, "sp", split_axis=0, concat_axis=0, tiled=True)


def from_experts(buffer_rows):
    return lax.all_to_all(buffer_rows, "sp", split_axis=0, concat_axis=0, tiled=True)


def grad_projections(grad_q, grad_k, grad_v, cosine, sine_table):
    rounded_q = lax.optimization_barrier(grad_q.astype(jnp.bfloat16)).astype(jnp.float32)
    rounded_k = lax.optimization_barrier(grad_k.astype(jnp.bfloat16)).astype(jnp.float32)
    return jnp.stack(
        [
            rotate_back(rounded_q, cosine, sine_table).astype(jnp.bfloat16),
            rotate_back(rounded_k, cosine, sine_table).astype(jnp.bfloat16),
            grad_v.astype(jnp.bfloat16),
        ],
        axis=0,
    )


def on_device(
    hidden_in,
    teacher,
    seq_lengths,
    routes,
    attn_norm,
    qkv_proj,
    qkv_bias,
    out_proj,
    ffn_norm,
    router,
    shared_gateup,
    shared_down,
    shared_switch,
    expert_gateup,
    expert_down,
):
    tok_rows, width = hidden_in.shape
    sp_size = lax.axis_size("sp")
    inputs = hidden_in.astype(jnp.float32)
    length_row = lax.dynamic_index_in_dim(seq_lengths, lax.axis_index("dp"), 0, keepdims=False)
    segment, position, is_valid = layout(length_row)
    cosine, sine_table = rope_tables(position)
    offset = lax.axis_index("sp") * tok_rows
    local_valid = lax.dynamic_slice_in_dim(is_valid, offset, tok_rows).astype(jnp.float32)
    gain_one = attn_norm.astype(jnp.float32)
    normed_f, inverse_one = normalize(inputs, gain_one)
    normed = normed_f.astype(jnp.bfloat16)
    normed_pack = pack_rows(normed)
    projected = jnp.einsum(
        "td,jdc->jtc", normed_pack, qkv_proj, preferred_element_type=jnp.float32
    ) + qkv_bias.reshape(3, 1, -1).astype(jnp.float32)
    queries = rotate(projected[0], cosine, sine_table).astype(jnp.bfloat16)
    key_rows = rotate(projected[1], cosine, sine_table).astype(jnp.bfloat16)
    values = projected[2].astype(jnp.bfloat16)
    mixed, log_total = attend_forward(queries, key_rows, values, segment, position, is_valid)
    mixed_low = mixed.astype(jnp.bfloat16)
    attn_out = row_sums(jnp.dot(mixed_low, out_proj, preferred_element_type=jnp.float32))
    middle = inputs + attn_out
    gain_two = ffn_norm.astype(jnp.float32)
    normed_two_f, inverse_two = normalize(middle, gain_two)
    normed_two = normed_two_f.astype(jnp.bfloat16)
    normed_wide = normed_two.astype(jnp.float32)
    probs = jax.nn.softmax(jnp.dot(normed_two, router, preferred_element_type=jnp.float32), axis=-1)
    chosen = jnp.take_along_axis(probs, routes, axis=1)
    experts = router.shape[1]
    top_k = routes.shape[1]
    capacity = min(tok_rows, 9 * tok_rows * top_k // (8 * experts))
    assign = tok_rows * top_k
    flat_routes = routes.reshape(assign)
    onehot = (flat_routes[:, None] == jnp.arange(experts, dtype=jnp.int32)[None, :]).astype(
        jnp.int32
    )
    slot_rank = jnp.sum((jnp.cumsum(onehot, axis=0) - onehot) * onehot, axis=1)
    target = flat_routes * capacity + slot_rank
    slot_source = (
        jnp.full((experts * capacity,), assign, jnp.int32)
        .at[target]
        .set(jnp.arange(assign, dtype=jnp.int32))
    )
    slot_token = jnp.where(slot_source < assign, slot_source // top_k, tok_rows)

    def fill_slots(rows, index):
        padded = jnp.concatenate([rows, jnp.zeros((1, width), rows.dtype)], axis=0)
        return padded[index].reshape(sp_size, -1, capacity, width)

    expert_rows = to_experts(fill_slots(normed_two, slot_token))
    gate_up = jnp.einsum(
        "secd,edgf->secgf", expert_rows, expert_gateup, preferred_element_type=jnp.float32
    )
    gate_part = gate_up[..., 0, :]
    up_part = gate_up[..., 1, :]
    acted = (jax.nn.silu(gate_part) * up_part).astype(jnp.bfloat16)
    produced = jnp.einsum(
        "secf,efd->secd", acted, expert_down, preferred_element_type=jnp.float32
    ).astype(jnp.bfloat16)
    returned = from_experts(produced).reshape(experts * capacity, width)
    picked = returned[target].reshape(tok_rows, top_k, width).astype(jnp.float32)
    mixture = jnp.sum(chosen[:, :, None] * picked, axis=1)
    normed_pack_two = pack_rows(normed_two)
    shared_mid = jnp.einsum(
        "td,dgf->tgf", normed_pack_two, shared_gateup, preferred_element_type=jnp.float32
    )
    shared_gate_part = shared_mid[:, 0]
    shared_up_part = shared_mid[:, 1]
    shared_act = (jax.nn.silu(shared_gate_part) * shared_up_part).astype(jnp.bfloat16)
    shared_sum = row_sums(jnp.dot(shared_act, shared_down, preferred_element_type=jnp.float32))
    switch_vec = shared_switch.astype(jnp.float32)
    switch = jax.nn.sigmoid(jnp.dot(normed_wide, switch_vec, precision=HIGH))
    output = middle + mixture + switch[:, None] * shared_sum
    error = (output - teacher.astype(jnp.float32)) * local_valid[:, None]
    squares = lax.psum(jnp.sum(error * error), ("dp", "sp"))
    count = jnp.sum(seq_lengths).astype(jnp.float32)
    loss_value = squares / (2.0 * count * D)
    grad_shared = (switch[:, None] * error).astype(jnp.bfloat16)
    grad_switch = jnp.sum(error * shared_sum, axis=1) * switch * (1.0 - switch)
    switch_term = jnp.dot(grad_switch, normed_wide, precision=HIGH)
    grad_normed = grad_switch[:, None] * switch_vec[None, :]
    grad_shared_pack = pack_rows(grad_shared)
    grad_act = jnp.einsum(
        "td,fd->tf", grad_shared_pack, shared_down, preferred_element_type=jnp.float32
    )
    shareddown_term = jnp.einsum(
        "tf,td->fd", shared_act, grad_shared_pack, preferred_element_type=jnp.float32
    )
    grad_mid = jnp.stack(
        [
            grad_act * shared_up_part * silu_slope(shared_gate_part),
            grad_act * jax.nn.silu(shared_gate_part),
        ],
        axis=1,
    ).astype(jnp.bfloat16)
    sharedgu_term = jnp.einsum(
        "td,tgf->dgf", normed_pack_two, grad_mid, preferred_element_type=jnp.float32
    )
    grad_normed = grad_normed + row_sums(
        jnp.einsum("tgf,dgf->td", grad_mid, shared_gateup, preferred_element_type=jnp.float32)
    )
    grad_pick = (chosen[:, :, None] * error[:, None, :]).astype(jnp.bfloat16).reshape(assign, width)
    grad_chosen = jnp.sum(error[:, None, :] * picked, axis=2)
    grad_rows = to_experts(fill_slots(grad_pick, slot_source))
    grad_acted = jnp.einsum(
        "secd,efd->secf", grad_rows, expert_down, preferred_element_type=jnp.float32
    )
    expertdown_term = jnp.einsum(
        "secf,secd->efd", acted, grad_rows, preferred_element_type=jnp.float32
    )
    grad_gu = jnp.stack(
        [grad_acted * up_part * silu_slope(gate_part), grad_acted * jax.nn.silu(gate_part)], axis=-2
    ).astype(jnp.bfloat16)
    expertgu_term = jnp.einsum(
        "secd,secgf->edgf", expert_rows, grad_gu, preferred_element_type=jnp.float32
    )
    grad_back = jnp.einsum(
        "secgf,edgf->secd", grad_gu, expert_gateup, preferred_element_type=jnp.float32
    ).astype(jnp.bfloat16)
    grad_return = from_experts(grad_back).reshape(experts * capacity, width)
    grad_normed = grad_normed + jnp.sum(
        grad_return[target].reshape(tok_rows, top_k, width).astype(jnp.float32), axis=1
    )
    route_hot = (routes[:, :, None] == jnp.arange(experts, dtype=jnp.int32)[None, None, :]).astype(
        jnp.float32
    )
    grad_probs = jnp.einsum("tk,tke->te", grad_chosen, route_hot, precision=HIGH)
    grad_logits = probs * (grad_probs - jnp.sum(probs * grad_probs, axis=1, keepdims=True))
    router_term = jnp.einsum("td,te->de", normed_wide, grad_logits, precision=HIGH)
    grad_normed = grad_normed + jnp.einsum(
        "te,de->td", grad_logits, router.astype(jnp.float32), precision=HIGH
    )
    grad_middle_n, ffnnorm_term = norm_back(middle, inverse_two, gain_two, grad_normed)
    grad_middle = error + grad_middle_n
    grad_attn = grad_middle.astype(jnp.bfloat16)
    grad_attn_pack = pack_rows(grad_attn)
    grad_mixed = jnp.einsum(
        "td,cd->tc", grad_attn_pack, out_proj, preferred_element_type=jnp.float32
    ).astype(jnp.bfloat16)
    outproj_term = jnp.einsum(
        "tc,td->cd", mixed_low, grad_attn_pack, preferred_element_type=jnp.float32
    )
    grad_q, grad_k, grad_v = attend_back(
        queries, key_rows, values, segment, position, is_valid, log_total, grad_mixed
    )
    grad_proj = grad_projections(grad_q, grad_k, grad_v, cosine, sine_table)
    qkvproj_term = jnp.einsum(
        "td,jtc->jdc", normed_pack, grad_proj, preferred_element_type=jnp.float32
    )
    qkvbias_term = jnp.sum(grad_proj.astype(jnp.float32), axis=1).reshape(3, -1, HD)
    grad_normed_one = row_sums(
        jnp.einsum("jtc,jdc->td", grad_proj, qkv_proj, preferred_element_type=jnp.float32)
    )
    grad_input_n, attnnorm_term = norm_back(inputs, inverse_one, gain_one, grad_normed_one)
    hidden_grad = grad_middle + grad_input_n
    reduced = (
        lax.psum_scatter(qkvproj_term, "dp", scatter_dimension=1, tiled=True),
        lax.psum_scatter(qkvbias_term, "dp", scatter_dimension=2, tiled=True),
        lax.psum_scatter(outproj_term, "dp", scatter_dimension=1, tiled=True),
        lax.psum_scatter(sharedgu_term, "dp", scatter_dimension=0, tiled=True),
        lax.psum_scatter(shareddown_term, "dp", scatter_dimension=1, tiled=True),
        lax.psum_scatter(expertgu_term, "dp", scatter_dimension=1, tiled=True),
        lax.psum_scatter(expertdown_term, "dp", scatter_dimension=2, tiled=True),
    )
    smaller = (
        lax.psum_scatter(attnnorm_term, ("dp", "sp"), scatter_dimension=0, tiled=True),
        lax.psum_scatter(ffnnorm_term, ("dp", "sp"), scatter_dimension=0, tiled=True),
        lax.psum_scatter(router_term, ("dp", "sp"), scatter_dimension=0, tiled=True),
        lax.psum_scatter(switch_term, ("dp", "sp"), scatter_dimension=0, tiled=True),
    )
    return (
        output,
        loss_value,
        hidden_grad,
        smaller[0],
        reduced[0],
        reduced[1],
        reduced[2],
        smaller[1],
        smaller[2],
        reduced[3],
        reduced[4],
        smaller[3],
        reduced[5],
        reduced[6],
    )


def solution(mesh):
    in_specs = (
        P(("dp", "sp"), None),
        P(("dp", "sp"), None),
        P(),
        P(("dp", "sp"), None),
        P(),
        P(None, None, "sp"),
        P(None, "sp", None),
        P("sp", None),
        P(),
        P(),
        P(None, None, "sp"),
        P("sp", None),
        P(),
        P("sp", None, None, None),
        P("sp", None, None),
    )
    out_specs = (
        P(("dp", "sp"), None),
        P(),
        P(("dp", "sp"), None),
        P(("dp", "sp")),
        P(None, "dp", "sp"),
        P(None, "sp", "dp"),
        P("sp", "dp"),
        P(("dp", "sp")),
        P(("dp", "sp"), None),
        P("dp", None, "sp"),
        P("sp", "dp"),
        P(("dp", "sp")),
        P("sp", "dp", None, None),
        P("sp", None, "dp"),
    )
    return jax.shard_map(
        on_device, mesh=mesh, in_specs=in_specs, out_specs=out_specs, check_vma=False
    )
```

profile of v0, /device:TPU:0, one launch (start us, length us, event | category | flops | bytes accessed | tf_op | source)
XLA Modules:
  0.0 1882.2 jit_solution(14764451275529531058)
XLA Ops:
  18.9 32.6 %all-gather.5.cloned.1.call-done = bf16[1024,2048]{1,0:T(8,128)(2,1)} async-done(((bf16[128,2048]{1,0:T(8,128)(2,1)}), bf16[1024,2048]{1,0:T(8,128)(2,1)}) %all-gather.5.cloned.1.call-update) | async-done | bytes 4194320 | tf_op jit(solution)/shard_map/all_gather | solution.py:157
  71.8 70.8 %reduce-scatter.17.cloned.1.call-done = f32[128,2048]{1,0:T(8,128)} async-done(((f32[1024,2048]{1,0:T(8,128)}), f32[128,2048]{1,0:T(8,128)}) %reduce-scatter.17.cloned.1.call-update) | async-done | bytes 1048592 | tf_op jit(solution)/shard_map/reduce_scatter | solution.py:161
  146.3 36.6 %all-gather.7.cloned.1.call-done = bf16[1024,2048]{1,0:T(8,128)(2,1)} async-done(((bf16[128,2048]{1,0:T(8,128)(2,1)}), bf16[1024,2048]{1,0:T(8,128)(2,1)}) %all-gather.7.cloned.1.call-update) | async-done | bytes 4194320 | tf_op jit(solution)/shard_map/all_gather | solution.py:157
  217.5 53.8 %all_to_all.20 = bf16[8,1,72,2048]{3,2,1,0:T(8,128)(2,1)S(1)} all-to-all(bf16[8,1,72,2048]{3,2,1,0:T(8,128)(2,1)} %bitcast.405), channel_id=1, replica_groups=mesh['dp'=4,'sp'=8] {'sp'}, dimensions={0} | all-to-all | bytes 4718592 | tf_op jit(solution)/shard_map/all_to_all | solution.py:165
  271.4 12.6 fusion.9
  302.9 23.2 %all-to-all-done.1 = bf16[8,1,72,2048]{3,2,1,0:T(8,128)(2,1)} async-done(((bf16[8,1,72,2048]{3,2,1,0:T(8,128)(2,1)}), bf16[8,1,72,2048]{3,2,1,0:T(8,128)(2,1)}, u32[]{:S(2)}, u32[]{:S(2)}) %all-to-all-start.1) | async-done | bytes 2359328 | tf_op jit(solution)/shard_map/all_to_all | solution.py:169
  348.5 35.8 %all-gather.9.cloned.1.call-done = bf16[1024,2048]{1,0:T(8,128)(2,1)} async-done(((bf16[128,2048]{1,0:T(8,128)(2,1)}), bf16[1024,2048]{1,0:T(8,128)(2,1)}) %all-gather.9.cloned.1.call-update) | async-done | bytes 4194320 | tf_op jit(solution)/shard_map/all_gather | solution.py:157
  429.5 51.9 %all_to_all.21 = bf16[8,1,72,2048]{3,2,1,0:T(8,128)(2,1)S(1)} all-to-all(bf16[8,1,72,2048]{3,2,1,0:T(8,128)(2,1)} %bitcast.406), channel_id=1, replica_groups=mesh['dp'=4,'sp'=8] {'sp'}, dimensions={0} | all-to-all | bytes 4718592 | tf_op jit(solution)/shard_map/all_to_all | solution.py:165
  492.5 11.6 fusion.56
  515.5 22.5 %all-to-all-done.3 = bf16[8,1,72,2048]{3,2,1,0:T(8,128)(2,1)} async-done(((bf16[8,1,72,2048]{3,2,1,0:T(8,128)(2,1)}), bf16[8,1,72,2048]{3,2,1,0:T(8,128)(2,1)}, u32[]{:S(2)}, u32[]{:S(2)}) %all-to-all-start.3) | async-done | bytes 2359328 | tf_op jit(solution)/shard_map/all_to_all | solution.py:169
  563.7 32.6 %all-gather.11.cloned.1.call-done = bf16[1024,2048]{1,0:T(8,128)(2,1)} async-done(((bf16[128,2048]{1,0:T(8,128)(2,1)}), bf16[1024,2048]{1,0:T(8,128)(2,1)}) %all-gather.11.cloned.1.call-update) | async-done | bytes 4194320 | tf_op jit(solution)/shard_map/all_gather | solution.py:157
  629.6 16.1 convolution_bitcast_fusion
  654.3 12.6 convolution_bitcast_fusion.1
  666.9 11.4 fusion.12
  686.8 47.2 %reduce-scatter.39.cloned.1.call-done = f32[64,8]{1,0:T(8,128)} async-done(((f32[2048,8]{1,0:T(8,128)}), f32[64,8]{1,0:T(8,128)}) %reduce-scatter.39.cloned.1.call-update) | async-done | bytes 2064
  735.5 15.8 reduce-scatter.37.cloned.1.call-done
  752.8 71.7 %reduce-scatter.23.cloned.1.call-done = f32[128,2048]{1,0:T(8,128)} async-done(((f32[1024,2048]{1,0:T(8,128)}), f32[128,2048]{1,0:T(8,128)}) %reduce-scatter.23.cloned.1.call-update) | async-done | bytes 1048592 | tf_op jit(solution)/shard_map/reduce_scatter | solution.py:161
  826.2 44.6 %all-reduce.7 = (f32[]{:T(128)}, f32[2048]{0:T(1024)S(1)}, f32[2048]{0:T(1024)S(1)}, f32[2048]{0:T(1024)S(1)}) all-reduce(f32[]{:T(128)} %get-tuple-element.153, f32[2048]{0:T(1024)S(1)} %get-tuple-element.150, f32[2048]{0:T(1024)S(1)} %get-tuple-element.148, f32[2048]{0:T(1024)S(1)} %bitcast.446), channel_id=1, replica_groups=mesh['dp'=4,'sp'=8] {'dp','sp'}, use_global_device_ids=true, to_apply=%region_20.21 | all-reduce | flops 6145 | bytes 49160 | tf_op jit(solution)/shard_map/psum | solution.py:276
  873.2 65.3 %reduce-scatter.25.cloned.1.call-done = f32[3,512,256]{1,2,0:T(8,128)} async-done(((f32[3,2048,256]{1,2,0:T(8,128)}), f32[3,512,256]{1,2,0:T(8,128)}) %reduce-scatter.25.cloned.1.call-update) | async-done | bytes 1572880 | tf_op jit(solution)/shard_map/reduce_scatter | solution.py:358
  944.7 377.3 %reduce-scatter.33.cloned.1.call-done = f32[1,512,2,1408]{3,1,2,0:T(8,128)} async-done(((f32[1,2048,2,1408]{3,1,2,0:T(8,128)}), f32[1,512,2,1408]{3,1,2,0:T(8,128)}) %reduce-scatter.33.cloned.1.call-update) | async-done | bytes 5767184 | tf_op jit(solution)/shard_map/reduce_scatter | solution.py:363
  1331.6 97.5 %reduce-scatter.31.cloned.1.call-done = f32[704,512]{1,0:T(8,128)} async-done(((f32[704,2048]{1,0:T(8,128)}), f32[704,512]{1,0:T(8,128)}) %reduce-scatter.31.cloned.1.call-update) | async-done | bytes 1441808 | tf_op jit(solution)/shard_map/reduce_scatter | solution.py:362
  1429.0 198.4 %reduce-scatter.35.cloned.1.call-done = f32[1,1408,512]{2,1,0:T(8,128)} async-done(((f32[1,1408,2048]{2,1,0:T(8,128)}), f32[1,1408,512]{2,1,0:T(8,128)}) %reduce-scatter.35.cloned.1.call-update) | async-done | bytes 2883600 | tf_op jit(solution)/shard_map/reduce_scatter | solution.py:364
  1627.4 198.9 %reduce-scatter.29.cloned.1.call-done = f32[512,2,704]{0,2,1:T(8,128)} async-done(((f32[2048,2,704]{0,2,1:T(8,128)}), f32[512,2,704]{0,2,1:T(8,128)}) %reduce-scatter.29.cloned.1.call-update) | async-done | bytes 2883600 | tf_op jit(solution)/shard_map/reduce_scatter | solution.py:361
  1826.3 47.8 %reduce-scatter.27.cloned.1.call-done = f32[256,512]{1,0:T(8,128)} async-done(((f32[256,2048]{1,0:T(8,128)}), f32[256,512]{1,0:T(8,128)}) %reduce-scatter.27.cloned.1.call-update) | async-done | bytes 524304 | tf_op jit(solution)/shard_map/reduce_scatter | solution.py:360
  (317 shorter events, 275.6 us)
Async XLA Ops:
  7.2 44.4 %copy-start = (bf16[3,2048,256]{2,1,0:T(8,128)(2,1)S(1)}, bf16[3,2048,256]{2,1,0:T(8,128)(2,1)}, u32[]{:S(2)}) copy-start(bf16[3,2048,256]{2,1,0:T(8,128)(2,1)} %param.32) | copy-start | bytes 9437188
  7.2 44.4 %all-gather.5.cloned.1.call-start = ((), (), s32[]{:S(2)}) async-start(), calls=%async_computation.16 | async-start | bytes 4718592 | tf_op jit(solution)/shard_map/all_gather | solution.py:157
  12.0 130.5 %reduce-scatter.17.cloned.1.call-start = ((), (), s32[]{:S(2)}) async-start(), calls=%async_computation.17 | async-start | bytes 9437184 | tf_op jit(solution)/shard_map/reduce_scatter | solution.py:161
  71.1 111.8 %all-gather.7.cloned.1.call-start = ((), (), s32[]{:S(2)}) async-start(), calls=%async_computation.18 | async-start | bytes 4718592 | tf_op jit(solution)/shard_map/all_gather | solution.py:157
  71.8 120.6 %copy-start.39 = (f32[2048]{0:T(1024)}, f32[2048]{0:T(1024)S(1)}, u32[]{:S(2)}) copy-start(f32[2048]{0:T(1024)S(1)} %convert_element_type.217) | copy-start | bytes 24580
  146.1 198.3 %reduce-scatter.19.cloned.1.call-start = ((), (), s32[]{:S(2)}) async-start(), calls=%async_computation.19 | async-start | bytes 9437184 | tf_op jit(solution)/shard_map/reduce_scatter | solution.py:161
  217.5 69.1 %slice-start = ((s8[5767168]{0:T(1024)(128)(4,1)}), s8[4194304]{0:T(1024)(128)(4,1)S(1)}, s32[]{:S(2)}) async-start(s8[5767168]{0:T(1024)(128)(4,1)} %bitcast.454), calls=%async_computation.32 | async-start | bytes 8388608
  271.4 15.2 slice-start.1
  292.1 34.0 %all-to-all-start.1 = ((bf16[8,1,72,2048]{3,2,1,0:T(8,128)(2,1)}), bf16[8,1,72,2048]{3,2,1,0:T(8,128)(2,1)}, u32[]{:S(2)}, u32[]{:S(2)}) async-start(bf16[8,1,72,2048]{3,2,1,0:T(8,128)(2,1)} %fusion.53), calls=%async_computation.2 | async-start | bytes 4718592 | tf_op jit(solution)/shard_map/all_to_all | solution.py:169
  296.6 87.7 %all-gather.9.cloned.1.call-start = ((), (), s32[]{:S(2)}) async-start(), calls=%async_computation.20 | async-start | bytes 4718592 | tf_op jit(solution)/shard_map/all_gather | solution.py:157
  348.2 207.5 %reduce-scatter.21.cloned.1.call-start = ((), (), s32[]{:S(2)}) async-start(), calls=%async_computation.21 | async-start | bytes 9437184 | tf_op jit(solution)/shard_map/reduce_scatter | solution.py:161
  504.1 33.8 %all-to-all-start.3 = ((bf16[8,1,72,2048]{3,2,1,0:T(8,128)(2,1)}), bf16[8,1,72,2048]{3,2,1,0:T(8,128)(2,1)}, u32[]{:S(2)}, u32[]{:S(2)}) async-start(bf16[8,1,72,2048]{3,2,1,0:T(8,128)(2,1)} %fusion.56), calls=%async_computation.6 | async-start | bytes 4718592 | tf_op jit(solution)/shard_map/all_to_all | solution.py:169
  508.5 87.8 %all-gather.11.cloned.1.call-start = ((), (), s32[]{:S(2)}) async-start(), calls=%async_computation.22 | async-start | bytes 4718592 | tf_op jit(solution)/shard_map/all_gather | solution.py:157
  560.3 173.7 %reduce-scatter.39.cloned.1.call-start = ((), (), s32[]{:S(2)}) async-start(), calls=%async_computation.31 | async-start | bytes 1081344
  563.2 188.1 %reduce-scatter.37.cloned.1.call-start = ((), (), s32[]{:S(2)}) async-start(), calls=%async_computation.30 | async-start | bytes 81920
  613.2 211.3 %reduce-scatter.23.cloned.1.call-start = ((), (), s32[]{:S(2)}) async-start(), calls=%async_computation.23 | async-start | bytes 9437184 | tf_op jit(solution)/shard_map/reduce_scatter | solution.py:161
  620.5 318.1 %reduce-scatter.25.cloned.1.call-start = ((), (), s32[]{:S(2)}) async-start(), calls=%async_computation.24 | async-start | bytes 7864320 | tf_op jit(solution)/shard_map/reduce_scatter | solution.py:358
  629.5 692.4 %reduce-scatter.33.cloned.1.call-start = ((), (), s32[]{:S(2)}) async-start(), calls=%async_computation.28 | async-start | bytes 28835840 | tf_op jit(solution)/shard_map/reduce_scatter | solution.py:363
  645.7 783.4 %reduce-scatter.31.cloned.1.call-start = ((), (), s32[]{:S(2)}) async-start(), calls=%async_computation.27 | async-start | bytes 7208960 | tf_op jit(solution)/shard_map/reduce_scatter | solution.py:362
  654.0 973.4 %reduce-scatter.35.cloned.1.call-start = ((), (), s32[]{:S(2)}) async-start(), calls=%async_computation.29 | async-start | bytes 14417920 | tf_op jit(solution)/shard_map/reduce_scatter | solution.py:364
  666.9 1159.4 %reduce-scatter.29.cloned.1.call-start = ((), (), s32[]{:S(2)}) async-start(), calls=%async_computation.26 | async-start | bytes 14417920 | tf_op jit(solution)/shard_map/reduce_scatter | solution.py:361
  678.4 146.1 %copy-start.37 = (f32[2048]{0:T(1024)S(1)}, f32[2048]{0:T(1024)}, u32[]{:S(2)}) copy-start(f32[2048]{0:T(1024)} %copy-done.36) | copy-start | bytes 24580
  678.4 146.1 %copy-start.52 = (f32[128]{0:T(128)S(1)}, f32[128]{0:T(128)}, u32[]{:S(2)}) copy-start(f32[128]{0:T(128)} %copy-done.51) | copy-start | bytes 1540
  678.4 1195.7 %reduce-scatter.27.cloned.1.call-start = ((), (), s32[]{:S(2)}) async-start(), calls=%async_computation.25 | async-start | bytes 2621440 | tf_op jit(solution)/shard_map/reduce_scatter | solution.py:360
  (59 other events, 147.0 us)
Sparse Core Ops, SparseCore 0:
  12.1 39.4 all-gather.4
  71.2 71.2 reduce-scatter.16
  146.2 36.6 all-gather.6
  202.3 91.4 reduce-scatter.18
  348.4 35.8 all-gather.8
  405.7 96.4 reduce-scatter.20
  560.5 35.8 all-gather.10
  599.2 134.7 reduce-scatter.38
  736.3 14.9 reduce-scatter.36
  755.0 69.4 reduce-scatter.22
  826.8 111.7 reduce-scatter.24
  940.8 381.1 reduce-scatter.32
  1325.0 104.0 reduce-scatter.30
  1431.9 195.4 reduce-scatter.34
  1630.3 195.9 reduce-scatter.28
  1829.1 44.8 reduce-scatter.26
where the time goes:
time: 1890 us; the launch traced here: 1880 us
  waiting for transfers between devices  1370 us (72%)
  matrix products  176 us (9%)
  blocking collectives  150 us (8%)
  local copies, waits for them, and re-layouts  98.8 us (5%)
  other arithmetic  53.6 us (3%)
    reduce_scatter x1, waiting for transfers between devices, on_device(): lax.psum_scatter(expertgu_term, 'dp', scatter_dimension=1, tiled=True)  377 us
    reduce_scatter x1, waiting for transfers between devices, on_device(): lax.psum_scatter(sharedgu_term, 'dp', scatter_dimension=0, tiled=True)  199 us
    reduce_scatter x1, waiting for transfers between devices, on_device(): lax.psum_scatter(expertdown_term, 'dp', scatter_dimension=2, tiled=True)  198 us
    reduce_scatter x4, waiting for transfers between devices, row_sums(): return lax.psum_scatter(values, 'sp', scatter_dimension=0, tiled=True)  142 us
    all_gather x4, waiting for transfers between devices, pack_rows(): return lax.all_gather(values, 'sp', axis=0, tiled=True)  138 us
    all_to_all x2, blocking collectives, to_experts(): lax.all_to_all(buffer_rows, 'sp', split_axis=0, concat_axis=0, tiled=True)  106 us
    reduce_scatter x1, waiting for transfers between devices, on_device(): lax.psum_scatter(shareddown_term, 'dp', scatter_dimension=1, tiled=True)  97.5 us
    reduce_scatter x1, waiting for transfers between devices, on_device(): lax.psum_scatter(qkvproj_term, 'dp', scatter_dimension=1, tiled=True)  65.3 us
  transfers between devices with their start and end apart: 18, of which 16 were waited for; matrix products, arithmetic and copies ran while one was open for 13% of the time, Pallas kernels for 0%

commit v1 on v0

v1 whole, which is shorter than its diff:
```python
import jax
import jax.numpy as jnp
from jax import lax
from jax.sharding import PartitionSpec as P

D = 2048
HD = 128
BLK = 128
MAXSEQ = 8

EPS = 1e-06
THETA = 1000000.0
FLOOR = -1e30
HIGH = lax.Precision.HIGHEST
BF = jnp.bfloat16
F32 = jnp.float32

ORDER = (0, 2, 4, 6, 1, 3, 5, 7)


def barrier(*values):
    return lax.optimization_barrier(values)


def dot(left, right, dims, dtype=F32):
    return lax.dot_general(left, right, (dims, ((), ())), preferred_element_type=F32).astype(dtype)


def swap(values, distance):
    return lax.ppermute(values, "sp", [(i, i ^ distance) for i in range(8)])


def gather_rows(own):
    half = own.shape[0] // 2
    over_x, over_y, over_c = swap(own, 2), swap(own, 4), swap(own, 1)
    far_top, far_bottom = swap(over_y[:half], 2), swap(over_x[half:], 4)
    far = jnp.concatenate([far_top, far_bottom], 0)
    rest = [swap(over_x, 1), swap(over_y, 1), swap(far, 1)]
    return jnp.concatenate([own, over_x, over_y, far, over_c] + rest, 0)


def gather_small(own):
    held = own[None]
    for distance in (2, 4, 1):
        held = jnp.concatenate([held, swap(held, distance)], 0)
    return held


def sum_small(parts):
    for distance in (1, 4, 2):
        keep = parts.shape[0] // 2
        parts = parts[:keep] + swap(parts[keep:], distance)
    return parts[0]


def sum_rows(upper, lower):
    rows = lower.shape[0] // 4
    half = rows // 2
    got = swap(upper, 1)
    chip = lower.astype(F32) + got.astype(F32)
    low = chip.astype(BF)
    own, over_x, over_y, far = (slice(k * rows, (k + 1) * rows) for k in range(4))
    low_x, low_y, low_far = low[over_x], low[over_y], low[far]
    from_x = swap(jnp.concatenate([low_far[:half], low_x[:half]], 0), 2)
    from_y = swap(jnp.concatenate([low_far[half:], low_y[half:]], 0), 4)
    pass_y = (chip[over_y][:half] + from_x[:half].astype(F32)).astype(BF)
    pass_x = (chip[over_x][half:] + from_y[:half].astype(F32)).astype(BF)
    last_y, last_x = swap(pass_y, 4), swap(pass_x, 2)
    mine = chip[own]
    top = mine[:half] + from_x[half:].astype(F32) + last_y.astype(F32)
    bottom = mine[half:] + from_y[half:].astype(F32) + last_x.astype(F32)
    return jnp.concatenate([top, bottom], 0)


def sum_groups(grads, dim):
    return lax.psum_scatter(grads, "dp", scatter_dimension=dim, tiled=True).astype(F32)


def shift_groups(blocks):
    size = lax.axis_size("dp")
    me = lax.axis_index("dp")
    pick = lambda k: lax.dynamic_index_in_dim(blocks, (me + k) % size, 0, keepdims=False)
    total = pick(0)
    for k in range(1, size):
        total = total + lax.ppermute(pick(k), "dp", [(i, (i + k) % size) for i in range(size)])
    return total


def sum_everywhere(values):
    for distance in (1, 2, 4):
        values = values + swap(values, distance)
    size = lax.axis_size("dp")
    step = 1
    while step < size:
        values = values + lax.ppermute(values, "dp", [(i, i ^ step) for i in range(size)])
        step *= 2
    return values


def layout(length_row, place):
    blocks = (length_row + BLK - 1) // BLK
    ends = jnp.cumsum(blocks)
    starts = ends - blocks
    which = jnp.sum((place[:, None] // BLK >= ends[None, :]).astype(jnp.int32), axis=1)
    member = which[:, None] == jnp.arange(length_row.shape[0], dtype=jnp.int32)[None, :]
    opening = jnp.sum(jnp.where(member, starts[None, :], 0), axis=1)
    seq_len = jnp.sum(jnp.where(member, length_row[None, :], 0), axis=1)
    position = place - opening * BLK
    return (which, position, position < seq_len)


def rope_tables(position):
    half_dim = HD // 2
    freq = THETA ** (-2.0 * jnp.arange(half_dim, dtype=F32) / HD)
    angle = position.astype(F32)[:, None] * freq[None, :]
    return (
        jnp.concatenate([jnp.cos(angle), jnp.cos(angle)], -1),
        jnp.concatenate([jnp.sin(angle), jnp.sin(angle)], -1),
    )


def rotate(flat_rows, cosine, sine_table):
    count = flat_rows.shape[0]
    shaped = flat_rows.reshape(count, -1, HD)
    half_dim = HD // 2
    turned = jnp.concatenate([-shaped[..., half_dim:], shaped[..., :half_dim]], -1)
    return (shaped * cosine[:, None, :] + turned * sine_table[:, None, :]).reshape(count, -1)


def rotate_back(flat_rows, cosine, sine_table):
    count = flat_rows.shape[0]
    shaped = flat_rows.reshape(count, -1, HD)
    half_dim = HD // 2
    sined = shaped * sine_table[:, None, :]
    turned = jnp.concatenate([sined[..., half_dim:], -sined[..., :half_dim]], -1)
    return (shaped * cosine[:, None, :] + turned).reshape(count, -1)


def normalize(values, gain_vec):
    inverse = lax.rsqrt(jnp.mean(values * values, axis=-1, keepdims=True) + EPS)
    return (values * inverse * gain_vec, inverse)


def norm_back(values, inverse, gain_vec, gradient):
    scaled = values * inverse
    gain_term = jnp.sum(gradient * scaled, axis=0)
    grad_scaled = gradient * gain_vec
    back = inverse * (grad_scaled - scaled * jnp.mean(grad_scaled * scaled, axis=-1, keepdims=True))
    return (back, gain_term)


def silu_slope(values):
    sig = jax.nn.sigmoid(values)
    return sig * (1.0 + values * (1.0 - sig))


def scores_of(queries, key_rows, allowed):
    scores = dot(queries, key_rows, ((1,), (1,))) * HD ** (-0.5)
    return jnp.where(allowed, scores, FLOOR)


def attend_forward(queries, key_rows, values, allowed):
    pieces, totals = [], []
    for start in range(0, queries.shape[1], HD):
        head = slice(start, start + HD)
        scores = scores_of(queries[:, head], key_rows[:, head], allowed)
        peak = jnp.max(scores, axis=-1, keepdims=True)
        expon = jnp.exp(scores - peak)
        summed = jnp.sum(expon, axis=-1, keepdims=True)
        weights = (expon / summed).astype(BF)
        pieces.append(dot(weights, values[:, head], ((1,), (0,)), BF))
        totals.append(peak + jnp.log(summed))
    return (jnp.concatenate(pieces, 1), totals)


def attend_back(queries, key_rows, values, allowed, totals, grad_mixed):
    scale = HD ** (-0.5)
    grads = ([], [], [])
    for start, total in zip(range(0, queries.shape[1], HD), totals):
        head = slice(start, start + HD)
        block_q, block_k, block_g = queries[:, head], key_rows[:, head], grad_mixed[:, head]
        probs = jnp.exp(scores_of(block_q, block_k, allowed) - total)
        grad_p = dot(block_g, values[:, head], ((1,), (1,)))
        grad_s = (probs * (grad_p - jnp.sum(probs * grad_p, axis=-1, keepdims=True))).astype(BF)
        grads[0].append((dot(grad_s, block_k, ((1,), (0,))) * scale).astype(BF))
        grads[1].append((dot(grad_s, block_q, ((0,), (0,))) * scale).astype(BF))
        grads[2].append(dot(probs.astype(BF), block_g, ((0,), (0,)), BF))
    return tuple(jnp.concatenate(g, 1) for g in grads)


def on_device(
    hidden_in,
    teacher,
    seq_lengths,
    routes,
    attn_norm,
    qkv_proj,
    qkv_bias,
    out_proj,
    ffn_norm,
    router,
    shared_gateup,
    shared_down,
    shared_switch,
    expert_gateup,
    expert_down,
):
    tok_rows, width = hidden_in.shape
    sp_size = lax.axis_size("sp")
    dp_size = lax.axis_size("dp")
    me = lax.axis_index("sp")
    total_rows = tok_rows * sp_size
    lower_rows = total_rows // 2
    experts = router.shape[1]
    top_k = routes.shape[1]
    capacity = sp_size * min(tok_rows, 9 * tok_rows * top_k // (8 * experts))

    inputs = hidden_in.astype(F32)
    gain_one = attn_norm.astype(F32)
    normed_f, inverse_one = normalize(inputs, gain_one)
    normed_all = gather_rows(normed_f.astype(BF))
    route_all = gather_small(routes.T)

    owners = me ^ jnp.array(ORDER, jnp.int32)
    place = (owners[:, None] * tok_rows + jnp.arange(tok_rows, dtype=jnp.int32)[None, :]).reshape(-1)
    length_row = lax.dynamic_index_in_dim(seq_lengths, lax.axis_index("dp"), 0, keepdims=False)
    segment, position, is_valid = layout(length_row, place)
    cosine, sine_table = rope_tables(position)
    local_valid = is_valid[:tok_rows].astype(F32)
    allowed = (
        (segment[:, None] == segment[None, :])
        & (position[None, :] <= position[:, None])
        & is_valid[None, :]
    )

    mask = jnp.any(route_all == me, axis=1).reshape(total_rows)
    slot = jnp.cumsum(mask.astype(jnp.int32)) - 1
    slot = jnp.where(mask, slot, -1)
    pick = (slot[None, :] == jnp.arange(capacity, dtype=jnp.int32)[:, None]).astype(BF)

    bias = qkv_bias.reshape(3, 1, -1).astype(F32)
    projected = [dot(normed_all, qkv_proj[j], ((1,), (0,))) + bias[j] for j in range(3)]
    queries = rotate(projected[0], cosine, sine_table).astype(BF)
    key_rows = rotate(projected[1], cosine, sine_table).astype(BF)
    values = projected[2].astype(BF)
    mixed, totals = attend_forward(queries, key_rows, values, allowed)
    upper = dot(mixed[lower_rows:], out_proj, ((1,), (0,)), BF)
    lower = dot(mixed[:lower_rows], out_proj, ((1,), (0,)), BF)
    middle = inputs + sum_rows(upper, lower)

    gain_two = ffn_norm.astype(F32)
    normed_two_f, inverse_two = normalize(middle, gain_two)
    normed_two = normed_two_f.astype(BF)
    two_all = gather_rows(normed_two)

    heads_in = jnp.concatenate([router, shared_switch[:, None]], axis=1)
    logits = dot(two_all, heads_in, ((1,), (0,)))
    probs = jax.nn.softmax(logits[:, :experts], axis=-1)
    switch = jax.nn.sigmoid(logits[:, experts:])
    is_me = (jnp.arange(experts) == me).astype(F32)
    share = jnp.sum(probs * is_me[None, :], axis=1) * mask.astype(F32)
    share_rows = jnp.sum(pick.astype(F32) * share[None, :], axis=1, keepdims=True)

    gate_w, up_w = expert_gateup[0, :, 0, :], expert_gateup[0, :, 1, :]
    down_w = expert_down[0]
    rows_in = dot(pick, two_all, ((1,), (0,)), BF)
    gate_e = dot(rows_in, gate_w, ((1,), (0,)))
    up_e = dot(rows_in, up_w, ((1,), (0,)))
    acted_e = (jax.nn.silu(gate_e) * up_e).astype(BF)
    made = dot(acted_e, down_w, ((1,), (0,)), BF)

    gate_sw, up_sw = shared_gateup[:, 0, :], shared_gateup[:, 1, :]
    gate_s = dot(two_all, gate_sw, ((1,), (0,)))
    up_s = dot(two_all, up_sw, ((1,), (0,)))
    acted_s = (jax.nn.silu(gate_s) * up_s).astype(BF)

    def ffn_part(rows):
        shared = dot(acted_s[rows], shared_down, ((1,), (0,)))
        routed = dot(pick[:, rows], made, ((0,), (0,)))
        return (switch[rows] * shared + share[rows, None] * routed).astype(BF)

    upper_half, lower_half = slice(lower_rows, None), slice(0, lower_rows)
    ffn_upper = ffn_part(upper_half)
    ffn_lower = ffn_part(lower_half)
    output = middle + sum_rows(ffn_upper, ffn_lower)

    error = (output - teacher.astype(F32)) * local_valid[:, None]
    squares = sum_everywhere(jnp.full((8, 128), jnp.sum(error * error), F32))[0, 0]
    count = jnp.sum(seq_lengths).astype(F32)
    loss_value = squares / (2.0 * count * D)

    error_all = gather_rows(error.astype(BF))
    rows_g = dot(pick, error_all, ((1,), (0,)))
    grad_made = (share_rows * rows_g).astype(BF)
    grad_acted = dot(grad_made, down_w, ((1,), (1,)))
    gain_rows = jnp.sum(acted_e.astype(F32) * grad_acted, axis=1, keepdims=True)
    grad_gate_e = (grad_acted * up_e * silu_slope(gate_e)).astype(BF)
    grad_up_e = (grad_acted * jax.nn.silu(gate_e)).astype(BF)
    gate_term = dot(rows_in, grad_gate_e, ((0,), (0,)), BF)
    up_term = dot(rows_in, grad_up_e, ((0,), (0,)), BF)
    down_term = dot(acted_e, grad_made, ((0,), (0,)), BF)
    expert_grads = (sum_groups(gate_term, 0), sum_groups(up_term, 0), sum_groups(down_term, 1))

    grad_shared = (switch * error_all.astype(F32)).astype(BF)
    grad_act_s = dot(grad_shared, shared_down, ((1,), (1,)))
    switch_part = jnp.sum(acted_s.astype(F32) * grad_act_s, axis=1)
    grad_gate_s = (grad_act_s * up_s * silu_slope(gate_s)).astype(BF)
    grad_up_s = (grad_act_s * jax.nn.silu(gate_s)).astype(BF)

    back_e = (dot(grad_gate_e, gate_w, ((1,), (1,))) + dot(grad_up_e, up_w, ((1,), (1,)))).astype(BF)

    def back_part(rows):
        return (
            dot(grad_gate_s[rows], gate_sw, ((1,), (1,)))
            + dot(grad_up_s[rows], up_sw, ((1,), (1,)))
            + dot(pick[:, rows], back_e, ((0,), (0,)))
        ).astype(BF)

    back_upper = back_part(upper_half)
    back_lower = back_part(lower_half)
    gain_tokens = jnp.sum(pick.astype(F32) * gain_rows, axis=0)
    scalars = jnp.concatenate(
        [gain_tokens[None, :] * is_me[:, None], switch_part[None, :], jnp.zeros((7, total_rows), F32)], axis=0
    )
    scalars = sum_small(scalars.reshape(16, sp_size, tok_rows).transpose(1, 0, 2))
    gains, switch_sum = scalars[:experts].T, scalars[experts]
    my_probs, my_switch = probs[:tok_rows], switch[:tok_rows, 0]
    grad_switch = switch_sum * (1.0 - my_switch)
    grad_logits = gains - my_probs * jnp.sum(gains, axis=1, keepdims=True)
    steer = jnp.concatenate([grad_logits, grad_switch[:, None]], axis=1)
    grad_normed = sum_rows(back_upper, back_lower) + jnp.einsum(
        "te,de->td", steer, heads_in.astype(F32), precision=HIGH
    )
    steer_term = jnp.einsum("te,td->ed", steer, normed_two.astype(F32), precision=HIGH)
    grad_middle_n, ffnnorm_term = norm_back(middle, inverse_two, gain_two, grad_normed)
    grad_middle = error + grad_middle_n

    shared_terms = (
        dot(two_all, grad_gate_s, ((0,), (0,)), BF),
        dot(two_all, grad_up_s, ((0,), (0,)), BF),
        dot(acted_s, grad_shared, ((0,), (0,)), BF),
    )

    attn_all = gather_rows(grad_middle.astype(BF))
    grad_mixed = dot(attn_all, out_proj, ((1,), (1,)), BF)
    grad_q, grad_k, grad_v = attend_back(
        queries, key_rows, values, allowed, totals, grad_mixed
    )
    grad_proj = (
        rotate_back(grad_q.astype(F32), cosine, sine_table).astype(BF),
        rotate_back(grad_k.astype(F32), cosine, sine_table).astype(BF),
        grad_v,
    )

    def input_part(rows):
        return sum(dot(grad_proj[j][rows], qkv_proj[j], ((1,), (1,))) for j in range(3)).astype(BF)

    input_upper = input_part(upper_half)
    input_lower = input_part(lower_half)
    grad_normed_one = sum_rows(input_upper, input_lower)
    grad_input_n, attnnorm_term = norm_back(inputs, inverse_one, gain_one, grad_normed_one)
    hidden_grad = grad_middle + grad_input_n
    outproj_term = dot(mixed, attn_all, ((0,), (0,)), BF)
    qkv_terms = jnp.stack([dot(normed_all, g, ((0,), (0,)), BF) for g in grad_proj], 0)
    bias_term = jnp.stack([jnp.sum(g.astype(F32), axis=0) for g in grad_proj], 0)

    shared_grads = (
        sum_groups(shared_terms[0], 0),
        sum_groups(shared_terms[1], 0),
        sum_groups(shared_terms[2], 1),
    )
    outproj_grad = sum_groups(outproj_term, 1)
    qkvproj_grad = sum_groups(qkv_terms, 1)

    small = jnp.concatenate([attnnorm_term[None], ffnnorm_term[None], steer_term], axis=0)
    kinds = small.shape[0]
    cell = width // (dp_size * sp_size)
    small = small.reshape(kinds, dp_size, sp_size, cell).transpose(2, 1, 0, 3)[owners]
    small = sum_small(small.reshape(sp_size, dp_size, kinds * cell))
    pairs = bias_term.reshape(-1, HD)
    bias_cells = pairs.reshape(pairs.shape[0], dp_size, -1).transpose(1, 0, 2).reshape(dp_size, -1)
    small = shift_groups(jnp.concatenate([small, bias_cells], axis=1))
    gains_out = small[: kinds * cell].reshape(kinds, cell)
    qkvbias_grad = small[kinds * cell :].reshape(3, -1, HD // dp_size)
    return (
        output,
        loss_value,
        hidden_grad,
        gains_out[0],
        qkvproj_grad,
        qkvbias_grad,
        outproj_grad,
        gains_out[1],
        gains_out[2 : 2 + experts].T,
        jnp.stack(shared_grads[:2], axis=1),
        shared_grads[2],
        gains_out[2 + experts],
        jnp.stack(expert_grads[:2], axis=1)[None],
        expert_grads[2][None],
    )


def solution(mesh):
    in_specs = (
        P(("dp", "sp"), None),
        P(("dp", "sp"), None),
        P(),
        P(("dp", "sp"), None),
        P(),
        P(None, None, "sp"),
        P(None, "sp", None),
        P("sp", None),
        P(),
        P(),
        P(None, None, "sp"),
        P("sp", None),
        P(),
        P("sp", None, None, None),
        P("sp", None, None),
    )
    out_specs = (
        P(("dp", "sp"), None),
        P(),
        P(("dp", "sp"), None),
        P(("dp", "sp")),
        P(None, "dp", "sp"),
        P(None, "sp", "dp"),
        P("sp", "dp"),
        P(("dp", "sp")),
        P(("dp", "sp"), None),
        P("dp", None, "sp"),
        P("sp", "dp"),
        P(("dp", "sp")),
        P("sp", "dp", None, None),
        P("sp", None, "dp"),
    )
    return jax.shard_map(
        on_device, mesh=mesh, in_specs=in_specs, out_specs=out_specs, check_vma=False
    )
```

time: 1890 us -> 860 us (0.46)
  waiting for transfers between devices: 1370 us -> 463 us
  blocking collectives: 150 us -> 0 us
  starting transfers between devices: 11.4 us -> 56.3 us
  local copies, waits for them, and re-layouts: 98.8 us -> 58.3 us
  matrix products: 176 us -> 196 us
    reduce_scatter x10 -> x8, waiting for transfers between devices: 1130 us -> 304 us  [sum_groups(): lax.psum_scatter(grads, 'dp', scatter_dimension=dim, tiled=True).astype(F32)]
    ppermute x0 -> x69, waiting for transfers between devices: none -> 159 us  [the longest x64 151 us: swap(): return lax.ppermute(values, 'sp', [(i, i ^ distance) for i in range(8)])]
    all_gather x4 -> x0, waiting for transfers between devices: 138 us -> none  [pack_rows(): return lax.all_gather(values, 'sp', axis=0, tiled=True)]
    all_to_all x2 -> x0, blocking collectives: 106 us -> none  [to_experts(): lax.all_to_all(buffer_rows, 'sp', split_axis=0, concat_axis=0, tiled=True)]
    unnamed x18 -> x8, waiting for transfers between devices: 63.3 us -> 0.13 us
    ppermute x0 -> x69, starting transfers between devices: none -> 55.2 us  [the longest x64 48.8 us: swap(): return lax.ppermute(values, 'sp', [(i, i ^ distance) for i in range(8)])]
    all_to_all x2 -> x0, waiting for transfers between devices: 45.6 us -> none  [from_experts(): lax.all_to_all(buffer_rows, 'sp', split_axis=0, concat_axis=0, tiled=True)]
    psum x1 -> x0, blocking collectives: 44.6 us -> none  [on_device(): squares = lax.psum(jnp.sum(error * error), ('dp', 'sp'))]
  transfers between devices with their start and end apart: 18 -> 77, of which waited for: 16 -> 44; matrix products, arithmetic and copies ran while one was open for 13% -> 25% of each run, Pallas kernels for 0% -> 0%
where the time goes in v1:
time: 860 us; the launch traced here: 850 us
  waiting for transfers between devices  463 us (54%)
  matrix products  196 us (23%)
  local copies, waits for them, and re-layouts  58.3 us (7%)
  other arithmetic  57.3 us (7%)
  starting transfers between devices  56.3 us (7%)
  between operations  19 us (2%)
    reduce_scatter x8, waiting for transfers between devices, sum_groups(): lax.psum_scatter(grads, 'dp', scatter_dimension=dim, tiled=True).astype(F32)  304 us
    dot_general x56, matrix products, dot(): lax.dot_general(left, right, (dims, ((), ())), preferred_element_type=F32)  193 us
    ppermute x64, waiting for transfers between devices, swap(): return lax.ppermute(values, 'sp', [(i, i ^ distance) for i in range(8)])  151 us
    ppermute x64, starting transfers between devices, swap(): return lax.ppermute(values, 'sp', [(i, i ^ distance) for i in range(8)])  48.8 us
    unnamed x234, local copies, waits for them, and re-layouts  31.4 us
    slice x1, local copies, waits for them, and re-layouts, on_device(): gate_w, up_w = (expert_gateup[0, :, 0, :], expert_gateup[0, :, 1, :])  17.8 us
  transfers between devices with their start and end apart: 77, of which 44 were waited for; matrix products, arithmetic and copies ran while one was open for 25% of the time, Pallas kernels for 0%

profile of v1, /device:TPU:0, one launch (start us, length us, event | category | flops | bytes accessed | tf_op | source)
XLA Modules:
  0.0 849.9 jit_solution(18075385737827090641)
XLA Ops:
  21.0 6.3 collective-permute-done.1
  66.1 17.8 %fusion.205 = (bf16[1,2048,1,1408]{3,2,1,0:T(2,128)(2,1)}, bf16[1,2048,1,1408]{3,2,1,0:T(2,128)(2,1)}) fusion(bf16[1,2048,2,1408]{3,2,1,0:T(2,128)(2,1)S(1)} %bitcast.247), kind=kLoop, calls=%fused_computation.443 | loop fusion | bytes 23068672 | tf_op jit(solution)/shard_map/slice | solution.py:264
  87.1 11.6 %collective-permute-done.11 = bf16[128,2048]{1,0:T(8,128)(2,1)S(1)} collective-permute-done((bf16[128,2048]{1,0:T(8,128)(2,1)S(1)}, bf16[128,2048]{1,0:T(8,128)(2,1)S(1)}, u32[]{:S(2)}, u32[]{:S(2)}) %collective-permute-start.11) | collective-permute-done | bytes 524320 | tf_op jit(solution)/shard_map/ppermute | solution.py:30
  118.2 9.0 %collective-permute-done.14 = bf16[128,2048]{1,0:T(8,128)(2,1)S(1)} collective-permute-done((bf16[128,2048]{1,0:T(8,128)(2,1)S(1)}, bf16[128,2048]{1,0:T(8,128)(2,1)S(1)}, u32[]{:S(2)}, u32[]{:S(2)}) %collective-permute-start.14) | collective-permute-done | bytes 524320 | tf_op jit(solution)/shard_map/ppermute | solution.py:30
  145.5 8.2 multiply_convert_fusion.9
  153.8 7.4 fusion.32
  161.2 7.9 multiply_convert_fusion.6
  169.1 7.8 fusion.9
  189.9 12.1 %collective-permute-done.25 = bf16[128,2048]{1,0:T(8,128)(2,1)S(1)} collective-permute-done((bf16[128,2048]{1,0:T(8,128)(2,1)S(1)}, bf16[128,2048]{1,0:T(8,128)(2,1)S(1)}, u32[]{:S(2)}, u32[]{:S(2)}) %collective-permute-start.25) | collective-permute-done | bytes 524320 | tf_op jit(solution)/shard_map/ppermute | solution.py:30
  203.6 6.4 collective-permute-done.26
  220.8 9.6 %collective-permute-done.35 = bf16[128,2048]{1,0:T(8,128)(2,1)S(1)} collective-permute-done((bf16[128,2048]{1,0:T(8,128)(2,1)S(1)}, bf16[128,2048]{1,0:T(8,128)(2,1)S(1)}, u32[]{:S(2)}, u32[]{:S(2)}) %collective-permute-start.35) | collective-permute-done | bytes 524320 | tf_op jit(solution)/shard_map/ppermute | solution.py:30
  257.0 11.8 %multiply_convert_fusion.4 = (bf16[576,1408]{1,0:T(8,128)(2,1)}, bf16[576,1408]{1,0:T(8,128)(2,1)S(1)}, f32[576]{0:T(1024)S(1)}) fusion(f32[576,1408]{1,0:T(8,128)} %fusion.32, f32[576,1408]{1,0:T(8,128)} %get-tuple-element.173, bf16[576,1408]{1,0:T(8,128)(2,1)} %copy-done.87, bf16[576,2048]{1,0:T(8,128)(2,1)} %multiply_convert_fusion.1, ...), kind=kOutput, calls=%fused_computation.42 | convolution fusion | flops 3334864384 | bytes 19482880 | tf_op jit(solution)/shard_map/dot_general | solution.py:26
  276.8 10.6 %fusion.31 = f32[576,2048]{1,0:T(8,128)} fusion(bf16[576,1408]{1,0:T(8,128)(2,1)S(1)} %get-tuple-element.101, bf16[1,2048,1,1408]{3,2,1,0:T(2,128)(2,1)} %get-tuple-element.98), kind=kOutput, calls=%fused_computation.90 | convolution fusion | flops 3321888768 | bytes 12107776 | tf_op jit(solution)/shard_map/dot_general | solution.py:26
  287.4 10.2 %add_convert_fusion = bf16[576,2048]{1,0:T(8,128)(2,1)S(1)} fusion(f32[576,2048]{1,0:T(8,128)} %fusion.31, bf16[576,1408]{1,0:T(8,128)(2,1)} %get-tuple-element.100, bf16[1,2048,1,1408]{3,2,1,0:T(2,128)(2,1)} %get-tuple-element.99), kind=kOutput, calls=%fused_computation.11 | convolution fusion | flops 3324248064 | bytes 14467072 | tf_op jit(solution)/shard_map/dot_general | solution.py:26
  318.8 6.6 fusion.220
  328.0 11.6 %collective-permute-done.43 = bf16[128,2048]{1,0:T(8,128)(2,1)S(1)} collective-permute-done((bf16[128,2048]{1,0:T(8,128)(2,1)S(1)}, bf16[128,2048]{1,0:T(8,128)(2,1)S(1)}, u32[]{:S(2)}, u32[]{:S(2)}) %collective-permute-start.43) | collective-permute-done | bytes 524320 | tf_op jit(solution)/shard_map/ppermute | solution.py:30
  416.1 8.6 %convolution_convert_fusion.1 = bf16[2048,1408]{1,0:T(8,128)(2,1)} fusion(bf16[576,2048]{1,0:T(8,128)(2,1)} %convolution_convert_fusion.6, bf16[576,1408]{1,0:T(8,128)(2,1)} %get-tuple-element.100), kind=kOutput, calls=%fused_computation.3 | convolution fusion | flops 3324772352 | bytes 9748480 | tf_op jit(solution)/shard_map/dot_general | solution.py:26
  424.8 8.6 %convolution_convert_fusion.2 = bf16[2048,1408]{1,0:T(8,128)(2,1)} fusion(bf16[576,2048]{1,0:T(8,128)(2,1)} %convolution_convert_fusion.6, bf16[576,1408]{1,0:T(8,128)(2,1)} %copy-done.88), kind=kOutput, calls=%fused_computation.4 | convolution fusion | flops 3324772352 | bytes 9748480 | tf_op jit(solution)/shard_map/dot_general | solution.py:26
  433.7 9.4 %convolution_convert_fusion = bf16[1408,2048]{1,0:T(8,128)(2,1)} fusion(bf16[576,1408]{1,0:T(8,128)(2,1)} %copy-done.87, bf16[576,2048]{1,0:T(8,128)(2,1)} %multiply_convert_fusion.1), kind=kOutput, calls=%fused_computation.2 | convolution fusion | flops 3324772352 | bytes 9748480 | tf_op jit(solution)/shard_map/dot_general | solution.py:26
  457.1 10.7 %collective-permute-done.59 = bf16[128,2048]{1,0:T(8,128)(2,1)S(1)} collective-permute-done((bf16[128,2048]{1,0:T(8,128)(2,1)S(1)}, bf16[128,2048]{1,0:T(8,128)(2,1)S(1)}, u32[]{:S(2)}, u32[]{:S(2)}) %collective-permute-start.59) | collective-permute-done | bytes 524320 | tf_op jit(solution)/shard_map/ppermute | solution.py:30
  525.2 102.8 %reduce-scatter.21.cloned.1.call-done = bf16[512,1408]{1,0:T(8,128)(2,1)} async-done(((bf16[2048,1408]{1,0:T(8,128)(2,1)}), bf16[512,1408]{1,0:T(8,128)(2,1)}) %reduce-scatter.21.cloned.1.call-update) | async-done | bytes 1441808 | tf_op jit(solution)/shard_map/reduce_scatter | solution.py:76
  628.0 105.2 %reduce-scatter.19.cloned.1.call-done = bf16[512,1408]{1,0:T(8,128)(2,1)} async-done(((bf16[2048,1408]{1,0:T(8,128)(2,1)}), bf16[512,1408]{1,0:T(8,128)(2,1)}) %reduce-scatter.19.cloned.1.call-update) | async-done | bytes 1441808 | tf_op jit(solution)/shard_map/reduce_scatter | solution.py:76
  735.4 7.0 copy.55
  742.4 96.0 %reduce-scatter.23.cloned.1.call-done = bf16[1408,512]{1,0:T(8,128)(2,1)} async-done(((bf16[1408,2048]{1,0:T(8,128)(2,1)}), bf16[1408,512]{1,0:T(8,128)(2,1)}) %reduce-scatter.23.cloned.1.call-update) | async-done | bytes 1441808 | tf_op jit(solution)/shard_map/reduce_scatter | solution.py:76
  (602 shorter events, 327.8 us)
Async XLA Ops:
  7.2 495.0 %reduce-scatter.13.cloned.1.call-start = ((), (), s32[]{:S(2)}) async-start(), calls=%async_computation.10 | async-start | bytes 3604480 | tf_op jit(solution)/shard_map/reduce_scatter | solution.py:76
  11.6 27.9 %collective-permute-start.4 = (bf16[128,2048]{1,0:T(8,128)(2,1)}, bf16[128,2048]{1,0:T(8,128)(2,1)}, u32[]{:S(2)}, u32[]{:S(2)}) collective-permute-start(bf16[128,2048]{1,0:T(8,128)(2,1)} %get-tuple-element.97), channel_id=1, source_target_pairs={{0,1},{1,0},{2,3},{3,2},{4,5},{5,4},{6,7},{7,6},{8,9},{9,8},{10,11... | collective-permute-start | bytes 1572872 | tf_op jit(solution)/shard_map/ppermute | solution.py:30
  12.0 15.3 %collective-permute-start.1 = (bf16[128,2048]{1,0:T(8,128)(2,1)}, bf16[128,2048]{1,0:T(8,128)(2,1)S(1)}, u32[]{:S(2)}, u32[]{:S(2)}) collective-permute-start(bf16[128,2048]{1,0:T(8,128)(2,1)} %get-tuple-element.97), channel_id=1, source_target_pairs={{0,4},{1,5},{2,6},{3,7},{4,0},{5,1},{6,2},{7,3},{8,12},{9,13},{10,... | collective-permute-start | bytes 1572872 | tf_op jit(solution)/shard_map/ppermute | solution.py:30
  14.6 14.5 %collective-permute-start = (bf16[128,2048]{1,0:T(8,128)(2,1)}, bf16[128,2048]{1,0:T(8,128)(2,1)}, u32[]{:S(2)}, u32[]{:S(2)}) collective-permute-start(bf16[128,2048]{1,0:T(8,128)(2,1)} %get-tuple-element.97), channel_id=1, source_target_pairs={{0,2},{1,3},{2,0},{3,1},{4,6},{5,7},{6,4},{7,5},{8,10},{9,11},{10,... | collective-permute-start | bytes 1572872 | tf_op jit(solution)/shard_map/ppermute | solution.py:30
  59.3 26.8 %collective-permute-start.21 = (s32[1,4,128]{2,1,0:T(4,128)S(1)}, s32[1,4,128]{2,1,0:T(4,128)S(1)}, u32[]{:S(2)}, u32[]{:S(2)}) collective-permute-start(s32[1,4,128]{2,1,0:T(4,128)S(1)} %bitcast.264), channel_id=1, source_target_pairs={{0,2},{1,3},{2,0},{3,1},{4,6},{5,7},{6,4},{7,5},{8,10},{9,11},{10,... | collective-permute-start | bytes 6152 | tf_op jit(solution)/shard_map/ppermute | solution.py:30
  64.9 20.0 %collective-permute-start.9 = (bf16[128,2048]{1,0:T(8,128)(2,1)}, bf16[128,2048]{1,0:T(8,128)(2,1)S(1)}, u32[]{:S(2)}, u32[]{:S(2)}) collective-permute-start(bf16[128,2048]{1,0:T(8,128)(2,1)} %pad_maximum_fusion.10), channel_id=1, source_target_pairs={{0,2},{1,3},{2,0},{3,1},{4,6},{5,7},{6,4},{7,5},{8,10},{9,11},{10,... | collective-permute-start | bytes 1572872 | tf_op jit(solution)/shard_map/ppermute | solution.py:30
  83.9 14.8 %collective-permute-start.11 = (bf16[128,2048]{1,0:T(8,128)(2,1)S(1)}, bf16[128,2048]{1,0:T(8,128)(2,1)S(1)}, u32[]{:S(2)}, u32[]{:S(2)}) collective-permute-start(bf16[128,2048]{1,0:T(8,128)(2,1)S(1)} %pad_maximum_fusion.11), channel_id=1, source_target_pairs={{0,4},{1,5},{2,6},{3,7},{4,0},{5,1},{6,2},{7,3},{8,12},{9,13},{10,... | collective-permute-start | bytes 1572872 | tf_op jit(solution)/shard_map/ppermute | solution.py:30
  85.0 18.6 %collective-permute-start.10 = (bf16[64,2048]{1,0:T(8,128)(2,1)S(1)}, bf16[64,2048]{1,0:T(8,128)(2,1)S(1)}, u32[]{:S(2)}, u32[]{:S(2)}) collective-permute-start(bf16[64,2048]{1,0:T(8,128)(2,1)S(1)} %fusion.136), channel_id=1, source_target_pairs={{0,4},{1,5},{2,6},{3,7},{4,0},{5,1},{6,2},{7,3},{8,12},{9,13},{10,... | collective-permute-start | bytes 786440 | tf_op jit(solution)/shard_map/ppermute | solution.py:30
  86.1 19.4 %collective-permute-start.22 = (s32[2,4,128]{2,1,0:T(4,128)S(1)}, s32[2,4,128]{2,1,0:T(4,128)S(1)}, u32[]{:S(2)}, u32[]{:S(2)}) collective-permute-start(s32[2,4,128]{2,1,0:T(4,128)S(1)} %pad_add_fusion.1), channel_id=1, source_target_pairs={{0,4},{1,5},{2,6},{3,7},{4,0},{5,1},{6,2},{7,3},{8,12},{9,13},{10,... | collective-permute-start | bytes 12296 | tf_op jit(solution)/shard_map/ppermute | solution.py:30
  118.1 16.9 %collective-permute-start.17 = (bf16[128,2048]{1,0:T(8,128)(2,1)S(1)}, bf16[128,2048]{1,0:T(8,128)(2,1)S(1)}, u32[]{:S(2)}, u32[]{:S(2)}) collective-permute-start(bf16[128,2048]{1,0:T(8,128)(2,1)S(1)} %get-tuple-element.91), channel_id=1, source_target_pairs={{0,1},{1,0},{2,3},{3,2},{4,5},{5,4},{6,7},{7,6},{8,9},{9,8},{10,11... | collective-permute-start | bytes 1572872 | tf_op jit(solution)/shard_map/ppermute | solution.py:30
  187.7 14.4 %collective-permute-start.25 = (bf16[128,2048]{1,0:T(8,128)(2,1)S(1)}, bf16[128,2048]{1,0:T(8,128)(2,1)S(1)}, u32[]{:S(2)}, u32[]{:S(2)}) collective-permute-start(bf16[128,2048]{1,0:T(8,128)(2,1)S(1)} %pad_maximum_fusion.13), channel_id=1, source_target_pairs={{0,2},{1,3},{2,0},{3,1},{4,6},{5,7},{6,4},{7,5},{8,10},{9,11},{10,... | collective-permute-start | bytes 1572872 | tf_op jit(solution)/shard_map/ppermute | solution.py:30
  220.7 17.7 %collective-permute-start.38 = (bf16[128,2048]{1,0:T(8,128)(2,1)S(1)}, bf16[128,2048]{1,0:T(8,128)(2,1)S(1)}, u32[]{:S(2)}, u32[]{:S(2)}) collective-permute-start(bf16[128,2048]{1,0:T(8,128)(2,1)S(1)} %get-tuple-element.86), channel_id=1, source_target_pairs={{0,1},{1,0},{2,3},{3,2},{4,5},{5,4},{6,7},{7,6},{8,9},{9,8},{10,11... | collective-permute-start | bytes 1572872 | tf_op jit(solution)/shard_map/ppermute | solution.py:30
  256.9 245.3 %reduce-scatter.15.cloned.1.call-start = ((), (), s32[]{:S(2)}) async-start(), calls=%async_computation.11 | async-start | bytes 3604480 | tf_op jit(solution)/shard_map/reduce_scatter | solution.py:76
  301.0 17.8 %collective-permute-start.42 = (bf16[512,2048]{1,0:T(8,128)(2,1)}, bf16[512,2048]{1,0:T(8,128)(2,1)}, u32[]{:S(2)}, u32[]{:S(2)}) collective-permute-start(bf16[512,2048]{1,0:T(8,128)(2,1)} %add_convert_fusion.3), channel_id=1, source_target_pairs={{0,1},{1,0},{2,3},{3,2},{4,5},{5,4},{6,7},{7,6},{8,9},{9,8},{10,11... | collective-permute-start | bytes 6291464 | tf_op jit(solution)/shard_map/ppermute | solution.py:30
  301.7 14.9 %collective-permute-start.47 = (f32[4,16,128]{2,1,0:T(8,128)S(1)}, f32[4,16,128]{2,1,0:T(8,128)S(1)}, u32[]{:S(2)}, u32[]{:S(2)}) collective-permute-start(f32[4,16,128]{2,1,0:T(8,128)S(1)} %slice.711), channel_id=1, source_target_pairs={{0,1},{1,0},{2,3},{3,2},{4,5},{5,4},{6,7},{7,6},{8,9},{9,8},{10,11... | collective-permute-start | bytes 98312 | tf_op jit(solution)/shard_map/ppermute | solution.py:30
  316.4 188.9 %reduce-scatter.17.cloned.1.call-start = ((), (), s32[]{:S(2)}) async-start(), calls=%async_computation.12 | async-start | bytes 3604480 | tf_op jit(solution)/shard_map/reduce_scatter | solution.py:76
  362.5 145.2 %reduce-scatter.11.cloned.1.call-start = ((), (), s32[]{:S(2)}) async-start(), calls=%async_computation.9 | async-start | bytes 1310720 | tf_op jit(solution)/shard_map/reduce_scatter | solution.py:76
  362.6 17.1 %collective-permute-start.54 = (bf16[128,2048]{1,0:T(8,128)(2,1)}, bf16[128,2048]{1,0:T(8,128)(2,1)S(1)}, u32[]{:S(2)}, u32[]{:S(2)}) collective-permute-start(bf16[128,2048]{1,0:T(8,128)(2,1)} %get-tuple-element.83), channel_id=1, source_target_pairs={{0,1},{1,0},{2,3},{3,2},{4,5},{5,4},{6,7},{7,6},{8,9},{9,8},{10,11... | collective-permute-start | bytes 1572872 | tf_op jit(solution)/shard_map/ppermute | solution.py:30
  401.8 121.1 %reduce-scatter.9.cloned.1.call-start = ((), (), s32[]{:S(2)}) async-start(), calls=%async_computation.8 | async-start | bytes 3932160 | tf_op jit(solution)/shard_map/reduce_scatter | solution.py:76
  416.1 211.9 %reduce-scatter.21.cloned.1.call-start = ((), (), s32[]{:S(2)}) async-start(), calls=%async_computation.14 | async-start | bytes 7208960 | tf_op jit(solution)/shard_map/reduce_scatter | solution.py:76
  424.7 308.5 %reduce-scatter.19.cloned.1.call-start = ((), (), s32[]{:S(2)}) async-start(), calls=%async_computation.13 | async-start | bytes 7208960 | tf_op jit(solution)/shard_map/reduce_scatter | solution.py:76
  433.4 405.0 %reduce-scatter.23.cloned.1.call-start = ((), (), s32[]{:S(2)}) async-start(), calls=%async_computation.15 | async-start | bytes 7208960 | tf_op jit(solution)/shard_map/reduce_scatter | solution.py:76
  456.4 32.3 %collective-permute-start.61 = (bf16[128,2048]{1,0:T(8,128)(2,1)S(1)}, bf16[128,2048]{1,0:T(8,128)(2,1)S(1)}, u32[]{:S(2)}, u32[]{:S(2)}) collective-permute-start(bf16[128,2048]{1,0:T(8,128)(2,1)S(1)} %pad_maximum_fusion.20), channel_id=1, source_target_pairs={{0,4},{1,5},{2,6},{3,7},{4,0},{5,1},{6,2},{7,3},{8,12},{9,13},{10,... | collective-permute-start | bytes 1572872 | tf_op jit(solution)/shard_map/ppermute | solution.py:30
  468.7 20.0 %collective-permute-start.60 = (bf16[64,2048]{1,0:T(8,128)(2,1)S(1)}, bf16[64,2048]{1,0:T(8,128)(2,1)S(1)}, u32[]{:S(2)}, u32[]{:S(2)}) collective-permute-start(bf16[64,2048]{1,0:T(8,128)(2,1)S(1)} %fusion.124), channel_id=1, source_target_pairs={{0,4},{1,5},{2,6},{3,7},{4,0},{5,1},{6,2},{7,3},{8,12},{9,13},{10,... | collective-permute-start | bytes 786440 | tf_op jit(solution)/shard_map/ppermute | solution.py:30
  (155 other events, 1863.0 us)
Sparse Core Ops, SparseCore 0:
  257.1 57.0 reduce-scatter.12
  317.0 56.6 reduce-scatter.14
  376.0 56.0 reduce-scatter.16
  434.2 26.9 reduce-scatter.10
  463.5 59.2 reduce-scatter.8
  525.6 102.3 reduce-scatter.20
  630.4 102.7 reduce-scatter.18
  735.6 102.7 reduce-scatter.22

commit v2 on v1

--- a/solution.py
+++ b/solution.py
@@ -1,6 +1,8 @@
 import jax
 import jax.numpy as jnp
 from jax import lax
+from jax.experimental import pallas as pl
+from jax.experimental.pallas import tpu as pltpu
 from jax.sharding import PartitionSpec as P
 
 D = 2048
@@ -18,8 +20,20 @@
 ORDER = (0, 2, 4, 6, 1, 3, 5, 7)
 
 
-def barrier(*values):
-    return lax.optimization_barrier(values)
+def after(values, work):
+    values, work = tuple(values), tuple(work)
+    if not work or not values:
+        return values, work
+    tied = lax.optimization_barrier((*values, *work))
+    return tied[: len(values)], tied[len(values) :]
+
+
+def between(first, last, task):
+    if task is None:
+        return tuple(last), ()
+    function, *inputs = task
+    inputs, _ = after(inputs, first)
+    return after(last, function(*inputs))
 
 
 def dot(left, right, dims, dtype=F32):
@@ -30,13 +44,18 @@
     return lax.ppermute(values, "sp", [(i, i ^ distance) for i in range(8)])
 
 
-def gather_rows(own):
+def gather_rows(own, task=None):
     half = own.shape[0] // 2
-    over_x, over_y, over_c = swap(own, 2), swap(own, 4), swap(own, 1)
+    over_x, over_y = swap(own, 2), swap(own, 4)
+    (over_x, over_y), work = between((own,), (over_x, over_y), task)
     far_top, far_bottom = swap(over_y[:half], 2), swap(over_x[half:], 4)
-    far = jnp.concatenate([far_top, far_bottom], 0)
-    rest = [swap(over_x, 1), swap(over_y, 1), swap(far, 1)]
-    return jnp.concatenate([own, over_x, over_y, far, over_c] + rest, 0)
+    lower = jnp.concatenate([own, over_x, over_y, far_top, far_bottom], 0)
+    return lower, swap(lower, 1), work
+
+
+def gather_far(own):
+    same = lax.all_gather(own, "sp", axis_index_groups=[[0, 2, 4, 6], [1, 3, 5, 7]])
+    return same, swap(same, 1)
 
 
 def gather_small(own):
@@ -46,14 +65,15 @@
     return held
 
 
-def sum_small(parts):
+def sum_small(parts, total):
     for distance in (1, 4, 2):
         keep = parts.shape[0] // 2
-        parts = parts[:keep] + swap(parts[keep:], distance)
-    return parts[0]
-
-
-def sum_rows(upper, lower):
+        got = swap(jnp.concatenate([parts[keep:], total], 0), distance)
+        parts, total = parts[:keep] + got[:keep], total + got[keep:]
+    return parts[0], total[0]
+
+
+def sum_rows(upper, lower, task=None):
     rows = lower.shape[0] // 4
     half = rows // 2
     got = swap(upper, 1)
@@ -63,38 +83,245 @@
     low_x, low_y, low_far = low[over_x], low[over_y], low[far]
     from_x = swap(jnp.concatenate([low_far[:half], low_x[:half]], 0), 2)
     from_y = swap(jnp.concatenate([low_far[half:], low_y[half:]], 0), 4)
+    (from_x, from_y), work = between((low,), (from_x, from_y), task)
     pass_y = (chip[over_y][:half] + from_x[:half].astype(F32)).astype(BF)
     pass_x = (chip[over_x][half:] + from_y[:half].astype(F32)).astype(BF)
     last_y, last_x = swap(pass_y, 4), swap(pass_x, 2)
     mine = chip[own]
     top = mine[:half] + from_x[half:].astype(F32) + last_y.astype(F32)
     bottom = mine[half:] + from_y[half:].astype(F32) + last_x.astype(F32)
-    return jnp.concatenate([top, bottom], 0)
+    return jnp.concatenate([top, bottom], 0), work
 
 
 def sum_groups(grads, dim):
     return lax.psum_scatter(grads, "dp", scatter_dimension=dim, tiled=True).astype(F32)
 
 
-def shift_groups(blocks):
+def shift_groups(blocks, total):
     size = lax.axis_size("dp")
     me = lax.axis_index("dp")
     pick = lambda k: lax.dynamic_index_in_dim(blocks, (me + k) % size, 0, keepdims=False)
-    total = pick(0)
+    mine = jnp.stack([pick(0), total])
+    summed = mine[0]
+    totals = jnp.zeros((size,) + total.shape, total.dtype).at[me].set(total)
     for k in range(1, size):
-        total = total + lax.ppermute(pick(k), "dp", [(i, (i + k) % size) for i in range(size)])
-    return total
-
-
-def sum_everywhere(values):
-    for distance in (1, 2, 4):
-        values = values + swap(values, distance)
+        got = lax.ppermute(jnp.stack([pick(k), total]), "dp", [(i, (i + k) % size) for i in range(size)])
+        summed = summed + got[0]
+        totals = totals.at[(me - k) % size].set(got[1])
+    return summed, jnp.sum(totals, axis=0)
+
+
+def fetch_groups(own):
     size = lax.axis_size("dp")
-    step = 1
-    while step < size:
-        values = values + lax.ppermute(values, "dp", [(i, i ^ step) for i in range(size)])
-        step *= 2
-    return values
+    return [lax.ppermute(own, "dp", [((i + k) % size, i) for i in range(size)]) for k in range(1, size)]
+
+
+def own_columns(values, axis):
+    share = values.shape[axis] // lax.axis_size("dp")
+    return lax.dynamic_slice_in_dim(values, lax.axis_index("dp") * share, share, axis)
+
+
+def slots_of(mask):
+    return jnp.where(mask, jnp.cumsum(mask.astype(jnp.int32), axis=-1) - 1, -1)
+
+
+def local_call(kernel, name, flops, **spec):
+    return pl.pallas_call(
+        kernel,
+        name=name,
+        cost_estimate=pl.CostEstimate(flops=flops, bytes_accessed=flops // 300, transcendentals=0),
+        compiler_params=pltpu.CompilerParams(vmem_limit_bytes=56 * 2**20),
+        **spec,
+    )
+
+
+def pick_kernel(slot_ref, scale_ref, lower_ref, upper_ref, out_ref):
+    capacity, columns = out_ref.shape
+    total = slot_ref.shape[-1]
+    chosen = (slot_ref[...] == lax.broadcasted_iota(jnp.int32, (capacity, total), 0)).astype(F32).astype(BF)
+    half = total // 2
+    rows = jnp.dot(chosen[:, :half], lower_ref[...].reshape(half, columns), preferred_element_type=F32)
+    rows += jnp.dot(chosen[:, half:], upper_ref[...].reshape(half, columns), preferred_element_type=F32)
+    out_ref[...] = (rows * scale_ref[...]).astype(BF)
+
+
+def pick_rows(slots, scale, lower, upper):
+    blocks, groups, count, width = lower.shape
+    total = 2 * blocks * count
+    capacity = scale.shape[1]
+    tile = 1024
+    rows = pl.BlockSpec((blocks, None, count, tile), lambda g, j: (0, g, 0, j))
+    return local_call(
+        pick_kernel,
+        "pick_rows",
+        2 * groups * capacity * total * width,
+        grid=(groups, width // tile),
+        in_specs=[
+            pl.BlockSpec((None, 1, total), lambda g, j: (g, 0, 0)),
+            pl.BlockSpec((None, capacity, 1), lambda g, j: (g, 0, 0)),
+            rows,
+            rows,
+        ],
+        out_specs=pl.BlockSpec((None, capacity, tile), lambda g, j: (g, 0, j)),
+        out_shape=jax.ShapeDtypeStruct((groups, capacity, width), BF),
+    )(slots[:, None, :], scale, lower, upper)
+
+
+def dot_nn(left, right):
+    return lax.dot_general(left, right, (((1,), (0,)), ((), ())), preferred_element_type=F32)
+
+
+def dot_nt(left, right):
+    return lax.dot_general(left, right, (((1,), (1,)), ((), ())), preferred_element_type=F32)
+
+
+def dot_tn(left, right):
+    return lax.dot_general(left, right, (((0,), (0,)), ((), ())), preferred_element_type=F32)
+
+
+def expert_kernel(x_ref, gateup_w, down_w, gate_ref, up_ref, act_ref, made_ref):
+    x = x_ref[...]
+    gate, up = dot_nn(x, gateup_w[0]), dot_nn(x, gateup_w[1])
+    gate_ref[...], up_ref[...] = gate, up
+    act = (gate * jax.nn.sigmoid(gate) * up).astype(BF)
+    act_ref[...] = act
+    made_ref[...] = dot_nn(act, down_w[...]).astype(BF)
+
+
+def row_spec(block, columns):
+    return pl.BlockSpec((block, columns), lambda i: (i, 0))
+
+
+def held_spec(array):
+    return pl.BlockSpec(array.shape, lambda i: (0,) * array.ndim, pipeline_mode=pl.Buffered(1))
+
+
+def row_block(count):
+    return max(b for b in range(16, min(count, 288) + 1, 16) if count % b == 0)
+
+
+def expert_forward(x, gateup_w, down_w):
+    count, width = x.shape
+    hidden = gateup_w.shape[2]
+    block = row_block(count)
+    wide_shape = lambda dtype: jax.ShapeDtypeStruct((count, hidden), dtype)
+    return local_call(
+        expert_kernel,
+        "expert_forward",
+        6 * count * width * hidden,
+        grid=(count // block,),
+        in_specs=[row_spec(block, width), held_spec(gateup_w), held_spec(down_w)],
+        out_specs=[row_spec(block, hidden)] * 3 + [row_spec(block, width)],
+        out_shape=[wide_shape(F32), wide_shape(F32), wide_shape(BF), jax.ShapeDtypeStruct((count, width), BF)],
+    )(x, gateup_w, down_w)
+
+
+def middle_grads(gate, up, grad):
+    sig = jax.nn.sigmoid(gate)
+    slope = sig * (1.0 + gate * (1.0 - sig))
+    return (grad * up * slope).astype(BF), (grad * (gate * sig)).astype(BF)
+
+
+def expert_back_kernel(g_ref, gate_ref, up_ref, act_ref, gateup_w, down_w, gg_ref, gu_ref, back_ref, gain_ref):
+    grad = dot_nt(g_ref[...], down_w[...])
+    gain_ref[...] = jnp.sum(act_ref[...].astype(F32) * grad, axis=1, keepdims=True)
+    grad_gate, grad_up = middle_grads(gate_ref[...], up_ref[...], grad)
+    gg_ref[...], gu_ref[...] = grad_gate, grad_up
+    back_ref[...] = (dot_nt(grad_gate, gateup_w[0]) + dot_nt(grad_up, gateup_w[1])).astype(BF)
+
+
+def expert_back(g, gate, up, act, gateup_w, down_w):
+    count, width = g.shape
+    hidden = gateup_w.shape[2]
+    block = row_block(count)
+    rows, mids = row_spec(block, width), row_spec(block, hidden)
+    return local_call(
+        expert_back_kernel,
+        "expert_back",
+        6 * count * width * hidden,
+        grid=(count // block,),
+        in_specs=[rows, mids, mids, mids, held_spec(gateup_w), held_spec(down_w)],
+        out_specs=[mids, mids, rows, row_spec(block, 1)],
+        out_shape=[jax.ShapeDtypeStruct((count, hidden), BF)] * 2
+        + [jax.ShapeDtypeStruct((count, width), BF), jax.ShapeDtypeStruct((count, 1), F32)],
+    )(g, gate, up, act, gateup_w, down_w)
+
+
+def expert_far_kernel(x_ref, g_ref, gateup_w, down_w, act_ref, gg_ref, gu_ref):
+    x = x_ref[...]
+    gate, up = dot_nn(x, gateup_w[0]), dot_nn(x, gateup_w[1])
+    act_ref[...] = (gate * jax.nn.sigmoid(gate) * up).astype(BF)
+    gg_ref[...], gu_ref[...] = middle_grads(gate, up, dot_nt(g_ref[...], down_w[...]))
+
+
+def expert_far(x, g, gateup_w, down_w):
+    count, width = x.shape
+    hidden = gateup_w.shape[2]
+    block = row_block(count)
+    rows, mids = row_spec(block, width), row_spec(block, hidden)
+    return local_call(
+        expert_far_kernel,
+        "expert_far",
+        6 * count * width * hidden,
+        grid=(count // block,),
+        in_specs=[rows, rows, held_spec(gateup_w), held_spec(down_w)],
+        out_specs=[mids] * 3,
+        out_shape=[jax.ShapeDtypeStruct((count, hidden), BF)] * 3,
+    )(x, g, gateup_w, down_w)
+
+
+def expert_grad_kernel(_, x, g, act, gg, gu, far_x, far_g, far_act, far_gg, far_gu, gateup_ref, down_ref, acc_g, acc_u):
+    step = pl.program_id(0)
+
+    @pl.when(step == 0)
+    def _():
+        rows = x[...]
+        acc_g[...] = dot_tn(rows, gg[...])
+        acc_u[...] = dot_tn(rows, gu[...])
+        down_ref[...] = dot_tn(act[...], g[...])
+
+    @pl.when(step > 0)
+    def _():
+        rows = far_x[...]
+        acc_g[...] += dot_tn(rows, far_gg[...])
+        acc_u[...] += dot_tn(rows, far_gu[...])
+        down_ref[...] += dot_tn(far_act[...], far_g[...])
+
+    @pl.when(step == pl.num_programs(0) - 1)
+    def _():
+        gateup_ref[:, 0, :] = acc_g[...]
+        gateup_ref[:, 1, :] = acc_u[...]
+
+
+def expert_grads_of(own, far):
+    count, width = own[0].shape
+    hidden = own[2].shape[1]
+    share = width // lax.axis_size("dp")
+    steps = 1 + far[0].shape[0] // count
+    held = lambda i, d: (0, 0)
+    near_rows = pl.BlockSpec((count, share), lambda i, d: (0, d[0]))
+    near_mid = pl.BlockSpec((count, hidden), held)
+    far_rows = pl.BlockSpec((count, share), lambda i, d: (jnp.maximum(i - 1, 0), d[0]))
+    far_mid = pl.BlockSpec((count, hidden), lambda i, d: (jnp.maximum(i - 1, 0), 0))
+    return local_call(
+        expert_grad_kernel,
+        "expert_grads",
+        6 * count * steps * share * hidden,
+        grid_spec=pltpu.PrefetchScalarGridSpec(
+            num_scalar_prefetch=1,
+            grid=(steps,),
+            in_specs=[near_rows, near_rows] + [near_mid] * 3 + [far_rows, far_rows] + [far_mid] * 3,
+            out_specs=[
+                pl.BlockSpec((share, 2, hidden), lambda i, d: (0, 0, 0)),
+                pl.BlockSpec((hidden, share), held),
+            ],
+            scratch_shapes=[pltpu.VMEM((share, hidden), F32)] * 2,
+        ),
+        out_shape=[
+            jax.ShapeDtypeStruct((share, 2, hidden), F32),
+            jax.ShapeDtypeStruct((hidden, share), F32),
+        ],
+    )(lax.axis_index("dp").reshape(1), *own, *far)
 
 
 def layout(length_row, place):
@@ -218,8 +445,15 @@
     inputs = hidden_in.astype(F32)
     gain_one = attn_norm.astype(F32)
     normed_f, inverse_one = normalize(inputs, gain_one)
-    normed_all = gather_rows(normed_f.astype(BF))
-    route_all = gather_small(routes.T)
+    *normed_halves, (gateup_w,) = gather_rows(
+        normed_f.astype(BF), (lambda w: (w.transpose(1, 0, 2),), expert_gateup[0])
+    )
+    wide = dp_size <= 4
+    route_own = routes.T[None]
+    if wide:
+        route_own = jnp.concatenate([route_own] + fetch_groups(route_own), 0)
+    route_all = gather_small(route_own.reshape(-1, tok_rows))
+    route_all = route_all.reshape(sp_size, -1, top_k, tok_rows)
 
     owners = me ^ jnp.array(ORDER, jnp.int32)
     place = (owners[:, None] * tok_rows + jnp.arange(tok_rows, dtype=jnp.int32)[None, :]).reshape(-1)
@@ -233,116 +467,165 @@
         & is_valid[None, :]
     )
 
-    mask = jnp.any(route_all == me, axis=1).reshape(total_rows)
-    slot = jnp.cumsum(mask.astype(jnp.int32)) - 1
-    slot = jnp.where(mask, slot, -1)
-    pick = (slot[None, :] == jnp.arange(capacity, dtype=jnp.int32)[:, None]).astype(BF)
+    masks = jnp.any(route_all == me, axis=2)
+    mask = masks[:, 0].reshape(total_rows)
+    slots = slots_of(mask)[None]
+    slot_range = jnp.arange(capacity, dtype=jnp.int32)
+    pick = (slots[0][None, :] == slot_range[:, None]).astype(BF)
 
     bias = qkv_bias.reshape(3, 1, -1).astype(F32)
-    projected = [dot(normed_all, qkv_proj[j], ((1,), (0,))) + bias[j] for j in range(3)]
+    projected = [
+        jnp.concatenate([dot(rows, qkv_proj[j], ((1,), (0,))) for rows in normed_halves], 0) + bias[j]
+        for j in range(3)
+    ]
     queries = rotate(projected[0], cosine, sine_table).astype(BF)
     key_rows = rotate(projected[1], cosine, sine_table).astype(BF)
     values = projected[2].astype(BF)
     mixed, totals = attend_forward(queries, key_rows, values, allowed)
     upper = dot(mixed[lower_rows:], out_proj, ((1,), (0,)), BF)
     lower = dot(mixed[:lower_rows], out_proj, ((1,), (0,)), BF)
-    middle = inputs + sum_rows(upper, lower)
+    middle = inputs + sum_rows(upper, lower)[0]
 
     gain_two = ffn_norm.astype(F32)
     normed_two_f, inverse_two = normalize(middle, gain_two)
     normed_two = normed_two_f.astype(BF)
-    two_all = gather_rows(normed_two)
+    *two_halves, _ = gather_rows(normed_two)
+    fetched_two = fetch_groups(normed_two) if wide else []
 
     heads_in = jnp.concatenate([router, shared_switch[:, None]], axis=1)
-    logits = dot(two_all, heads_in, ((1,), (0,)))
-    probs = jax.nn.softmax(logits[:, :experts], axis=-1)
-    switch = jax.nn.sigmoid(logits[:, experts:])
     is_me = (jnp.arange(experts) == me).astype(F32)
+
+    def steer_rows(rows):
+        logits = dot(rows, heads_in, ((1,), (0,)))
+        return jax.nn.softmax(logits[:, :experts], axis=-1), jax.nn.sigmoid(logits[:, experts:])
+
+    steered = [steer_rows(rows) for rows in two_halves]
+    probs, switch = (jnp.concatenate(both, 0) for both in zip(*steered))
     share = jnp.sum(probs * is_me[None, :], axis=1) * mask.astype(F32)
     share_rows = jnp.sum(pick.astype(F32) * share[None, :], axis=1, keepdims=True)
 
-    gate_w, up_w = expert_gateup[0, :, 0, :], expert_gateup[0, :, 1, :]
     down_w = expert_down[0]
-    rows_in = dot(pick, two_all, ((1,), (0,)), BF)
-    gate_e = dot(rows_in, gate_w, ((1,), (0,)))
-    up_e = dot(rows_in, up_w, ((1,), (0,)))
-    acted_e = (jax.nn.silu(gate_e) * up_e).astype(BF)
-    made = dot(acted_e, down_w, ((1,), (0,)), BF)
+    blocks = (sp_size // 2, 1, tok_rows, width)
+    ones = jnp.ones((1, capacity, 1), F32)
+    rows_in = pick_rows(slots, ones, *(rows.reshape(blocks) for rows in two_halves))[0]
+    gate_e, up_e, acted_e, made = expert_forward(rows_in, gateup_w, down_w)
 
     gate_sw, up_sw = shared_gateup[:, 0, :], shared_gateup[:, 1, :]
-    gate_s = dot(two_all, gate_sw, ((1,), (0,)))
-    up_s = dot(two_all, up_sw, ((1,), (0,)))
-    acted_s = (jax.nn.silu(gate_s) * up_s).astype(BF)
-
-    def ffn_part(rows):
-        shared = dot(acted_s[rows], shared_down, ((1,), (0,)))
+    gate_s = [dot(rows, gate_sw, ((1,), (0,))) for rows in two_halves]
+    up_s = [dot(rows, up_sw, ((1,), (0,))) for rows in two_halves]
+    acted_s = [(jax.nn.silu(g) * u).astype(BF) for g, u in zip(gate_s, up_s)]
+    (acted_s[1],), fetched_two = after((acted_s[1],), fetched_two)
+    if wide:
+        two_far = gather_far(jnp.stack(fetched_two, 0))
+    halves = (slice(0, lower_rows), slice(lower_rows, None))
+
+    def ffn_part(side):
+        rows = halves[side]
+        shared = dot(acted_s[side], shared_down, ((1,), (0,)))
         routed = dot(pick[:, rows], made, ((0,), (0,)))
-        return (switch[rows] * shared + share[rows, None] * routed).astype(BF)
-
-    upper_half, lower_half = slice(lower_rows, None), slice(0, lower_rows)
-    ffn_upper = ffn_part(upper_half)
-    ffn_lower = ffn_part(lower_half)
-    output = middle + sum_rows(ffn_upper, ffn_lower)
+        return (steered[side][1] * shared + share[rows, None] * routed).astype(BF)
+
+    ffn_upper = ffn_part(1)
+    ffn_lower = ffn_part(0)
+    output = middle + sum_rows(ffn_upper, ffn_lower)[0]
 
     error = (output - teacher.astype(F32)) * local_valid[:, None]
-    squares = sum_everywhere(jnp.full((8, 128), jnp.sum(error * error), F32))[0, 0]
+    squares = jnp.sum(error * error)
     count = jnp.sum(seq_lengths).astype(F32)
-    loss_value = squares / (2.0 * count * D)
-
-    error_all = gather_rows(error.astype(BF))
-    rows_g = dot(pick, error_all, ((1,), (0,)))
-    grad_made = (share_rows * rows_g).astype(BF)
-    grad_acted = dot(grad_made, down_w, ((1,), (1,)))
-    gain_rows = jnp.sum(acted_e.astype(F32) * grad_acted, axis=1, keepdims=True)
-    grad_gate_e = (grad_acted * up_e * silu_slope(gate_e)).astype(BF)
-    grad_up_e = (grad_acted * jax.nn.silu(gate_e)).astype(BF)
-    gate_term = dot(rows_in, grad_gate_e, ((0,), (0,)), BF)
-    up_term = dot(rows_in, grad_up_e, ((0,), (0,)), BF)
-    down_term = dot(acted_e, grad_made, ((0,), (0,)), BF)
-    expert_grads = (sum_groups(gate_term, 0), sum_groups(up_term, 0), sum_groups(down_term, 1))
-
-    grad_shared = (switch * error_all.astype(F32)).astype(BF)
-    grad_act_s = dot(grad_shared, shared_down, ((1,), (1,)))
-    switch_part = jnp.sum(acted_s.astype(F32) * grad_act_s, axis=1)
-    grad_gate_s = (grad_act_s * up_s * silu_slope(gate_s)).astype(BF)
-    grad_up_s = (grad_act_s * jax.nn.silu(gate_s)).astype(BF)
-
-    back_e = (dot(grad_gate_e, gate_w, ((1,), (1,))) + dot(grad_up_e, up_w, ((1,), (1,)))).astype(BF)
-
-    def back_part(rows):
+
+    far_task = None
+    if wide:
+        others = dp_size - 1
+        sides = (me % 2) ^ jnp.arange(2, dtype=jnp.int32)
+        in_order = (2 * jnp.arange(sp_size // 2, dtype=jnp.int32)[None, :] + sides[:, None]).reshape(-1)
+        in_order = jnp.argmax((in_order[:, None] ^ me) == jnp.array(ORDER, jnp.int32)[None, :], axis=1)
+        far_slots = slots_of(masks[:, 1:].transpose(1, 0, 2).reshape(others, total_rows))
+        sp_slots = far_slots.reshape(others, sp_size, tok_rows)[:, in_order].reshape(others, total_rows)
+
+        def pick_far(*rows_far):
+            far_probs = [steer_rows(rows.reshape(-1, width))[0] for rows in rows_far]
+            share = jnp.concatenate([jnp.sum(p * is_me[None, :], axis=1) for p in far_probs], 0)
+            share = share.reshape(sp_size, others, tok_rows).transpose(1, 0, 2).reshape(others, 1, total_rows)
+            share = jnp.where(sp_slots[:, None, :] == slot_range[None, :, None], share, 0.0)
+            share = jnp.sum(share, axis=2, keepdims=True)
+            return share, pick_rows(sp_slots, jnp.ones_like(share), *rows_far).reshape(-1, width)
+
+        far_task = (pick_far, *two_far)
+
+    error_low = error.astype(BF)
+    fetched_error = fetch_groups(error_low) if wide else []
+    *error_halves, far_work = gather_rows(error_low, far_task)
+    grad_shared = [(s[1] * rows.astype(F32)).astype(BF) for s, rows in zip(steered, error_halves)]
+    joined = lambda sides: jnp.concatenate(sides, 0)
+    down_term = dot(joined(acted_s), joined(grad_shared), ((0,), (0,)), BF)
+    grad_made = pick_rows(slots, share_rows[None], *(rows.reshape(blocks) for rows in error_halves))[0]
+    (grad_made,), (down_term, *fetched_error) = after((grad_made,), (down_term, *fetched_error))
+    down_shared = sum_groups(down_term, 1)
+    if wide:
+        far_own = jnp.stack(fetched_error, 0)
+        far_half = tok_rows // 2
+        far_x, far_y = swap(far_own, 2), swap(far_own, 4)
+    grad_gate_e, grad_up_e, back_e, gain_rows = expert_back(
+        grad_made, gate_e, up_e, acted_e, gateup_w, down_w
+    )
+
+    if wide:
+        (back_e,), (far_x, far_y) = after((back_e,), (far_x, far_y))
+        far_diag = jnp.concatenate([swap(far_y[:, :far_half], 2), swap(far_x[:, far_half:], 4)], 1)
+    grad_act_s = [dot(g, shared_down, ((1,), (1,))) for g in grad_shared]
+    switch_part = jnp.concatenate(
+        [jnp.sum(a.astype(F32) * g, axis=1) for a, g in zip(acted_s, grad_act_s)], 0
+    )
+    grad_gate_s = [(g * u * silu_slope(v)).astype(BF) for g, u, v in zip(grad_act_s, up_s, gate_s)]
+    grad_up_s = [(g * jax.nn.silu(v)).astype(BF) for g, v in zip(grad_act_s, gate_s)]
+
+    def back_part(side):
         return (
-            dot(grad_gate_s[rows], gate_sw, ((1,), (1,)))
-            + dot(grad_up_s[rows], up_sw, ((1,), (1,)))
-            + dot(pick[:, rows], back_e, ((0,), (0,)))
+            dot(grad_gate_s[side], gate_sw, ((1,), (1,)))
+            + dot(grad_up_s[side], up_sw, ((1,), (1,)))
+            + dot(pick[:, halves[side]], back_e, ((0,), (0,)))
         ).astype(BF)
 
-    back_upper = back_part(upper_half)
-    back_lower = back_part(lower_half)
+    back_upper = back_part(1)
+    back_lower = back_part(0)
     gain_tokens = jnp.sum(pick.astype(F32) * gain_rows, axis=0)
     scalars = jnp.concatenate(
         [gain_tokens[None, :] * is_me[:, None], switch_part[None, :], jnp.zeros((7, total_rows), F32)], axis=0
     )
-    scalars = sum_small(scalars.reshape(16, sp_size, tok_rows).transpose(1, 0, 2))
+    scalars, _ = sum_small(scalars.reshape(16, sp_size, tok_rows).transpose(1, 0, 2), jnp.zeros((1, 16, tok_rows), F32))
     gains, switch_sum = scalars[:experts].T, scalars[experts]
     my_probs, my_switch = probs[:tok_rows], switch[:tok_rows, 0]
     grad_switch = switch_sum * (1.0 - my_switch)
     grad_logits = gains - my_probs * jnp.sum(gains, axis=1, keepdims=True)
     steer = jnp.concatenate([grad_logits, grad_switch[:, None]], axis=1)
-    grad_normed = sum_rows(back_upper, back_lower) + jnp.einsum(
+    if wide:
+        (back_lower,), (far_diag,) = after((back_lower,), (far_diag,))
+        error_far = jnp.stack([far_own, far_x, far_y, far_diag], 0)
+        error_far = (error_far, swap(error_far, 1))
+    summed, (gate_term, up_term) = sum_rows(
+        back_upper,
+        back_lower,
+        (
+            lambda rows, *grads: [dot(rows, g, ((0,), (0,)), BF) for g in grads],
+            joined(two_halves),
+            joined(grad_gate_s),
+            joined(grad_up_s),
+        ),
+    )
+    gate_shared, up_shared = sum_groups(gate_term, 0), sum_groups(up_term, 0)
+    grad_normed = summed + jnp.einsum(
         "te,de->td", steer, heads_in.astype(F32), precision=HIGH
     )
     steer_term = jnp.einsum("te,td->ed", steer, normed_two.astype(F32), precision=HIGH)
     grad_middle_n, ffnnorm_term = norm_back(middle, inverse_two, gain_two, grad_normed)
     grad_middle = error + grad_middle_n
 
-    shared_terms = (
-        dot(two_all, grad_gate_s, ((0,), (0,)), BF),
-        dot(two_all, grad_up_s, ((0,), (0,)), BF),
-        dot(acted_s, grad_shared, ((0,), (0,)), BF),
-    )
-
-    attn_all = gather_rows(grad_middle.astype(BF))
-    grad_mixed = dot(attn_all, out_proj, ((1,), (1,)), BF)
+    far_task = None
+    if wide:
+        far_share, far_in = far_work
+        far_task = (lambda *rows: (pick_rows(far_slots, far_share, *rows).reshape(-1, width),), *error_far)
+    *attn_halves, far_work = gather_rows(grad_middle.astype(BF), far_task)
+    grad_mixed = joined([dot(rows, out_proj, ((1,), (1,)), BF) for rows in attn_halves])
     grad_q, grad_k, grad_v = attend_back(
         queries, key_rows, values, allowed, totals, grad_mixed
     )
@@ -355,20 +638,36 @@
     def input_part(rows):
         return sum(dot(grad_proj[j][rows], qkv_proj[j], ((1,), (1,))) for j in range(3)).astype(BF)
 
-    input_upper = input_part(upper_half)
-    input_lower = input_part(lower_half)
-    grad_normed_one = sum_rows(input_upper, input_lower)
+    input_upper = input_part(halves[1])
+    input_lower = input_part(halves[0])
+    normed_all = joined(normed_halves)
+    outproj_term = dot(mixed, joined(attn_halves), ((0,), (0,)), BF)
+    qkv_terms = jnp.stack([dot(normed_all, g, ((0,), (0,)), BF) for g in grad_proj], 0)
+    bias_term = jnp.stack([jnp.sum(g.astype(F32), axis=0) for g in grad_proj], 0)
+    if wide:
+        (far_made,) = far_work
+        grad_normed_one, far_work = sum_rows(
+            input_upper,
+            input_lower,
+            (lambda made, *terms: (*terms, made, *expert_far(far_in, made, gateup_w, down_w)), far_made, outproj_term, qkv_terms),
+        )
+        outproj_term, qkv_terms, far_made, far_act, far_gate, far_up = far_work
+        gateup_expert, down_expert = expert_grads_of(
+            (rows_in, grad_made, acted_e, grad_gate_e, grad_up_e),
+            (far_in, far_made, far_act, far_gate, far_up),
+        )
+    else:
+        grad_normed_one, _ = sum_rows(input_upper, input_lower)
+        gateup_expert = jnp.stack(
+            [
+                sum_groups(dot(rows_in, grad_gate_e, ((0,), (0,)), BF), 0),
+                sum_groups(dot(rows_in, grad_up_e, ((0,), (0,)), BF), 0),
+            ],
+            axis=1,
+        )
+        down_expert = sum_groups(dot(acted_e, grad_made, ((0,), (0,)), BF), 1)
     grad_input_n, attnnorm_term = norm_back(inputs, inverse_one, gain_one, grad_normed_one)
     hidden_grad = grad_middle + grad_input_n
-    outproj_term = dot(mixed, attn_all, ((0,), (0,)), BF)
-    qkv_terms = jnp.stack([dot(normed_all, g, ((0,), (0,)), BF) for g in grad_proj], 0)
-    bias_term = jnp.stack([jnp.sum(g.astype(F32), axis=0) for g in grad_proj], 0)
-
-    shared_grads = (
-        sum_groups(shared_terms[0], 0),
-        sum_groups(shared_terms[1], 0),
-        sum_groups(shared_terms[2], 1),
-    )
     outproj_grad = sum_groups(outproj_term, 1)
     qkvproj_grad = sum_groups(qkv_terms, 1)
 
@@ -376,10 +675,13 @@
     kinds = small.shape[0]
     cell = width // (dp_size * sp_size)
     small = small.reshape(kinds, dp_size, sp_size, cell).transpose(2, 1, 0, 3)[owners]
-    small = sum_small(small.reshape(sp_size, dp_size, kinds * cell))
+    small = small.reshape(sp_size, dp_size, kinds * cell)
+    small, squares = sum_small(small, jnp.full((1,) + small.shape[1:], squares, F32))
     pairs = bias_term.reshape(-1, HD)
     bias_cells = pairs.reshape(pairs.shape[0], dp_size, -1).transpose(1, 0, 2).reshape(dp_size, -1)
-    small = shift_groups(jnp.concatenate([small, bias_cells], axis=1))
+    small = jnp.concatenate([small, bias_cells], axis=1)
+    small, squares = shift_groups(small, jnp.full(small.shape[1:], squares[0, 0], F32))
+    loss_value = squares[0] / (2.0 * count * D)
     gains_out = small[: kinds * cell].reshape(kinds, cell)
     qkvbias_grad = small[kinds * cell :].reshape(3, -1, HD // dp_size)
     return (
@@ -392,11 +694,11 @@
         outproj_grad,
         gains_out[1],
         gains_out[2 : 2 + experts].T,
-        jnp.stack(shared_grads[:2], axis=1),
-        shared_grads[2],
+        jnp.stack([gate_shared, up_shared], axis=1),
+        down_shared,
         gains_out[2 + experts],
-        jnp.stack(expert_grads[:2], axis=1)[None],
-        expert_grads[2][None],
+        gateup_expert[None],
+        down_expert[None],
     )
 
 

time: 860 us -> 694 us (0.81)
  waiting for transfers between devices: 463 us -> 160 us
  Pallas kernels: 0 us -> 145 us
  matrix products: 196 us -> 129 us
  other arithmetic: 57.3 us -> 83.8 us
  starting transfers between devices: 56.3 us -> 75.7 us
  local copies, waits for them, and re-layouts: 58.3 us -> 68.6 us
    reduce_scatter x8 -> x5, waiting for transfers between devices: 304 us -> 17 us  [sum_groups(): lax.psum_scatter(grads, 'dp', scatter_dimension=dim, tiled=True).astype(F32)]
    pallas_call x0 -> x8, Pallas kernels: none -> 145 us  [the longest x1 43.3 us: expert_far(): local_call(expert_far_kernel, 'expert_far', 6 * count * width * hidden, g...]
    dot_general x56 -> x55, matrix products: 193 us -> 127 us  [dot(): lax.dot_general(left, right, (dims, ((), ())), preferred_element_type=F32)]
    ppermute x64 -> x55, waiting for transfers between devices: 151 us -> 98.9 us  [swap(): return lax.ppermute(values, 'sp', [(i, i ^ distance) for i in range(8)])]
    ppermute x5 -> x12, waiting for transfers between devices: 8.22 us -> 31 us  [the longest x9 31 us: fetch_groups(): lax.ppermute(own, 'dp', [((i + k) % size, i) for i in range(size)])]
    ppermute x5 -> x12, starting transfers between devices: 6.43 us -> 28.9 us  [the longest x9 24.3 us: fetch_groups(): lax.ppermute(own, 'dp', [((i + k) % size, i) for i in range(size)])]
    another operation x4 -> x13, other arithmetic: 3.62 us -> 18.3 us  [the longest x2 8.56 us: on_device(): error_far = jnp.stack([far_own, far_x, far_y, far_diag], 0)]
    slice x15 -> x19, local copies, waits for them, and re-layouts: 18.6 us -> 5.06 us  [the longest x1 1.21 us: on_device(): far_y[:, :far_half]]
  transfers between devices with their start and end apart: 77 -> 73, of which waited for: 44 -> 38; matrix products, arithmetic and copies ran while one was open for 25% -> 36% of each run, Pallas kernels for 0% -> 21%
where the time goes in v2:
time: 694 us; the launch traced here: 683 us
  waiting for transfers between devices  160 us (23%)
  Pallas kernels  145 us (21%)
  matrix products  129 us (19%)
  other arithmetic  83.8 us (12%)
  starting transfers between devices  75.7 us (11%)
  local copies, waits for them, and re-layouts  68.6 us (10%)
  between operations  21 us (3%)
    dot_general x55, matrix products, dot(): lax.dot_general(left, right, (dims, ((), ())), preferred_element_type=F32)  127 us
    ppermute x55, waiting for transfers between devices, swap(): return lax.ppermute(values, 'sp', [(i, i ^ distance) for i in range(8)])  98.9 us
    ppermute x55, starting transfers between devices, swap(): return lax.ppermute(values, 'sp', [(i, i ^ distance) for i in range(8)])  46 us
    pallas_call x1, Pallas kernels, expert_far(): local_call(expert_far_kernel, 'expert_far', 6 * count * width * hidden, g...  43.3 us
    pallas_call x4, Pallas kernels, pick_rows(): local_call(pick_kernel, 'pick_rows', 2 * groups * capacity * total * widt...  37 us
    unnamed x280, local copies, waits for them, and re-layouts  36.3 us
    ppermute x9, waiting for transfers between devices, fetch_groups(): lax.ppermute(own, 'dp', [((i + k) % size, i) for i in range(size)])  31 us
    pallas_call x1, Pallas kernels, expert_grads_of(): local_call(expert_grad_kernel, 'expert_grads', 6 * count * steps * share...  24.6 us
  transfers between devices with their start and end apart: 73, of which 38 were waited for; matrix products, arithmetic and copies ran while one was open for 36% of the time, Pallas kernels for 21%

profile of v2, /device:TPU:0, one launch (start us, length us, event | category | flops | bytes accessed | tf_op | source)
XLA Modules:
  0.0 682.6 jit_solution(10446013522640952012)
XLA Ops:
  20.1 11.3 %copy.121 = bf16[1,2048,2,1408]{3,1,2,0:T(8,128)(2,1)} copy(bf16[1,2048,2,1408]{3,2,1,0:T(2,128)(2,1)} %param.38) | data formatting | bytes 23068672 | tf_op args[13]
  65.2 12.3 %collective-permute-done.6 = bf16[128,2048]{1,0:T(8,128)(2,1)S(1)} collective-permute-done((bf16[128,2048]{1,0:T(8,128)(2,1)S(1)}, bf16[128,2048]{1,0:T(8,128)(2,1)S(1)}, u32[]{:S(2)}, u32[]{:S(2)}) %collective-permute-start.6) | collective-permute-done | bytes 524320 | tf_op jit(solution)/shard_map/ppermute | solution.py:44
  78.4 6.8 collective-permute-done.7
  86.4 5.6 collective-permute-done.9
  94.2 9.8 %collective-permute-done.11 = bf16[128,2048]{1,0:T(8,128)(2,1)S(1)} collective-permute-done((bf16[128,2048]{1,0:T(8,128)(2,1)S(1)}, bf16[128,2048]{1,0:T(8,128)(2,1)S(1)}, u32[]{:S(2)}, u32[]{:S(2)}) %collective-permute-start.11) | collective-permute-done | bytes 524320 | tf_op jit(solution)/shard_map/ppermute | solution.py:44
  122.8 6.2 collective-permute-done.23
  129.0 22.1 %collective-permute-done.22 = bf16[128,2048]{1,0:T(8,128)(2,1)S(1)} collective-permute-done((bf16[128,2048]{1,0:T(8,128)(2,1)S(1)}, bf16[128,2048]{1,0:T(8,128)(2,1)S(1)}, u32[]{:S(2)}, u32[]{:S(2)}) %collective-permute-start.22) | collective-permute-done | bytes 524320 | tf_op jit(solution)/shard_map/ppermute | solution.py:116
  152.5 11.8 %collective-permute-start.16 = (s32[1,4,128]{2,1,0:T(4,128)S(1)}, s32[1,4,128]{2,1,0:T(4,128)S(1)}, u32[]{:S(2)}, u32[]{:S(2)}) collective-permute-start(s32[1,4,128]{2,1,0:T(4,128)S(1)} %bitcast.377), channel_id=1, source_target_pairs={{24,0},{0,8},{8,16},{16,24},{25,1},{1,9},{9,17},{17,25},{26,2},{2,... | collective-permute-start | bytes 6152 | tf_op jit(solution)/shard_map/ppermute | solution.py:116
  190.9 18.9 %expert_forward.1 = (f32[576,1408]{1,0:T(8,128)}, f32[576,1408]{1,0:T(8,128)}, bf16[576,1408]{1,0:T(8,128)(2,1)}, bf16[576,2048]{1,0:T(8,128)(2,1)}) custom-call(bf16[576,2048]{1,0:T(8,128)(2,1)} %bitcast.338, bf16[2,2048,1408]{2,1,0:T(8,128)(2,1)} %bitcast.323, bf16[1408,2048]{1,0:T(8,128)(2,1)} %bitcast.382), custom_call_target="tpu_custom_call" | custom-call | flops 9965666304 | bytes 33218888 | tf_op jit(solution)/shard_map/expert_forward/pallas_call | solution.py:208
  220.0 13.2 %all-gather.3.cloned.1.call-done = bf16[12,128,2048]{2,1,0:T(8,128)(2,1)} async-done(((bf16[3,128,2048]{2,1,0:T(8,128)(2,1)}), bf16[12,128,2048]{2,1,0:T(8,128)(2,1)}) %all-gather.3.cloned.1.call-update) | async-done | bytes 6291472 | tf_op jit(solution)/shard_map/all_gather | solution.py:57
  234.0 5.9 multiply_convert_fusion.9
  255.9 7.3 %collective-permute-done.27 = bf16[128,2048]{1,0:T(8,128)(2,1)} collective-permute-done((bf16[128,2048]{1,0:T(8,128)(2,1)S(1)}, bf16[128,2048]{1,0:T(8,128)(2,1)}, u32[]{:S(2)}, u32[]{:S(2)}) %collective-permute-start.27) | collective-permute-done | bytes 524320 | tf_op jit(solution)/shard_map/ppermute | solution.py:44
  295.6 12.6 %pick_rows.5 = bf16[3,576,2048]{2,1,0:T(8,128)(2,1)} custom-call(s32[3,1,1024]{2,1,0:T(1,128)} %bitcast.367, f32[3,576,1]{2,1,0:T(8,128)} %broadcast_in_dim.87.scale_ref, bf16[4,3,128,2048]{3,2,1,0:T(8,128)(2,1)} %bitcast.327, bf16[4,3,128,2048]{3,2,1,0:T(8,128)(2,1)} %collective-permute-done.31.upper_ref), custom_call_target="tpu_custom_call" | custom-call | flops 7247757312 | bytes 24159192 | tf_op jit(solution)/shard_map/pick_rows/pallas_call | solution.py:154
  337.3 6.2 pick_rows.6
  343.5 6.0 fusion.6
  359.7 20.9 %expert_back.1 = (bf16[576,1408]{1,0:T(8,128)(2,1)}, bf16[576,1408]{1,0:T(8,128)(2,1)}, bf16[576,2048]{1,0:T(8,128)(2,1)}, f32[576,1]{1,0:T(8,128)}) custom-call(bf16[576,2048]{1,0:T(8,128)(2,1)} %bitcast.340, f32[576,1408]{1,0:T(8,128)} %get-tuple-element.138.gate_ref, f32[576,1408]{1,0:T(8,128)} %get-tuple-element.139.up_ref, ...), custom_call_target="tpu_custom_call" | custom-call | flops 9965666304 | bytes 33218888 | tf_op jit(solution)/shard_map/expert_back/pallas_call | solution.py:238
  382.5 5.7 fusion.11
  404.9 12.9 %collective-permute-done.41 = bf16[3,64,2048]{2,1,0:T(8,128)(2,1)S(1)} collective-permute-done((bf16[3,64,2048]{2,1,0:T(8,128)(2,1)S(1)}, bf16[3,64,2048]{2,1,0:T(8,128)(2,1)S(1)}, u32[]{:S(2)}, u32[]{:S(2)}) %collective-permute-start.41) | collective-permute-done | bytes 786464 | tf_op jit(solution)/shard_map/ppermute | solution.py:44
  434.6 6.6 convolution_convert_fusion
  460.3 12.7 %pick_rows.7 = bf16[3,576,2048]{2,1,0:T(8,128)(2,1)} custom-call(s32[3,1,1024]{2,1,0:T(1,128)} %bitcast.359, f32[3,576,1]{2,1,0:T(8,128)} %copy.107.scale_ref, bf16[4,3,128,2048]{3,2,1,0:T(8,128)(2,1)} %pad_maximum_fusion.lower_ref, bf16[4,3,128,2048]{3,2,1,0:T(8,128)(2,1)} %collective-permute-done.52.upper_ref), custom_call_target="tpu_custom_call" | custom-call | flops 7247757312 | bytes 24159192 | tf_op jit(solution)/shard_map/pick_rows/pallas_call | solution.py:154
  529.7 7.5 %fusion.241 = (bf16[512,2048]{1,0:T(8,128)(2,1)S(1)}, f32[512,2048]{1,0:T(8,128)}) fusion(bf16[512,2048]{1,0:T(8,128)(2,1)} %collective-permute-done.56, bf16[3,2048,256]{2,1,0:T(8,128)(2,1)} %param.30, bf16[1024,128]{0,1:T(8,128)(2,1)S(1)} %fusion.57, bf16[1024,128]{0,1:T(8,128)(2,1)S(1)} %fusion.60, f32[512,2048]{1,0:T(8,128)} %fusion.105, ...), kind=kOutput, calls=%fused_computation.532 | convolution fusion | flops 544735232 | bytes 18350080 | tf_op jit(solution)/shard_map/dot_general | solution.py:40
  539.6 43.3 %expert_far.1 = (bf16[1728,1408]{1,0:T(8,128)(2,1)}, bf16[1728,1408]{1,0:T(8,128)(2,1)}, bf16[1728,1408]{1,0:T(8,128)(2,1)}) custom-call(bf16[1728,2048]{1,0:T(8,128)(2,1)} %bitcast.332, bf16[1728,2048]{1,0:T(8,128)(2,1)} %bitcast.334, bf16[2,2048,1408]{2,1,0:T(8,128)(2,1)} %bitcast.325, bf16[1408,2048]{1,0:T(8,128)(2,1)} %bitcast.384), custom_call_target="tpu_custom_call" | custom-call | flops 29896998912 | bytes 99656664 | tf_op jit(solution)/shard_map/expert_far/pallas_call | solution.py:262
  607.3 24.6 %expert_grads.1 = (f32[512,2,1408]{2,1,0:T(2,128)}, f32[1408,512]{1,0:T(8,128)}) custom-call(s32[1]{0:T(128)} %bitcast.109._, bf16[576,2048]{1,0:T(8,128)(2,1)} %bitcast.339, bf16[576,2048]{1,0:T(8,128)(2,1)} %bitcast.341, bf16[576,1408]{1,0:T(8,128)(2,1)} %get-tuple-element.140.act_ref.act, bf16[576,1408]{1,0:T(8,128)(2,1)} %get-tuple-element.176.gg, ...), custom_call_target="tpu_custom_call" | custom-call | flops 9965666304 | bytes 33218888 | tf_op jit(solution)/shard_map/expert_grads/pallas_call | solution.py:306
  654.8 17.0 %reduce-scatter.6.cloned.1.call-done = bf16[3,512,256]{2,1,0:T(8,128)(2,1)} async-done(((bf16[3,2048,256]{2,1,0:T(8,128)(2,1)}), bf16[3,512,256]{2,1,0:T(8,128)(2,1)}) %reduce-scatter.6.cloned.1.call-update) | async-done | bytes 786448 | tf_op jit(solution)/shard_map/reduce_scatter | solution.py:97
  (703 shorter events, 354.6 us)
Async XLA Ops:
  7.2 226.0 %all-gather.3.cloned.1.call-start = ((), (), s32[]{:S(2)}) async-start(), calls=%async_computation.10 | async-start | bytes 7864320 | tf_op jit(solution)/shard_map/all_gather | solution.py:57
  11.4 20.9 %collective-permute-start.1 = (bf16[128,2048]{1,0:T(8,128)(2,1)S(1)}, bf16[128,2048]{1,0:T(8,128)(2,1)}, u32[]{:S(2)}, u32[]{:S(2)}) collective-permute-start(bf16[128,2048]{1,0:T(8,128)(2,1)S(1)} %get-tuple-element.201), channel_id=1, source_target_pairs={{0,4},{1,5},{2,6},{3,7},{4,0},{5,1},{6,2},{7,3},{8,12},{9,13},{10,... | collective-permute-start | bytes 1572872 | tf_op jit(solution)/shard_map/ppermute | solution.py:44
  113.8 37.2 %collective-permute-start.22 = (bf16[128,2048]{1,0:T(8,128)(2,1)S(1)}, bf16[128,2048]{1,0:T(8,128)(2,1)S(1)}, u32[]{:S(2)}, u32[]{:S(2)}) collective-permute-start(bf16[128,2048]{1,0:T(8,128)(2,1)S(1)} %get-tuple-element.206), channel_id=1, source_target_pairs={{16,0},{24,8},{0,16},{8,24},{17,1},{25,9},{1,17},{9,25},{18,2},{26... | collective-permute-start | bytes 1572872 | tf_op jit(solution)/shard_map/ppermute | solution.py:116
  116.5 34.5 %collective-permute-start.21 = (bf16[128,2048]{1,0:T(8,128)(2,1)S(1)}, bf16[128,2048]{1,0:T(8,128)(2,1)S(1)}, u32[]{:S(2)}, u32[]{:S(2)}) collective-permute-start(bf16[128,2048]{1,0:T(8,128)(2,1)S(1)} %get-tuple-element.206), channel_id=1, source_target_pairs={{8,0},{16,8},{24,16},{0,24},{9,1},{17,9},{25,17},{1,25},{10,2},{18... | collective-permute-start | bytes 1572872 | tf_op jit(solution)/shard_map/ppermute | solution.py:116
  152.4 442.6 %reduce-scatter.14.cloned.1.call-start = ((), (), s32[]{:S(2)}) async-start(), calls=%async_computation.9 | async-start | bytes 3604480 | tf_op jit(solution)/shard_map/reduce_scatter | solution.py:97
  217.1 26.9 %collective-permute-start.24 = (bf16[512,2048]{1,0:T(8,128)(2,1)}, bf16[512,2048]{1,0:T(8,128)(2,1)}, u32[]{:S(2)}, u32[]{:S(2)}) collective-permute-start(bf16[512,2048]{1,0:T(8,128)(2,1)} %add_convert_fusion.4), channel_id=1, source_target_pairs={{0,1},{1,0},{2,3},{3,2},{4,5},{5,4},{6,7},{7,6},{8,9},{9,8},{10,11... | collective-permute-start | bytes 6291464 | tf_op jit(solution)/shard_map/ppermute | solution.py:44
  233.2 51.4 %collective-permute-start.31 = (bf16[4,3,128,2048]{3,2,1,0:T(8,128)(2,1)}, bf16[4,3,128,2048]{3,2,1,0:T(8,128)(2,1)}, u32[]{:S(2)}, u32[]{:S(2)}) collective-permute-start(bf16[4,3,128,2048]{3,2,1,0:T(8,128)(2,1)} %bitcast.326), channel_id=1, source_target_pairs={{0,1},{1,0},{2,3},{3,2},{4,5},{5,4},{6,7},{7,6},{8,9},{9,8},{10,11... | collective-permute-start | bytes 18874376 | tf_op jit(solution)/shard_map/ppermute | solution.py:44
  278.7 70.8 %collective-permute-start.36 = (bf16[128,2048]{1,0:T(8,128)(2,1)}, bf16[128,2048]{1,0:T(8,128)(2,1)}, u32[]{:S(2)}, u32[]{:S(2)}) collective-permute-start(bf16[128,2048]{1,0:T(8,128)(2,1)} %get-tuple-element.208), channel_id=1, source_target_pairs={{16,0},{24,8},{0,16},{8,24},{17,1},{25,9},{1,17},{9,25},{18,2},{26... | collective-permute-start | bytes 1572872 | tf_op jit(solution)/shard_map/ppermute | solution.py:116
  281.1 68.5 %collective-permute-start.35 = (bf16[128,2048]{1,0:T(8,128)(2,1)}, bf16[128,2048]{1,0:T(8,128)(2,1)}, u32[]{:S(2)}, u32[]{:S(2)}) collective-permute-start(bf16[128,2048]{1,0:T(8,128)(2,1)} %get-tuple-element.208), channel_id=1, source_target_pairs={{8,0},{16,8},{24,16},{0,24},{9,1},{17,9},{25,17},{1,25},{10,2},{18... | collective-permute-start | bytes 1572872 | tf_op jit(solution)/shard_map/ppermute | solution.py:116
  282.5 67.0 %collective-permute-start.37 = (bf16[128,2048]{1,0:T(8,128)(2,1)}, bf16[128,2048]{1,0:T(8,128)(2,1)}, u32[]{:S(2)}, u32[]{:S(2)}) collective-permute-start(bf16[128,2048]{1,0:T(8,128)(2,1)} %get-tuple-element.208), channel_id=1, source_target_pairs={{24,0},{0,8},{8,16},{16,24},{25,1},{1,9},{9,17},{17,25},{26,2},{2,... | collective-permute-start | bytes 1572872 | tf_op jit(solution)/shard_map/ppermute | solution.py:116
  283.1 25.1 %collective-permute-start.30 = (bf16[128,2048]{1,0:T(8,128)(2,1)}, bf16[128,2048]{1,0:T(8,128)(2,1)}, u32[]{:S(2)}, u32[]{:S(2)}) collective-permute-start(bf16[128,2048]{1,0:T(8,128)(2,1)} %get-tuple-element.208), channel_id=1, source_target_pairs={{0,4},{1,5},{2,6},{3,7},{4,0},{5,1},{6,2},{7,3},{8,12},{9,13},{10,... | collective-permute-start | bytes 1572872 | tf_op jit(solution)/shard_map/ppermute | solution.py:44
  284.6 23.6 %collective-permute-start.29 = (bf16[128,2048]{1,0:T(8,128)(2,1)}, bf16[128,2048]{1,0:T(8,128)(2,1)}, u32[]{:S(2)}, u32[]{:S(2)}) collective-permute-start(bf16[128,2048]{1,0:T(8,128)(2,1)} %get-tuple-element.208), channel_id=1, source_target_pairs={{0,2},{1,3},{2,0},{3,1},{4,6},{5,7},{6,4},{7,5},{8,10},{9,11},{10,... | collective-permute-start | bytes 1572872 | tf_op jit(solution)/shard_map/ppermute | solution.py:44
  353.0 42.9 %collective-permute-start.39 = (bf16[3,128,2048]{2,1,0:T(8,128)(2,1)}, bf16[3,128,2048]{2,1,0:T(8,128)(2,1)}, u32[]{:S(2)}, u32[]{:S(2)}) collective-permute-start(bf16[3,128,2048]{2,1,0:T(8,128)(2,1)} %get-tuple-element.252), channel_id=1, source_target_pairs={{0,4},{1,5},{2,6},{3,7},{4,0},{5,1},{6,2},{7,3},{8,12},{9,13},{10,... | collective-permute-start | bytes 4718600 | tf_op jit(solution)/shard_map/ppermute | solution.py:44
  353.5 42.4 %collective-permute-start.38 = (bf16[3,128,2048]{2,1,0:T(8,128)(2,1)}, bf16[3,128,2048]{2,1,0:T(8,128)(2,1)}, u32[]{:S(2)}, u32[]{:S(2)}) collective-permute-start(bf16[3,128,2048]{2,1,0:T(8,128)(2,1)} %get-tuple-element.252), channel_id=1, source_target_pairs={{0,2},{1,3},{2,0},{3,1},{4,6},{5,7},{6,4},{7,5},{8,10},{9,11},{10,... | collective-permute-start | bytes 4718600 | tf_op jit(solution)/shard_map/ppermute | solution.py:44
  389.5 208.0 %reduce-scatter.10.cloned.1.call-start = ((), (), s32[]{:S(2)}) async-start(), calls=%async_computation.7 | async-start | bytes 3604480 | tf_op jit(solution)/shard_map/reduce_scatter | solution.py:97
  394.4 29.5 %collective-permute-start.49 = (f32[2,16,128]{2,1,0:T(8,128)S(1)}, f32[2,16,128]{2,1,0:T(8,128)S(1)}, u32[]{:S(2)}, u32[]{:S(2)}) collective-permute-start(f32[2,16,128]{2,1,0:T(8,128)S(1)} %pad_maximum_fusion.30), channel_id=1, source_target_pairs={{0,2},{1,3},{2,0},{3,1},{4,6},{5,7},{6,4},{7,5},{8,10},{9,11},{10,... | collective-permute-start | bytes 49160 | tf_op jit(solution)/shard_map/ppermute | solution.py:44
  402.7 21.3 %collective-permute-start.42 = (bf16[512,2048]{1,0:T(8,128)(2,1)S(1)}, bf16[512,2048]{1,0:T(8,128)(2,1)S(1)}, u32[]{:S(2)}, u32[]{:S(2)}) collective-permute-start(bf16[512,2048]{1,0:T(8,128)(2,1)S(1)} %add_convert_fusion.2), channel_id=1, source_target_pairs={{0,1},{1,0},{2,3},{3,2},{4,5},{5,4},{6,7},{7,6},{8,9},{9,8},{10,11... | collective-permute-start | bytes 6291464 | tf_op jit(solution)/shard_map/ppermute | solution.py:44
  423.7 36.6 %collective-permute-start.52 = (bf16[4,3,128,2048]{3,2,1,0:T(8,128)(2,1)}, bf16[4,3,128,2048]{3,2,1,0:T(8,128)(2,1)}, u32[]{:S(2)}, u32[]{:S(2)}) collective-permute-start(bf16[4,3,128,2048]{3,2,1,0:T(8,128)(2,1)} %pad_maximum_fusion.lower_ref), channel_id=1, source_target_pairs={{0,1},{1,0},{2,3},{3,2},{4,5},{5,4},{6,7},{7,6},{8,9},{9,8},{10,11... | collective-permute-start | bytes 18874376 | tf_op jit(solution)/shard_map/ppermute | solution.py:44
  443.7 153.8 %reduce-scatter.12.cloned.1.call-start = ((), (), s32[]{:S(2)}) async-start(), calls=%async_computation.8 | async-start | bytes 3604480 | tf_op jit(solution)/shard_map/reduce_scatter | solution.py:97
  485.2 167.8 %reduce-scatter.8.cloned.1.call-start = ((), (), s32[]{:S(2)}) async-start(), calls=%async_computation.6 | async-start | bytes 1310720 | tf_op jit(solution)/shard_map/reduce_scatter | solution.py:97
  537.3 45.6 %collective-permute-start.57 = (bf16[128,2048]{1,0:T(8,128)(2,1)S(1)}, bf16[128,2048]{1,0:T(8,128)(2,1)S(1)}, u32[]{:S(2)}, u32[]{:S(2)}) collective-permute-start(bf16[128,2048]{1,0:T(8,128)(2,1)S(1)} %pad_maximum_fusion.21), channel_id=1, source_target_pairs={{0,2},{1,3},{2,0},{3,1},{4,6},{5,7},{6,4},{7,5},{8,10},{9,11},{10,... | collective-permute-start | bytes 1572872 | tf_op jit(solution)/shard_map/ppermute | solution.py:44
  538.2 44.7 %collective-permute-start.58 = (bf16[128,2048]{1,0:T(8,128)(2,1)S(1)}, bf16[128,2048]{1,0:T(8,128)(2,1)S(1)}, u32[]{:S(2)}, u32[]{:S(2)}) collective-permute-start(bf16[128,2048]{1,0:T(8,128)(2,1)S(1)} %pad_maximum_fusion.22), channel_id=1, source_target_pairs={{0,4},{1,5},{2,6},{3,7},{4,0},{5,1},{6,2},{7,3},{8,12},{9,13},{10,... | collective-permute-start | bytes 1572872 | tf_op jit(solution)/shard_map/ppermute | solution.py:44
  582.9 88.9 %reduce-scatter.6.cloned.1.call-start = ((), (), s32[]{:S(2)}) async-start(), calls=%async_computation.5 | async-start | bytes 3932160 | tf_op jit(solution)/shard_map/reduce_scatter | solution.py:97
  606.1 25.7 %collective-permute-start.62 = (f32[3,4,704]{2,1,0:T(4,128)S(1)}, f32[3,4,704]{2,1,0:T(4,128)S(1)}, u32[]{:S(2)}, u32[]{:S(2)}) collective-permute-start(f32[3,4,704]{2,1,0:T(4,128)S(1)} %pad_maximum_fusion.27), channel_id=1, source_target_pairs={{0,4},{1,5},{2,6},{3,7},{4,0},{5,1},{6,2},{7,3},{8,12},{9,13},{10,... | collective-permute-start | bytes 101384 | tf_op jit(solution)/shard_map/ppermute | solution.py:44
  (179 other events, 1960.0 us)
Sparse Core Ops, SparseCore 0:
  152.5 80.6 all-gather.2
  389.6 56.2 reduce-scatter.13
  448.8 56.0 reduce-scatter.9
  507.6 56.0 reduce-scatter.11
  583.0 27.0 reduce-scatter.7
  612.3 59.3 reduce-scatter.5

commit v3 on v2

--- a/solution.py
+++ b/solution.py
@@ -44,18 +44,18 @@
     return lax.ppermute(values, "sp", [(i, i ^ distance) for i in range(8)])
 
 
-def gather_rows(own, task=None):
+def gather_rows(own, task=None, first=()):
     half = own.shape[0] // 2
     over_x, over_y = swap(own, 2), swap(own, 4)
     (over_x, over_y), work = between((own,), (over_x, over_y), task)
+    (over_x, over_y), first = after((over_x, over_y), first)
     far_top, far_bottom = swap(over_y[:half], 2), swap(over_x[half:], 4)
     lower = jnp.concatenate([own, over_x, over_y, far_top, far_bottom], 0)
-    return lower, swap(lower, 1), work
-
-
-def gather_far(own):
-    same = lax.all_gather(own, "sp", axis_index_groups=[[0, 2, 4, 6], [1, 3, 5, 7]])
-    return same, swap(same, 1)
+    return lower, swap(lower, 1), work, first
+
+
+def gather_side(own):
+    return lax.all_gather(own, "sp", axis_index_groups=[[0, 2, 4, 6], [1, 3, 5, 7]])
 
 
 def gather_small(own):
@@ -111,9 +111,13 @@
     return summed, jnp.sum(totals, axis=0)
 
 
-def fetch_groups(own):
+def fetch_groups(own, chained=True):
     size = lax.axis_size("dp")
-    return [lax.ppermute(own, "dp", [((i + k) % size, i) for i in range(size)]) for k in range(1, size)]
+    got = []
+    for k in range(1, size):
+        moved, _ = after((own,), got[-1:] if chained else ())
+        got.append(lax.ppermute(moved[0], "dp", [((i + k) % size, i) for i in range(size)]))
+    return got
 
 
 def own_columns(values, axis):
@@ -445,15 +449,10 @@
     inputs = hidden_in.astype(F32)
     gain_one = attn_norm.astype(F32)
     normed_f, inverse_one = normalize(inputs, gain_one)
-    *normed_halves, (gateup_w,) = gather_rows(
+    *normed_halves, (gateup_w,), _ = gather_rows(
         normed_f.astype(BF), (lambda w: (w.transpose(1, 0, 2),), expert_gateup[0])
     )
     wide = dp_size <= 4
-    route_own = routes.T[None]
-    if wide:
-        route_own = jnp.concatenate([route_own] + fetch_groups(route_own), 0)
-    route_all = gather_small(route_own.reshape(-1, tok_rows))
-    route_all = route_all.reshape(sp_size, -1, top_k, tok_rows)
 
     owners = me ^ jnp.array(ORDER, jnp.int32)
     place = (owners[:, None] * tok_rows + jnp.arange(tok_rows, dtype=jnp.int32)[None, :]).reshape(-1)
@@ -467,30 +466,34 @@
         & is_valid[None, :]
     )
 
-    masks = jnp.any(route_all == me, axis=2)
-    mask = masks[:, 0].reshape(total_rows)
-    slots = slots_of(mask)[None]
-    slot_range = jnp.arange(capacity, dtype=jnp.int32)
-    pick = (slots[0][None, :] == slot_range[:, None]).astype(BF)
-
     bias = qkv_bias.reshape(3, 1, -1).astype(F32)
-    projected = [
-        jnp.concatenate([dot(rows, qkv_proj[j], ((1,), (0,))) for rows in normed_halves], 0) + bias[j]
-        for j in range(3)
-    ]
+    normed_all = jnp.concatenate(normed_halves, 0)
+    projected = [dot(normed_all, qkv_proj[j], ((1,), (0,))) + bias[j] for j in range(3)]
     queries = rotate(projected[0], cosine, sine_table).astype(BF)
     key_rows = rotate(projected[1], cosine, sine_table).astype(BF)
     values = projected[2].astype(BF)
     mixed, totals = attend_forward(queries, key_rows, values, allowed)
     upper = dot(mixed[lower_rows:], out_proj, ((1,), (0,)), BF)
     lower = dot(mixed[:lower_rows], out_proj, ((1,), (0,)), BF)
+
+    (route_own,), _ = after((routes.T[None],), (mixed,))
+    if wide:
+        route_own = jnp.concatenate([route_own] + fetch_groups(route_own, False), 0)
+    route_all = gather_small(route_own.reshape(-1, tok_rows))
+    route_all = route_all.reshape(sp_size, -1, top_k, tok_rows)
+    masks = jnp.any(route_all == me, axis=2)
+    mask = masks[:, 0].reshape(total_rows)
+    slots = slots_of(mask)[None]
+    slot_range = jnp.arange(capacity, dtype=jnp.int32)
+    pick = (slots[0][None, :] == slot_range[:, None]).astype(BF)
+
     middle = inputs + sum_rows(upper, lower)[0]
 
     gain_two = ffn_norm.astype(F32)
     normed_two_f, inverse_two = normalize(middle, gain_two)
     normed_two = normed_two_f.astype(BF)
-    *two_halves, _ = gather_rows(normed_two)
-    fetched_two = fetch_groups(normed_two) if wide else []
+    fetched_two = fetch_groups(normed_two, False) if wide else []
+    *two_halves, _, (pick, slots) = gather_rows(normed_two, None, (pick, slots))
 
     heads_in = jnp.concatenate([router, shared_switch[:, None]], axis=1)
     is_me = (jnp.arange(experts) == me).astype(F32)
@@ -509,14 +512,12 @@
     ones = jnp.ones((1, capacity, 1), F32)
     rows_in = pick_rows(slots, ones, *(rows.reshape(blocks) for rows in two_halves))[0]
     gate_e, up_e, acted_e, made = expert_forward(rows_in, gateup_w, down_w)
+    two_halves, (made, *fetched_two) = after(two_halves, (made, *fetched_two))
 
     gate_sw, up_sw = shared_gateup[:, 0, :], shared_gateup[:, 1, :]
     gate_s = [dot(rows, gate_sw, ((1,), (0,))) for rows in two_halves]
     up_s = [dot(rows, up_sw, ((1,), (0,))) for rows in two_halves]
     acted_s = [(jax.nn.silu(g) * u).astype(BF) for g, u in zip(gate_s, up_s)]
-    (acted_s[1],), fetched_two = after((acted_s[1],), fetched_two)
-    if wide:
-        two_far = gather_far(jnp.stack(fetched_two, 0))
     halves = (slice(0, lower_rows), slice(lower_rows, None))
 
     def ffn_part(side):
@@ -528,39 +529,46 @@
     ffn_upper = ffn_part(1)
     ffn_lower = ffn_part(0)
     output = middle + sum_rows(ffn_upper, ffn_lower)[0]
-
     error = (output - teacher.astype(F32)) * local_valid[:, None]
     squares = jnp.sum(error * error)
     count = jnp.sum(seq_lengths).astype(F32)
 
-    far_task = None
     if wide:
         others = dp_size - 1
         sides = (me % 2) ^ jnp.arange(2, dtype=jnp.int32)
         in_order = (2 * jnp.arange(sp_size // 2, dtype=jnp.int32)[None, :] + sides[:, None]).reshape(-1)
-        in_order = jnp.argmax((in_order[:, None] ^ me) == jnp.array(ORDER, jnp.int32)[None, :], axis=1)
+        same_place = (in_order[:, None] ^ me) == jnp.array(ORDER, jnp.int32)[None, :]
+        in_order = jnp.argmax(same_place, axis=1)
         far_slots = slots_of(masks[:, 1:].transpose(1, 0, 2).reshape(others, total_rows))
         sp_slots = far_slots.reshape(others, sp_size, tok_rows)[:, in_order].reshape(others, total_rows)
 
-        def pick_far(*rows_far):
+        def share_far(*rows_far):
             far_probs = [steer_rows(rows.reshape(-1, width))[0] for rows in rows_far]
             share = jnp.concatenate([jnp.sum(p * is_me[None, :], axis=1) for p in far_probs], 0)
             share = share.reshape(sp_size, others, tok_rows).transpose(1, 0, 2).reshape(others, 1, total_rows)
             share = jnp.where(sp_slots[:, None, :] == slot_range[None, :, None], share, 0.0)
-            share = jnp.sum(share, axis=2, keepdims=True)
-            return share, pick_rows(sp_slots, jnp.ones_like(share), *rows_far).reshape(-1, width)
-
-        far_task = (pick_far, *two_far)
+            return jnp.sum(share, axis=2, keepdims=True)
 
     error_low = error.astype(BF)
     fetched_error = fetch_groups(error_low) if wide else []
-    *error_halves, far_work = gather_rows(error_low, far_task)
+    *error_halves, _, fetched_error[:1] = gather_rows(error_low, None, fetched_error[:1])
+    if wide:
+        fetched_two, _ = after(fetched_two, error_halves)
+        two_side = gather_side(jnp.stack(fetched_two, 0))
     grad_shared = [(s[1] * rows.astype(F32)).astype(BF) for s, rows in zip(steered, error_halves)]
     joined = lambda sides: jnp.concatenate(sides, 0)
-    down_term = dot(joined(acted_s), joined(grad_shared), ((0,), (0,)), BF)
+    grad_act_s = [dot(g, shared_down, ((1,), (1,))) for g in grad_shared]
+    grad_gate_s = [(g * u * silu_slope(v)).astype(BF) for g, u, v in zip(grad_act_s, up_s, gate_s)]
+    grad_up_s = [(g * jax.nn.silu(v)).astype(BF) for g, v in zip(grad_act_s, gate_s)]
+    own_act, own_grad = joined(acted_s), joined(grad_shared)
+    down_term = dot(own_act, own_grad, ((0,), (0,)), BF)
+    grad_up_s, (down_term, *fetched_error[1:2]) = after(grad_up_s, (down_term, *fetched_error[1:2]))
+    two_all = joined(two_halves)
+    mid_term = dot(two_all, jnp.concatenate([joined(grad_gate_s), joined(grad_up_s)], 1), ((0,), (0,)), BF)
     grad_made = pick_rows(slots, share_rows[None], *(rows.reshape(blocks) for rows in error_halves))[0]
-    (grad_made,), (down_term, *fetched_error) = after((grad_made,), (down_term, *fetched_error))
+    (grad_made,), (mid_term, *fetched_error[2:]) = after((grad_made,), (mid_term, *fetched_error[2:]))
     down_shared = sum_groups(down_term, 1)
+    mid_shared = sum_groups(mid_term, 0)
     if wide:
         far_own = jnp.stack(fetched_error, 0)
         far_half = tok_rows // 2
@@ -568,16 +576,12 @@
     grad_gate_e, grad_up_e, back_e, gain_rows = expert_back(
         grad_made, gate_e, up_e, acted_e, gateup_w, down_w
     )
-
     if wide:
         (back_e,), (far_x, far_y) = after((back_e,), (far_x, far_y))
         far_diag = jnp.concatenate([swap(far_y[:, :far_half], 2), swap(far_x[:, far_half:], 4)], 1)
-    grad_act_s = [dot(g, shared_down, ((1,), (1,))) for g in grad_shared]
     switch_part = jnp.concatenate(
         [jnp.sum(a.astype(F32) * g, axis=1) for a, g in zip(acted_s, grad_act_s)], 0
     )
-    grad_gate_s = [(g * u * silu_slope(v)).astype(BF) for g, u, v in zip(grad_act_s, up_s, gate_s)]
-    grad_up_s = [(g * jax.nn.silu(v)).astype(BF) for g, v in zip(grad_act_s, gate_s)]
 
     def back_part(side):
         return (
@@ -602,17 +606,17 @@
         (back_lower,), (far_diag,) = after((back_lower,), (far_diag,))
         error_far = jnp.stack([far_own, far_x, far_y, far_diag], 0)
         error_far = (error_far, swap(error_far, 1))
-    summed, (gate_term, up_term) = sum_rows(
-        back_upper,
-        back_lower,
-        (
-            lambda rows, *grads: [dot(rows, g, ((0,), (0,)), BF) for g in grads],
-            joined(two_halves),
-            joined(grad_gate_s),
-            joined(grad_up_s),
-        ),
-    )
-    gate_shared, up_shared = sum_groups(gate_term, 0), sum_groups(up_term, 0)
+        two_far = (two_side, swap(two_side, 1))
+    far_task = None
+    if wide:
+
+        def make_far(lower, upper, *rows_far):
+            share = share_far(*rows_far)
+            return pick_rows(far_slots, share, lower, upper).reshape(-1, width), *rows_far
+
+        far_task = (make_far, *error_far, *two_far)
+    (back_lower,), (down_shared,) = after((back_lower,), (down_shared,))
+    summed, far_work = sum_rows(back_upper, back_lower, far_task)
     grad_normed = summed + jnp.einsum(
         "te,de->td", steer, heads_in.astype(F32), precision=HIGH
     )
@@ -622,9 +626,10 @@
 
     far_task = None
     if wide:
-        far_share, far_in = far_work
-        far_task = (lambda *rows: (pick_rows(far_slots, far_share, *rows).reshape(-1, width),), *error_far)
-    *attn_halves, far_work = gather_rows(grad_middle.astype(BF), far_task)
+        far_made, *two_far = far_work
+        ones_far = jnp.ones((others, capacity, 1), F32)
+        far_task = (lambda *rows: (pick_rows(sp_slots, ones_far, *rows).reshape(-1, width),), *two_far)
+    *attn_halves, far_work, _ = gather_rows(grad_middle.astype(BF), far_task)
     grad_mixed = joined([dot(rows, out_proj, ((1,), (1,)), BF) for rows in attn_halves])
     grad_q, grad_k, grad_v = attend_back(
         queries, key_rows, values, allowed, totals, grad_mixed
@@ -640,18 +645,17 @@
 
     input_upper = input_part(halves[1])
     input_lower = input_part(halves[0])
-    normed_all = joined(normed_halves)
     outproj_term = dot(mixed, joined(attn_halves), ((0,), (0,)), BF)
     qkv_terms = jnp.stack([dot(normed_all, g, ((0,), (0,)), BF) for g in grad_proj], 0)
     bias_term = jnp.stack([jnp.sum(g.astype(F32), axis=0) for g in grad_proj], 0)
     if wide:
-        (far_made,) = far_work
+        (far_in,) = far_work
         grad_normed_one, far_work = sum_rows(
             input_upper,
             input_lower,
-            (lambda made, *terms: (*terms, made, *expert_far(far_in, made, gateup_w, down_w)), far_made, outproj_term, qkv_terms),
+            (lambda made, *_: (made, *expert_far(far_in, made, gateup_w, down_w)), far_made, outproj_term, qkv_terms, mid_shared),
         )
-        outproj_term, qkv_terms, far_made, far_act, far_gate, far_up = far_work
+        far_made, far_act, far_gate, far_up = far_work
         gateup_expert, down_expert = expert_grads_of(
             (rows_in, grad_made, acted_e, grad_gate_e, grad_up_e),
             (far_in, far_made, far_act, far_gate, far_up),
@@ -694,7 +698,7 @@
         outproj_grad,
         gains_out[1],
         gains_out[2 : 2 + experts].T,
-        jnp.stack([gate_shared, up_shared], axis=1),
+        mid_shared.reshape(-1, 2, gate_sw.shape[1]),
         down_shared,
         gains_out[2 + experts],
         gateup_expert[None],

time: 694 us -> 662 us (0.954)
  local copies, waits for them, and re-layouts: 68.6 us -> 53.6 us
  other arithmetic: 83.8 us -> 74.4 us
  matrix products: 129 us -> 121 us
    ppermute x55, waiting for transfers between devices: 98.9 us -> 125 us  [swap(): return lax.ppermute(values, 'sp', [(i, i ^ distance) for i in range(8)])]
    reduce_scatter x5 -> x4, waiting for transfers between devices: 17 us -> 0.02 us  [sum_groups(): lax.psum_scatter(grads, 'dp', scatter_dimension=dim, tiled=True).astype(F32)]
    all_gather x1, waiting for transfers between devices: 13.2 us -> 0.02 us  [gather_side(): lax.all_gather(own, 'sp', axis_index_groups=[[0, 2, 4, 6], [1, 3, 5, 7]])]
    dot_general x55 -> x51, matrix products: 127 us -> 120 us  [dot(): lax.dot_general(left, right, (dims, ((), ())), preferred_element_type=F32)]
    unnamed x280 -> x240, local copies, waits for them, and re-layouts: 36.3 us -> 31.8 us
  transfers between devices with their start and end apart: 73 -> 72, of which waited for: 38 -> 38; matrix products, arithmetic and copies ran while one was open for 36% -> 29% of each run, Pallas kernels for 21% -> 22%
where the time goes in v3:
time: 662 us; the launch traced here: 651 us
  waiting for transfers between devices  156 us (24%)
  Pallas kernels  145 us (22%)
  matrix products  121 us (18%)
  starting transfers between devices  78.4 us (12%)
  other arithmetic  74.4 us (11%)
  local copies, waits for them, and re-layouts  53.6 us (8%)
  between operations  22.3 us (3%)
    ppermute x55, waiting for transfers between devices, swap(): return lax.ppermute(values, 'sp', [(i, i ^ distance) for i in range(8)])  125 us
    dot_general x51, matrix products, dot(): lax.dot_general(left, right, (dims, ((), ())), preferred_element_type=F32)  120 us
    ppermute x55, starting transfers between devices, swap(): return lax.ppermute(values, 'sp', [(i, i ^ distance) for i in range(8)])  47.9 us
    pallas_call x1, Pallas kernels, expert_far(): local_call(expert_far_kernel, 'expert_far', 6 * count * width * hidden, g...  43.2 us
    pallas_call x4, Pallas kernels, pick_rows(): local_call(pick_kernel, 'pick_rows', 2 * groups * capacity * total * widt...  36.8 us
    unnamed x240, local copies, waits for them, and re-layouts  31.8 us
    ppermute x9, waiting for transfers between devices, fetch_groups(): lax.ppermute(moved[0], 'dp', [((i + k) % size, i) for i in range(size)])  31.2 us
    pallas_call x1, Pallas kernels, expert_grads_of(): local_call(expert_grad_kernel, 'expert_grads', 6 * count * steps * share...  24.6 us
  transfers between devices with their start and end apart: 72, of which 38 were waited for; matrix products, arithmetic and copies ran while one was open for 29% of the time, Pallas kernels for 22%

profile of v3, /device:TPU:0, one launch (start us, length us, event | category | flops | bytes accessed | tf_op | source)
XLA Modules:
  0.0 650.5 jit_solution(16842110951338207983)
XLA Ops:
  18.4 11.4 %copy.127 = bf16[1,2048,2,1408]{3,1,2,0:T(8,128)(2,1)} copy(bf16[1,2048,2,1408]{3,2,1,0:T(2,128)(2,1)} %param.38) | data formatting | bytes 23068672 | tf_op args[13]
  70.0 9.7 %collective-permute-done.6 = bf16[128,2048]{1,0:T(8,128)(2,1)S(1)} collective-permute-done((bf16[128,2048]{1,0:T(8,128)(2,1)S(1)}, bf16[128,2048]{1,0:T(8,128)(2,1)S(1)}, u32[]{:S(2)}, u32[]{:S(2)}) %collective-permute-start.6) | collective-permute-done | bytes 524320 | tf_op jit(solution)/shard_map/ppermute | solution.py:44
  81.9 5.6 collective-permute-done.16
  91.8 6.9 %collective-permute-done.9 = bf16[64,2048]{1,0:T(8,128)(2,1)} collective-permute-done((bf16[64,2048]{1,0:T(8,128)(2,1)}, bf16[64,2048]{1,0:T(8,128)(2,1)}, u32[]{:S(2)}, u32[]{:S(2)}) %collective-permute-start.9) | collective-permute-done | bytes 262176 | tf_op jit(solution)/shard_map/ppermute | solution.py:44
  104.3 10.3 %collective-permute-done.11 = bf16[128,2048]{1,0:T(8,128)(2,1)S(1)} collective-permute-done((bf16[128,2048]{1,0:T(8,128)(2,1)S(1)}, bf16[128,2048]{1,0:T(8,128)(2,1)S(1)}, u32[]{:S(2)}, u32[]{:S(2)}) %collective-permute-start.11) | collective-permute-done | bytes 524320 | tf_op jit(solution)/shard_map/ppermute | solution.py:44
  132.1 5.5 pick_rows.4
  137.6 19.0 %expert_forward.1 = (f32[576,1408]{1,0:T(8,128)}, f32[576,1408]{1,0:T(8,128)}, bf16[576,1408]{1,0:T(8,128)(2,1)}, bf16[576,2048]{1,0:T(8,128)(2,1)}) custom-call(bf16[576,2048]{1,0:T(8,128)(2,1)} %bitcast.317, bf16[2,2048,1408]{2,1,0:T(8,128)(2,1)} %bitcast.299, bf16[1408,2048]{1,0:T(8,128)(2,1)} %bitcast.358), custom_call_target="tpu_custom_call" | custom-call | flops 9965666304 | bytes 33218888 | tf_op jit(solution)/shard_map/expert_forward/pallas_call | solution.py:212
  165.3 5.2 multiply_convert_fusion.8
  187.5 11.7 %collective-permute-done.27 = bf16[128,2048]{1,0:T(8,128)(2,1)S(1)} collective-permute-done((bf16[128,2048]{1,0:T(8,128)(2,1)S(1)}, bf16[128,2048]{1,0:T(8,128)(2,1)S(1)}, u32[]{:S(2)}, u32[]{:S(2)}) %collective-permute-start.27) | collective-permute-done | bytes 524320 | tf_op jit(solution)/shard_map/ppermute | solution.py:44
  201.9 6.0 collective-permute-done.26
  210.5 12.8 %collective-permute-start.31 = (bf16[128,2048]{1,0:T(8,128)(2,1)}, bf16[128,2048]{1,0:T(8,128)(2,1)S(1)}, u32[]{:S(2)}, u32[]{:S(2)}) collective-permute-start(bf16[128,2048]{1,0:T(8,128)(2,1)} %get-tuple-element.152), channel_id=1, source_target_pairs={{8,0},{16,8},{24,16},{0,24},{9,1},{17,9},{25,17},{1,25},{10,2},{18... | collective-permute-start | bytes 1572872 | tf_op jit(solution)/shard_map/ppermute | solution.py:119
  225.4 7.4 %collective-permute-done.31 = bf16[128,2048]{1,0:T(8,128)(2,1)S(1)} collective-permute-done((bf16[128,2048]{1,0:T(8,128)(2,1)}, bf16[128,2048]{1,0:T(8,128)(2,1)S(1)}, u32[]{:S(2)}, u32[]{:S(2)}) %collective-permute-start.31) | collective-permute-done | bytes 524320 | tf_op jit(solution)/shard_map/ppermute | solution.py:119
  262.7 18.6 %collective-permute-done.35 = bf16[128,2048]{1,0:T(8,128)(2,1)S(1)} collective-permute-done((bf16[128,2048]{1,0:T(8,128)(2,1)}, bf16[128,2048]{1,0:T(8,128)(2,1)S(1)}, u32[]{:S(2)}, u32[]{:S(2)}) %collective-permute-start.35) | collective-permute-done | bytes 524320 | tf_op jit(solution)/shard_map/ppermute | solution.py:119
  294.7 15.9 %convolution_convert_fusion = bf16[2048,1408]{1,0:T(8,128)(2,1)} fusion(bf16[512,2048]{1,0:T(8,128)(2,1)S(1)} %copy-done.44, bf16[512,2048]{1,0:T(8,128)(2,1)S(1)} %copy-done.36, bf16[512,704]{0,1:T(8,128)(2,1)S(1)} %get-tuple-element.151, bf16[512,704]{0,1:T(8,128)(2,1)S(1)} %copy-done.61, bf16[512,704]{0,1:T(8,128)(2,1)S(1)} %get-tuple-element.269, ...), kind=kOutput, calls=%fused_computation.3 | convolution fusion | flops 5928386560 | bytes 12845056 | tf_op jit(solution)/shard_map/dot_general | solution.py:40
  310.6 5.7 pick_rows.5
  320.8 5.6 fusion.31
  326.5 21.4 %expert_back.1 = (bf16[576,1408]{1,0:T(8,128)(2,1)}, bf16[576,1408]{1,0:T(8,128)(2,1)}, bf16[576,2048]{1,0:T(8,128)(2,1)}, f32[576,1]{1,0:T(8,128)}) custom-call(bf16[576,2048]{1,0:T(8,128)(2,1)} %bitcast.319, f32[576,1408]{1,0:T(8,128)} %get-tuple-element.154.gate_ref, f32[576,1408]{1,0:T(8,128)} %get-tuple-element.155.up_ref, ...), custom_call_target="tpu_custom_call" | custom-call | flops 9965666304 | bytes 33218888 | tf_op jit(solution)/shard_map/expert_back/pallas_call | solution.py:242
  347.9 7.6 %collective-permute-done.38 = bf16[3,128,2048]{2,1,0:T(8,128)(2,1)} collective-permute-done((bf16[3,128,2048]{2,1,0:T(8,128)(2,1)}, bf16[3,128,2048]{2,1,0:T(8,128)(2,1)}, u32[]{:S(2)}, u32[]{:S(2)}) %collective-permute-start.38) | collective-permute-done | bytes 1572896 | tf_op jit(solution)/shard_map/ppermute | solution.py:44
  368.1 8.6 %collective-permute-done.40 = bf16[3,64,2048]{2,1,0:T(8,128)(2,1)S(1)} collective-permute-done((bf16[3,64,2048]{2,1,0:T(8,128)(2,1)S(1)}, bf16[3,64,2048]{2,1,0:T(8,128)(2,1)S(1)}, u32[]{:S(2)}, u32[]{:S(2)}) %collective-permute-start.40) | collective-permute-done | bytes 786464 | tf_op jit(solution)/shard_map/ppermute | solution.py:44
  378.0 5.5 pad_maximum_fusion.lower_ref
  428.8 12.7 %pick_rows.6 = bf16[3,576,2048]{2,1,0:T(8,128)(2,1)} custom-call(s32[3,1,1024]{2,1,0:T(1,128)} %bitcast.333, f32[3,576,1]{2,1,0:T(8,128)} %copy.111.scale_ref, bf16[4,3,128,2048]{3,2,1,0:T(8,128)(2,1)} %pad_maximum_fusion.lower_ref, bf16[4,3,128,2048]{3,2,1,0:T(8,128)(2,1)} %collective-permute-done.44.upper_ref), custom_call_target="tpu_custom_call" | custom-call | flops 7247757312 | bytes 24159192 | tf_op jit(solution)/shard_map/pick_rows/pallas_call | solution.py:158
  456.7 12.8 %pick_rows.7 = bf16[3,576,2048]{2,1,0:T(8,128)(2,1)} custom-call(s32[3,1,1024]{2,1,0:T(1,128)} %bitcast.341, f32[3,576,1]{2,1,0:T(8,128)} %broadcast_in_dim.91.scale_ref, bf16[4,3,128,2048]{3,2,1,0:T(8,128)(2,1)} %bitcast.303, bf16[4,3,128,2048]{3,2,1,0:T(8,128)(2,1)} %collective-permute-done.45.upper_ref), custom_call_target="tpu_custom_call" | custom-call | flops 7247757312 | bytes 24159192 | tf_op jit(solution)/shard_map/pick_rows/pallas_call | solution.py:158
  524.1 43.2 %expert_far.1 = (bf16[1728,1408]{1,0:T(8,128)(2,1)}, bf16[1728,1408]{1,0:T(8,128)(2,1)}, bf16[1728,1408]{1,0:T(8,128)(2,1)}) custom-call(bf16[1728,2048]{1,0:T(8,128)(2,1)} %bitcast.309, bf16[1728,2048]{1,0:T(8,128)(2,1)} %bitcast.307, bf16[2,2048,1408]{2,1,0:T(8,128)(2,1)} %bitcast.301, bf16[1408,2048]{1,0:T(8,128)(2,1)} %bitcast.360), custom_call_target="tpu_custom_call" | custom-call | flops 29896998912 | bytes 99656664 | tf_op jit(solution)/shard_map/expert_far/pallas_call | solution.py:266
  592.2 24.6 %expert_grads.1 = (f32[512,2,1408]{2,1,0:T(2,128)}, f32[1408,512]{1,0:T(8,128)}) custom-call(s32[1]{0:T(128)} %bitcast.104._, bf16[576,2048]{1,0:T(8,128)(2,1)} %bitcast.318, bf16[576,2048]{1,0:T(8,128)(2,1)} %bitcast.320, bf16[576,1408]{1,0:T(8,128)(2,1)} %get-tuple-element.156.act_ref.act, bf16[576,1408]{1,0:T(8,128)(2,1)} %get-tuple-element.198.gg, ...), custom_call_target="tpu_custom_call" | custom-call | flops 9965666304 | bytes 33218888 | tf_op jit(solution)/shard_map/expert_grads/pallas_call | solution.py:310
  (650 shorter events, 334.5 us)
Async XLA Ops:
  8.0 375.5 %all-gather.3.cloned.1.call-start = ((), (), s32[]{:S(2)}) async-start(), calls=%async_computation.8 | async-start | bytes 7864320 | tf_op jit(solution)/shard_map/all_gather | solution.py:58
  12.2 17.6 %collective-permute-start.1 = (bf16[128,2048]{1,0:T(8,128)(2,1)S(1)}, bf16[128,2048]{1,0:T(8,128)(2,1)}, u32[]{:S(2)}, u32[]{:S(2)}) collective-permute-start(bf16[128,2048]{1,0:T(8,128)(2,1)S(1)} %get-tuple-element.250), channel_id=1, source_target_pairs={{0,4},{1,5},{2,6},{3,7},{4,0},{5,1},{6,2},{7,3},{8,12},{9,13},{10,... | collective-permute-start | bytes 1572872 | tf_op jit(solution)/shard_map/ppermute | solution.py:44
  69.4 19.3 %collective-permute-start.8 = (bf16[128,2048]{1,0:T(8,128)(2,1)S(1)}, bf16[128,2048]{1,0:T(8,128)(2,1)S(1)}, u32[]{:S(2)}, u32[]{:S(2)}) collective-permute-start(bf16[128,2048]{1,0:T(8,128)(2,1)S(1)} %pad_maximum_fusion.13), channel_id=1, source_target_pairs={{0,4},{1,5},{2,6},{3,7},{4,0},{5,1},{6,2},{7,3},{8,12},{9,13},{10,... | collective-permute-start | bytes 1572872 | tf_op jit(solution)/shard_map/ppermute | solution.py:44
  122.9 33.7 %collective-permute-start.23 = (bf16[128,2048]{1,0:T(8,128)(2,1)S(1)}, bf16[128,2048]{1,0:T(8,128)(2,1)}, u32[]{:S(2)}, u32[]{:S(2)}) collective-permute-start(bf16[128,2048]{1,0:T(8,128)(2,1)S(1)} %get-tuple-element.244), channel_id=1, source_target_pairs={{24,0},{0,8},{8,16},{16,24},{25,1},{1,9},{9,17},{17,25},{26,2},{2,... | collective-permute-start | bytes 1572872 | tf_op jit(solution)/shard_map/ppermute | solution.py:119
  124.0 37.8 %collective-permute-start.22 = (bf16[128,2048]{1,0:T(8,128)(2,1)S(1)}, bf16[128,2048]{1,0:T(8,128)(2,1)}, u32[]{:S(2)}, u32[]{:S(2)}) collective-permute-start(bf16[128,2048]{1,0:T(8,128)(2,1)S(1)} %get-tuple-element.244), channel_id=1, source_target_pairs={{16,0},{24,8},{0,16},{8,24},{17,1},{25,9},{1,17},{9,25},{18,2},{26... | collective-permute-start | bytes 1572872 | tf_op jit(solution)/shard_map/ppermute | solution.py:119
  127.1 34.7 %collective-permute-start.21 = (bf16[128,2048]{1,0:T(8,128)(2,1)S(1)}, bf16[128,2048]{1,0:T(8,128)(2,1)}, u32[]{:S(2)}, u32[]{:S(2)}) collective-permute-start(bf16[128,2048]{1,0:T(8,128)(2,1)S(1)} %get-tuple-element.244), channel_id=1, source_target_pairs={{8,0},{16,8},{24,16},{0,24},{9,1},{17,9},{25,17},{1,25},{10,2},{18... | collective-permute-start | bytes 1572872 | tf_op jit(solution)/shard_map/ppermute | solution.py:119
  210.5 22.3 %collective-permute-start.31 = (bf16[128,2048]{1,0:T(8,128)(2,1)}, bf16[128,2048]{1,0:T(8,128)(2,1)S(1)}, u32[]{:S(2)}, u32[]{:S(2)}) collective-permute-start(bf16[128,2048]{1,0:T(8,128)(2,1)} %get-tuple-element.152), channel_id=1, source_target_pairs={{8,0},{16,8},{24,16},{0,24},{9,1},{17,9},{25,17},{1,25},{10,2},{18... | collective-permute-start | bytes 1572872 | tf_op jit(solution)/shard_map/ppermute | solution.py:119
  253.7 156.9 %reduce-scatter.5.cloned.1.call-start = ((), (), s32[]{:S(2)}) async-start(), calls=%async_computation.4 | async-start | bytes 3604480 | tf_op jit(solution)/shard_map/reduce_scatter | solution.py:97
  256.4 24.8 %collective-permute-start.35 = (bf16[128,2048]{1,0:T(8,128)(2,1)}, bf16[128,2048]{1,0:T(8,128)(2,1)S(1)}, u32[]{:S(2)}, u32[]{:S(2)}) collective-permute-start(bf16[128,2048]{1,0:T(8,128)(2,1)} %get-tuple-element.152), channel_id=1, source_target_pairs={{16,0},{24,8},{0,16},{8,24},{17,1},{25,9},{1,17},{9,25},{18,2},{26... | collective-permute-start | bytes 1572872 | tf_op jit(solution)/shard_map/ppermute | solution.py:119
  282.1 34.3 %collective-permute-start.36 = (bf16[128,2048]{1,0:T(8,128)(2,1)}, bf16[128,2048]{1,0:T(8,128)(2,1)}, u32[]{:S(2)}, u32[]{:S(2)}) collective-permute-start(bf16[128,2048]{1,0:T(8,128)(2,1)} %get-tuple-element.152), channel_id=1, source_target_pairs={{24,0},{0,8},{8,16},{16,24},{25,1},{1,9},{9,17},{17,25},{26,2},{2,... | collective-permute-start | bytes 1572872 | tf_op jit(solution)/shard_map/ppermute | solution.py:119
  318.9 36.7 %collective-permute-start.38 = (bf16[3,128,2048]{2,1,0:T(8,128)(2,1)}, bf16[3,128,2048]{2,1,0:T(8,128)(2,1)}, u32[]{:S(2)}, u32[]{:S(2)}) collective-permute-start(bf16[3,128,2048]{2,1,0:T(8,128)(2,1)} %get-tuple-element.288), channel_id=1, source_target_pairs={{0,4},{1,5},{2,6},{3,7},{4,0},{5,1},{6,2},{7,3},{8,12},{9,13},{10,... | collective-permute-start | bytes 4718600 | tf_op jit(solution)/shard_map/ppermute | solution.py:44
  319.4 36.4 %collective-permute-start.37 = (bf16[3,128,2048]{2,1,0:T(8,128)(2,1)}, bf16[3,128,2048]{2,1,0:T(8,128)(2,1)}, u32[]{:S(2)}, u32[]{:S(2)}) collective-permute-start(bf16[3,128,2048]{2,1,0:T(8,128)(2,1)} %get-tuple-element.288), channel_id=1, source_target_pairs={{0,2},{1,3},{2,0},{3,1},{4,6},{5,7},{6,4},{7,5},{8,10},{9,11},{10,... | collective-permute-start | bytes 4718600 | tf_op jit(solution)/shard_map/ppermute | solution.py:44
  326.4 194.4 %reduce-scatter.7.cloned.1.call-start = ((), (), s32[]{:S(2)}) async-start(), calls=%async_computation.5 | async-start | bytes 7208960 | tf_op jit(solution)/shard_map/reduce_scatter | solution.py:97
  358.2 18.5 %collective-permute-start.40 = (bf16[3,64,2048]{2,1,0:T(8,128)(2,1)S(1)}, bf16[3,64,2048]{2,1,0:T(8,128)(2,1)S(1)}, u32[]{:S(2)}, u32[]{:S(2)}) collective-permute-start(bf16[3,64,2048]{2,1,0:T(8,128)(2,1)S(1)} %slice.674), channel_id=1, source_target_pairs={{0,4},{1,5},{2,6},{3,7},{4,0},{5,1},{6,2},{7,3},{8,12},{9,13},{10,... | collective-permute-start | bytes 2359304 | tf_op jit(solution)/shard_map/ppermute | solution.py:44
  359.8 18.0 %collective-permute-start.39 = (bf16[3,64,2048]{2,1,0:T(8,128)(2,1)S(1)}, bf16[3,64,2048]{2,1,0:T(8,128)(2,1)S(1)}, u32[]{:S(2)}, u32[]{:S(2)}) collective-permute-start(bf16[3,64,2048]{2,1,0:T(8,128)(2,1)S(1)} %slice.673), channel_id=1, source_target_pairs={{0,2},{1,3},{2,0},{3,1},{4,6},{5,7},{6,4},{7,5},{8,10},{9,11},{10,... | collective-permute-start | bytes 2359304 | tf_op jit(solution)/shard_map/ppermute | solution.py:44
  383.4 36.6 %collective-permute-start.44 = (bf16[4,3,128,2048]{3,2,1,0:T(8,128)(2,1)}, bf16[4,3,128,2048]{3,2,1,0:T(8,128)(2,1)}, u32[]{:S(2)}, u32[]{:S(2)}) collective-permute-start(bf16[4,3,128,2048]{3,2,1,0:T(8,128)(2,1)} %pad_maximum_fusion.lower_ref), channel_id=1, source_target_pairs={{0,1},{1,0},{2,3},{3,2},{4,5},{5,4},{6,7},{7,6},{8,9},{9,8},{10,11... | collective-permute-start | bytes 18874376 | tf_op jit(solution)/shard_map/ppermute | solution.py:44
  383.6 36.5 %collective-permute-start.45 = (bf16[4,3,128,2048]{3,2,1,0:T(8,128)(2,1)}, bf16[4,3,128,2048]{3,2,1,0:T(8,128)(2,1)}, u32[]{:S(2)}, u32[]{:S(2)}) collective-permute-start(bf16[4,3,128,2048]{3,2,1,0:T(8,128)(2,1)} %bitcast.302), channel_id=1, source_target_pairs={{0,1},{1,0},{2,3},{3,2},{4,5},{5,4},{6,7},{7,6},{8,9},{9,8},{10,11... | collective-permute-start | bytes 18874376 | tf_op jit(solution)/shard_map/ppermute | solution.py:44
  409.5 179.6 %reduce-scatter.11.cloned.1.call-start = ((), (), s32[]{:S(2)}) async-start(), calls=%async_computation.7 | async-start | bytes 1310720 | tf_op jit(solution)/shard_map/reduce_scatter | solution.py:97
  417.9 23.6 %collective-permute-start.42 = (bf16[128,2048]{1,0:T(8,128)(2,1)S(1)}, bf16[128,2048]{1,0:T(8,128)(2,1)S(1)}, u32[]{:S(2)}, u32[]{:S(2)}) collective-permute-start(bf16[128,2048]{1,0:T(8,128)(2,1)S(1)} %pad_maximum_fusion.16), channel_id=1, source_target_pairs={{0,2},{1,3},{2,0},{3,1},{4,6},{5,7},{6,4},{7,5},{8,10},{9,11},{10,... | collective-permute-start | bytes 1572872 | tf_op jit(solution)/shard_map/ppermute | solution.py:44
  419.2 22.3 %collective-permute-start.43 = (bf16[128,2048]{1,0:T(8,128)(2,1)S(1)}, bf16[128,2048]{1,0:T(8,128)(2,1)}, u32[]{:S(2)}, u32[]{:S(2)}) collective-permute-start(bf16[128,2048]{1,0:T(8,128)(2,1)S(1)} %pad_maximum_fusion.17), channel_id=1, source_target_pairs={{0,4},{1,5},{2,6},{3,7},{4,0},{5,1},{6,2},{7,3},{8,12},{9,13},{10,... | collective-permute-start | bytes 1572872 | tf_op jit(solution)/shard_map/ppermute | solution.py:44
  503.7 135.6 %reduce-scatter.9.cloned.1.call-start = ((), (), s32[]{:S(2)}) async-start(), calls=%async_computation.6 | async-start | bytes 3932160 | tf_op jit(solution)/shard_map/reduce_scatter | solution.py:97
  521.8 45.5 %collective-permute-start.57 = (bf16[128,2048]{1,0:T(8,128)(2,1)S(1)}, bf16[128,2048]{1,0:T(8,128)(2,1)S(1)}, u32[]{:S(2)}, u32[]{:S(2)}) collective-permute-start(bf16[128,2048]{1,0:T(8,128)(2,1)S(1)} %pad_maximum_fusion.18), channel_id=1, source_target_pairs={{0,2},{1,3},{2,0},{3,1},{4,6},{5,7},{6,4},{7,5},{8,10},{9,11},{10,... | collective-permute-start | bytes 1572872 | tf_op jit(solution)/shard_map/ppermute | solution.py:44
  522.6 44.7 %collective-permute-start.58 = (bf16[128,2048]{1,0:T(8,128)(2,1)S(1)}, bf16[128,2048]{1,0:T(8,128)(2,1)S(1)}, u32[]{:S(2)}, u32[]{:S(2)}) collective-permute-start(bf16[128,2048]{1,0:T(8,128)(2,1)S(1)} %pad_maximum_fusion.19), channel_id=1, source_target_pairs={{0,4},{1,5},{2,6},{3,7},{4,0},{5,1},{6,2},{7,3},{8,12},{9,13},{10,... | collective-permute-start | bytes 1572872 | tf_op jit(solution)/shard_map/ppermute | solution.py:44
  591.7 25.1 %collective-permute-start.62 = (f32[3,4,704]{2,1,0:T(4,128)S(1)}, f32[3,4,704]{2,1,0:T(4,128)S(1)}, u32[]{:S(2)}, u32[]{:S(2)}) collective-permute-start(f32[3,4,704]{2,1,0:T(4,128)S(1)} %pad_maximum_fusion.24), channel_id=1, source_target_pairs={{0,4},{1,5},{2,6},{3,7},{4,0},{5,1},{6,2},{7,3},{8,12},{9,13},{10,... | collective-permute-start | bytes 101384 | tf_op jit(solution)/shard_map/ppermute | solution.py:44
  (158 other events, 1575.3 us)
Sparse Core Ops, SparseCore 0:
  253.8 67.6 all-gather.2
Sparse Core Ops, SparseCore 1:
  326.5 56.8 reduce-scatter.4
  409.5 101.2 reduce-scatter.6
  513.5 27.7 reduce-scatter.10
  569.1 60.8 reduce-scatter.8

commit v4 on v3

--- a/solution.py
+++ b/solution.py
@@ -512,12 +512,13 @@
     ones = jnp.ones((1, capacity, 1), F32)
     rows_in = pick_rows(slots, ones, *(rows.reshape(blocks) for rows in two_halves))[0]
     gate_e, up_e, acted_e, made = expert_forward(rows_in, gateup_w, down_w)
-    two_halves, (made, *fetched_two) = after(two_halves, (made, *fetched_two))
+    two_halves, (made, *fetched_two[:1]) = after(two_halves, (made, *fetched_two[:1]))
 
     gate_sw, up_sw = shared_gateup[:, 0, :], shared_gateup[:, 1, :]
     gate_s = [dot(rows, gate_sw, ((1,), (0,))) for rows in two_halves]
     up_s = [dot(rows, up_sw, ((1,), (0,))) for rows in two_halves]
     acted_s = [(jax.nn.silu(g) * u).astype(BF) for g, u in zip(gate_s, up_s)]
+    (acted_s[1],), fetched_two[1:2] = after((acted_s[1],), fetched_two[1:2])
     halves = (slice(0, lower_rows), slice(lower_rows, None))
 
     def ffn_part(side):
@@ -528,6 +529,7 @@
 
     ffn_upper = ffn_part(1)
     ffn_lower = ffn_part(0)
+    (ffn_lower,), fetched_two[2:] = after((ffn_lower,), fetched_two[2:])
     output = middle + sum_rows(ffn_upper, ffn_lower)[0]
     error = (output - teacher.astype(F32)) * local_valid[:, None]
     squares = jnp.sum(error * error)
@@ -550,11 +552,16 @@
             return jnp.sum(share, axis=2, keepdims=True)
 
     error_low = error.astype(BF)
-    fetched_error = fetch_groups(error_low) if wide else []
+    fetched_error = fetch_groups(error_low, False) if wide else []
     *error_halves, _, fetched_error[:1] = gather_rows(error_low, None, fetched_error[:1])
     if wide:
-        fetched_two, _ = after(fetched_two, error_halves)
+        fetched_two, _ = after(fetched_two, (output,))
         two_side = gather_side(jnp.stack(fetched_two, 0))
+    grad_made = pick_rows(slots, share_rows[None], *(rows.reshape(blocks) for rows in error_halves))[0]
+    grad_gate_e, grad_up_e, back_e, gain_rows = expert_back(
+        grad_made, gate_e, up_e, acted_e, gateup_w, down_w
+    )
+    error_halves, (back_e, *fetched_error[1:2]) = after(error_halves, (back_e, *fetched_error[1:2]))
     grad_shared = [(s[1] * rows.astype(F32)).astype(BF) for s, rows in zip(steered, error_halves)]
     joined = lambda sides: jnp.concatenate(sides, 0)
     grad_act_s = [dot(g, shared_down, ((1,), (1,))) for g in grad_shared]
@@ -562,22 +569,17 @@
     grad_up_s = [(g * jax.nn.silu(v)).astype(BF) for g, v in zip(grad_act_s, gate_s)]
     own_act, own_grad = joined(acted_s), joined(grad_shared)
     down_term = dot(own_act, own_grad, ((0,), (0,)), BF)
-    grad_up_s, (down_term, *fetched_error[1:2]) = after(grad_up_s, (down_term, *fetched_error[1:2]))
-    two_all = joined(two_halves)
-    mid_term = dot(two_all, jnp.concatenate([joined(grad_gate_s), joined(grad_up_s)], 1), ((0,), (0,)), BF)
-    grad_made = pick_rows(slots, share_rows[None], *(rows.reshape(blocks) for rows in error_halves))[0]
-    (grad_made,), (mid_term, *fetched_error[2:]) = after((grad_made,), (mid_term, *fetched_error[2:]))
-    down_shared = sum_groups(down_term, 1)
-    mid_shared = sum_groups(mid_term, 0)
+    grad_up_s, (down_term, *fetched_error[2:]) = after(grad_up_s, (down_term, *fetched_error[2:]))
     if wide:
         far_own = jnp.stack(fetched_error, 0)
         far_half = tok_rows // 2
         far_x, far_y = swap(far_own, 2), swap(far_own, 4)
-    grad_gate_e, grad_up_e, back_e, gain_rows = expert_back(
-        grad_made, gate_e, up_e, acted_e, gateup_w, down_w
-    )
-    if wide:
-        (back_e,), (far_x, far_y) = after((back_e,), (far_x, far_y))
+    two_all = joined(two_halves)
+    mid_term = dot(two_all, jnp.concatenate([joined(grad_gate_s), joined(grad_up_s)], 1), ((0,), (0,)), BF)
+    down_shared = sum_groups(down_term, 1)
+    mid_shared = sum_groups(mid_term, 0)
+    if wide:
+        (back_e,), (far_x, far_y, _) = after((back_e,), (far_x, far_y, mid_term))
         far_diag = jnp.concatenate([swap(far_y[:, :far_half], 2), swap(far_x[:, far_half:], 4)], 1)
     switch_part = jnp.concatenate(
         [jnp.sum(a.astype(F32) * g, axis=1) for a, g in zip(acted_s, grad_act_s)], 0

time: 662 us -> 658 us (level)
  matrix products: 121 us -> 114 us
    ppermute x55, waiting for transfers between devices: 125 us -> 133 us  [swap(): return lax.ppermute(values, 'sp', [(i, i ^ distance) for i in range(8)])]
    unnamed x240 -> x228, local copies, waits for them, and re-layouts: 31.8 us -> 29.8 us
  transfers between devices with their start and end apart: 72 -> 72, of which waited for: 38 -> 35; matrix products, arithmetic and copies ran while one was open for 29% -> 30% of each run, Pallas kernels for 22% -> 22%
where the time goes in v4:
time: 658 us; the launch traced here: 646 us
  waiting for transfers between devices  162 us (25%)
  Pallas kernels  144 us (22%)
  matrix products  114 us (17%)
  starting transfers between devices  78 us (12%)
  other arithmetic  73.2 us (11%)
  local copies, waits for them, and re-layouts  51.7 us (8%)
  between operations  22.2 us (3%)
    ppermute x55, waiting for transfers between devices, swap(): return lax.ppermute(values, 'sp', [(i, i ^ distance) for i in range(8)])  133 us
    dot_general x51, matrix products, dot(): lax.dot_general(left, right, (dims, ((), ())), preferred_element_type=F32)  113 us
    ppermute x55, starting transfers between devices, swap(): return lax.ppermute(values, 'sp', [(i, i ^ distance) for i in range(8)])  47.7 us
    pallas_call x1, Pallas kernels, expert_far(): local_call(expert_far_kernel, 'expert_far', 6 * count * width * hidden, g...  43.2 us
    pallas_call x4, Pallas kernels, pick_rows(): local_call(pick_kernel, 'pick_rows', 2 * groups * capacity * total * widt...  36.5 us
    unnamed x228, local copies, waits for them, and re-layouts  29.8 us
    ppermute x9, waiting for transfers between devices, fetch_groups(): lax.ppermute(moved[0], 'dp', [((i + k) % size, i) for i in range(size)])  28.6 us
    ppermute x9, starting transfers between devices, fetch_groups(): lax.ppermute(moved[0], 'dp', [((i + k) % size, i) for i in range(size)])  26.1 us
  transfers between devices with their start and end apart: 72, of which 35 were waited for; matrix products, arithmetic and copies ran while one was open for 30% of the time, Pallas kernels for 22%

profile of v4, /device:TPU:0, one launch (start us, length us, event | category | flops | bytes accessed | tf_op | source)
XLA Modules:
  0.0 645.7 jit_solution(10185892230439077101)
XLA Ops:
  18.4 11.4 %copy.127 = bf16[1,2048,2,1408]{3,1,2,0:T(8,128)(2,1)} copy(bf16[1,2048,2,1408]{3,2,1,0:T(2,128)(2,1)} %param.38) | data formatting | bytes 23068672 | tf_op args[13]
  70.0 9.7 %collective-permute-done.6 = bf16[128,2048]{1,0:T(8,128)(2,1)S(1)} collective-permute-done((bf16[128,2048]{1,0:T(8,128)(2,1)S(1)}, bf16[128,2048]{1,0:T(8,128)(2,1)S(1)}, u32[]{:S(2)}, u32[]{:S(2)}) %collective-permute-start.6) | collective-permute-done | bytes 524320 | tf_op jit(solution)/shard_map/ppermute | solution.py:44
  81.9 5.6 collective-permute-done.16
  91.8 6.9 %collective-permute-done.9 = bf16[64,2048]{1,0:T(8,128)(2,1)} collective-permute-done((bf16[64,2048]{1,0:T(8,128)(2,1)}, bf16[64,2048]{1,0:T(8,128)(2,1)}, u32[]{:S(2)}, u32[]{:S(2)}) %collective-permute-start.9) | collective-permute-done | bytes 262176 | tf_op jit(solution)/shard_map/ppermute | solution.py:44
  104.3 10.3 %collective-permute-done.11 = bf16[128,2048]{1,0:T(8,128)(2,1)S(1)} collective-permute-done((bf16[128,2048]{1,0:T(8,128)(2,1)S(1)}, bf16[128,2048]{1,0:T(8,128)(2,1)S(1)}, u32[]{:S(2)}, u32[]{:S(2)}) %collective-permute-start.11) | collective-permute-done | bytes 524320 | tf_op jit(solution)/shard_map/ppermute | solution.py:44
  133.0 5.5 pick_rows.4
  138.5 19.0 %expert_forward.1 = (f32[576,1408]{1,0:T(8,128)}, f32[576,1408]{1,0:T(8,128)}, bf16[576,1408]{1,0:T(8,128)(2,1)}, bf16[576,2048]{1,0:T(8,128)(2,1)}) custom-call(bf16[576,2048]{1,0:T(8,128)(2,1)} %bitcast.317, bf16[2,2048,1408]{2,1,0:T(8,128)(2,1)} %bitcast.299, bf16[1408,2048]{1,0:T(8,128)(2,1)} %bitcast.358), custom_call_target="tpu_custom_call" | custom-call | flops 9965666304 | bytes 33218888 | tf_op jit(solution)/shard_map/expert_forward/pallas_call | solution.py:212
  188.4 11.6 %collective-permute-done.27 = bf16[128,2048]{1,0:T(8,128)(2,1)S(1)} collective-permute-done((bf16[128,2048]{1,0:T(8,128)(2,1)S(1)}, bf16[128,2048]{1,0:T(8,128)(2,1)S(1)}, u32[]{:S(2)}, u32[]{:S(2)}) %collective-permute-start.27) | collective-permute-done | bytes 524320 | tf_op jit(solution)/shard_map/ppermute | solution.py:44
  202.8 6.0 collective-permute-done.26
  220.3 16.3 %collective-permute-done.31 = bf16[128,2048]{1,0:T(8,128)(2,1)S(1)} collective-permute-done((bf16[128,2048]{1,0:T(8,128)(2,1)}, bf16[128,2048]{1,0:T(8,128)(2,1)S(1)}, u32[]{:S(2)}, u32[]{:S(2)}) %collective-permute-start.31) | collective-permute-done | bytes 524320 | tf_op jit(solution)/shard_map/ppermute | solution.py:119
  239.1 11.1 %collective-permute-done.32 = bf16[64,2048]{1,0:T(8,128)(2,1)S(1)} collective-permute-done((bf16[64,2048]{1,0:T(8,128)(2,1)S(1)}, bf16[64,2048]{1,0:T(8,128)(2,1)S(1)}, u32[]{:S(2)}, u32[]{:S(2)}) %collective-permute-start.32) | collective-permute-done | bytes 262176 | tf_op jit(solution)/shard_map/ppermute | solution.py:44
  252.5 12.2 %collective-permute-start.35 = (bf16[128,2048]{1,0:T(8,128)(2,1)}, bf16[128,2048]{1,0:T(8,128)(2,1)S(1)}, u32[]{:S(2)}, u32[]{:S(2)}) collective-permute-start(bf16[128,2048]{1,0:T(8,128)(2,1)} %get-tuple-element.242), channel_id=1, source_target_pairs={{16,0},{24,8},{0,16},{8,24},{17,1},{25,9},{1,17},{9,25},{18,2},{26... | collective-permute-start | bytes 1572872 | tf_op jit(solution)/shard_map/ppermute | solution.py:119
  266.0 5.5 pick_rows.5
  271.5 21.0 %expert_back.1 = (bf16[576,1408]{1,0:T(8,128)(2,1)}, bf16[576,1408]{1,0:T(8,128)(2,1)}, bf16[576,2048]{1,0:T(8,128)(2,1)}, f32[576,1]{1,0:T(8,128)}) custom-call(bf16[576,2048]{1,0:T(8,128)(2,1)} %bitcast.319, f32[576,1408]{1,0:T(8,128)} %get-tuple-element.152.gate_ref, f32[576,1408]{1,0:T(8,128)} %get-tuple-element.153.up_ref, ...), custom_call_target="tpu_custom_call" | custom-call | flops 9965666304 | bytes 33218888 | tf_op jit(solution)/shard_map/expert_back/pallas_call | solution.py:242
  292.5 7.3 %collective-permute-done.35 = bf16[128,2048]{1,0:T(8,128)(2,1)S(1)} collective-permute-done((bf16[128,2048]{1,0:T(8,128)(2,1)}, bf16[128,2048]{1,0:T(8,128)(2,1)S(1)}, u32[]{:S(2)}, u32[]{:S(2)}) %collective-permute-start.35) | collective-permute-done | bytes 524320 | tf_op jit(solution)/shard_map/ppermute | solution.py:119
  317.7 5.6 fusion.31
  324.5 10.7 %convolution_convert_fusion = bf16[2048,1408]{1,0:T(8,128)(2,1)} fusion(bf16[512,2048]{1,0:T(8,128)(2,1)} %copy-done.42, bf16[512,2048]{1,0:T(8,128)(2,1)} %copy-done.34, bf16[512,704]{0,1:T(8,128)(2,1)S(1)} %copy-done.56, bf16[512,704]{0,1:T(8,128)(2,1)} %get-tuple-element.158, bf16[512,704]{0,1:T(8,128)(2,1)} %get-tuple-element.272, ...), kind=kOutput, calls=%fused_computation.3 | convolution fusion | flops 5928386560 | bytes 12845056 | tf_op jit(solution)/shard_map/dot_general | solution.py:40
  335.2 17.6 %collective-permute-done.38 = bf16[3,128,2048]{2,1,0:T(8,128)(2,1)} collective-permute-done((bf16[3,128,2048]{2,1,0:T(8,128)(2,1)}, bf16[3,128,2048]{2,1,0:T(8,128)(2,1)}, u32[]{:S(2)}, u32[]{:S(2)}) %collective-permute-start.38) | collective-permute-done | bytes 1572896 | tf_op jit(solution)/shard_map/ppermute | solution.py:44
  364.9 8.7 %collective-permute-done.40 = bf16[3,64,2048]{2,1,0:T(8,128)(2,1)S(1)} collective-permute-done((bf16[3,64,2048]{2,1,0:T(8,128)(2,1)S(1)}, bf16[3,64,2048]{2,1,0:T(8,128)(2,1)S(1)}, u32[]{:S(2)}, u32[]{:S(2)}) %collective-permute-start.40) | collective-permute-done | bytes 786464 | tf_op jit(solution)/shard_map/ppermute | solution.py:44
  375.0 5.5 pad_maximum_fusion.lower_ref
  425.6 12.8 %pick_rows.6 = bf16[3,576,2048]{2,1,0:T(8,128)(2,1)} custom-call(s32[3,1,1024]{2,1,0:T(1,128)} %bitcast.333, f32[3,576,1]{2,1,0:T(8,128)} %copy.111.scale_ref, bf16[4,3,128,2048]{3,2,1,0:T(8,128)(2,1)} %pad_maximum_fusion.lower_ref, bf16[4,3,128,2048]{3,2,1,0:T(8,128)(2,1)} %collective-permute-done.44.upper_ref), custom_call_target="tpu_custom_call" | custom-call | flops 7247757312 | bytes 24159192 | tf_op jit(solution)/shard_map/pick_rows/pallas_call | solution.py:158
  454.0 12.8 %pick_rows.7 = bf16[3,576,2048]{2,1,0:T(8,128)(2,1)} custom-call(s32[3,1,1024]{2,1,0:T(1,128)} %bitcast.341, f32[3,576,1]{2,1,0:T(8,128)} %broadcast_in_dim.91.scale_ref, bf16[4,3,128,2048]{3,2,1,0:T(8,128)(2,1)} %bitcast.303, bf16[4,3,128,2048]{3,2,1,0:T(8,128)(2,1)} %collective-permute-done.45.upper_ref), custom_call_target="tpu_custom_call" | custom-call | flops 7247757312 | bytes 24159192 | tf_op jit(solution)/shard_map/pick_rows/pallas_call | solution.py:158
  520.7 43.2 %expert_far.1 = (bf16[1728,1408]{1,0:T(8,128)(2,1)}, bf16[1728,1408]{1,0:T(8,128)(2,1)}, bf16[1728,1408]{1,0:T(8,128)(2,1)}) custom-call(bf16[1728,2048]{1,0:T(8,128)(2,1)} %bitcast.309, bf16[1728,2048]{1,0:T(8,128)(2,1)} %bitcast.307, bf16[2,2048,1408]{2,1,0:T(8,128)(2,1)} %bitcast.301, bf16[1408,2048]{1,0:T(8,128)(2,1)} %bitcast.360), custom_call_target="tpu_custom_call" | custom-call | flops 29896998912 | bytes 99656664 | tf_op jit(solution)/shard_map/expert_far/pallas_call | solution.py:266
  589.4 24.7 %expert_grads.1 = (f32[512,2,1408]{2,1,0:T(2,128)}, f32[1408,512]{1,0:T(8,128)}) custom-call(s32[1]{0:T(128)} %bitcast.104._, bf16[576,2048]{1,0:T(8,128)(2,1)} %bitcast.318, bf16[576,2048]{1,0:T(8,128)(2,1)} %bitcast.320, bf16[576,1408]{1,0:T(8,128)(2,1)} %get-tuple-element.154.act_ref.act, bf16[576,1408]{1,0:T(8,128)(2,1)} %get-tuple-element.200.gg, ...), custom_call_target="tpu_custom_call" | custom-call | flops 9965666304 | bytes 33218888 | tf_op jit(solution)/shard_map/expert_grads/pallas_call | solution.py:310
  (638 shorter events, 322.6 us)
Async XLA Ops:
  8.0 372.5 %all-gather.3.cloned.1.call-start = ((), (), s32[]{:S(2)}) async-start(), calls=%async_computation.8 | async-start | bytes 7864320 | tf_op jit(solution)/shard_map/all_gather | solution.py:58
  69.5 19.3 %collective-permute-start.8 = (bf16[128,2048]{1,0:T(8,128)(2,1)S(1)}, bf16[128,2048]{1,0:T(8,128)(2,1)S(1)}, u32[]{:S(2)}, u32[]{:S(2)}) collective-permute-start(bf16[128,2048]{1,0:T(8,128)(2,1)S(1)} %pad_maximum_fusion.13), channel_id=1, source_target_pairs={{0,4},{1,5},{2,6},{3,7},{4,0},{5,1},{6,2},{7,3},{8,12},{9,13},{10,... | collective-permute-start | bytes 1572872 | tf_op jit(solution)/shard_map/ppermute | solution.py:44
  123.0 48.2 %collective-permute-start.23 = (bf16[128,2048]{1,0:T(8,128)(2,1)S(1)}, bf16[128,2048]{1,0:T(8,128)(2,1)}, u32[]{:S(2)}, u32[]{:S(2)}) collective-permute-start(bf16[128,2048]{1,0:T(8,128)(2,1)S(1)} %get-tuple-element.246), channel_id=1, source_target_pairs={{16,0},{24,8},{0,16},{8,24},{17,1},{25,9},{1,17},{9,25},{18,2},{26... | collective-permute-start | bytes 1572872 | tf_op jit(solution)/shard_map/ppermute | solution.py:119
  125.6 59.1 %collective-permute-start.22 = (bf16[128,2048]{1,0:T(8,128)(2,1)S(1)}, bf16[128,2048]{1,0:T(8,128)(2,1)}, u32[]{:S(2)}, u32[]{:S(2)}) collective-permute-start(bf16[128,2048]{1,0:T(8,128)(2,1)S(1)} %get-tuple-element.246), channel_id=1, source_target_pairs={{24,0},{0,8},{8,16},{16,24},{25,1},{1,9},{9,17},{17,25},{26,2},{2,... | collective-permute-start | bytes 1572872 | tf_op jit(solution)/shard_map/ppermute | solution.py:119
  127.2 35.3 %collective-permute-start.21 = (bf16[128,2048]{1,0:T(8,128)(2,1)S(1)}, bf16[128,2048]{1,0:T(8,128)(2,1)}, u32[]{:S(2)}, u32[]{:S(2)}) collective-permute-start(bf16[128,2048]{1,0:T(8,128)(2,1)S(1)} %get-tuple-element.246), channel_id=1, source_target_pairs={{8,0},{16,8},{24,16},{0,24},{9,1},{17,9},{25,17},{1,25},{10,2},{18... | collective-permute-start | bytes 1572872 | tf_op jit(solution)/shard_map/ppermute | solution.py:119
  213.9 193.6 %reduce-scatter.5.cloned.1.call-start = ((), (), s32[]{:S(2)}) async-start(), calls=%async_computation.4 | async-start | bytes 3604480 | tf_op jit(solution)/shard_map/reduce_scatter | solution.py:97
  216.2 20.4 %collective-permute-start.31 = (bf16[128,2048]{1,0:T(8,128)(2,1)}, bf16[128,2048]{1,0:T(8,128)(2,1)S(1)}, u32[]{:S(2)}, u32[]{:S(2)}) collective-permute-start(bf16[128,2048]{1,0:T(8,128)(2,1)} %get-tuple-element.242), channel_id=1, source_target_pairs={{8,0},{16,8},{24,16},{0,24},{9,1},{17,9},{25,17},{1,25},{10,2},{18... | collective-permute-start | bytes 1572872 | tf_op jit(solution)/shard_map/ppermute | solution.py:119
  218.2 18.4 %collective-permute-start.30 = (bf16[128,2048]{1,0:T(8,128)(2,1)}, bf16[128,2048]{1,0:T(8,128)(2,1)S(1)}, u32[]{:S(2)}, u32[]{:S(2)}) collective-permute-start(bf16[128,2048]{1,0:T(8,128)(2,1)} %get-tuple-element.242), channel_id=1, source_target_pairs={{0,4},{1,5},{2,6},{3,7},{4,0},{5,1},{6,2},{7,3},{8,12},{9,13},{10,... | collective-permute-start | bytes 1572872 | tf_op jit(solution)/shard_map/ppermute | solution.py:44
  252.5 47.3 %collective-permute-start.35 = (bf16[128,2048]{1,0:T(8,128)(2,1)}, bf16[128,2048]{1,0:T(8,128)(2,1)S(1)}, u32[]{:S(2)}, u32[]{:S(2)}) collective-permute-start(bf16[128,2048]{1,0:T(8,128)(2,1)} %get-tuple-element.242), channel_id=1, source_target_pairs={{16,0},{24,8},{0,16},{8,24},{17,1},{25,9},{1,17},{9,25},{18,2},{26... | collective-permute-start | bytes 1572872 | tf_op jit(solution)/shard_map/ppermute | solution.py:119
  264.7 48.9 %collective-permute-start.36 = (bf16[128,2048]{1,0:T(8,128)(2,1)}, bf16[128,2048]{1,0:T(8,128)(2,1)}, u32[]{:S(2)}, u32[]{:S(2)}) collective-permute-start(bf16[128,2048]{1,0:T(8,128)(2,1)} %get-tuple-element.242), channel_id=1, source_target_pairs={{24,0},{0,8},{8,16},{16,24},{25,1},{1,9},{9,17},{17,25},{26,2},{2,... | collective-permute-start | bytes 1572872 | tf_op jit(solution)/shard_map/ppermute | solution.py:119
  316.4 36.4 %collective-permute-start.38 = (bf16[3,128,2048]{2,1,0:T(8,128)(2,1)}, bf16[3,128,2048]{2,1,0:T(8,128)(2,1)}, u32[]{:S(2)}, u32[]{:S(2)}) collective-permute-start(bf16[3,128,2048]{2,1,0:T(8,128)(2,1)} %get-tuple-element.290), channel_id=1, source_target_pairs={{0,4},{1,5},{2,6},{3,7},{4,0},{5,1},{6,2},{7,3},{8,12},{9,13},{10,... | collective-permute-start | bytes 4718600 | tf_op jit(solution)/shard_map/ppermute | solution.py:44
  317.0 36.1 %collective-permute-start.37 = (bf16[3,128,2048]{2,1,0:T(8,128)(2,1)}, bf16[3,128,2048]{2,1,0:T(8,128)(2,1)}, u32[]{:S(2)}, u32[]{:S(2)}) collective-permute-start(bf16[3,128,2048]{2,1,0:T(8,128)(2,1)} %get-tuple-element.290), channel_id=1, source_target_pairs={{0,2},{1,3},{2,0},{3,1},{4,6},{5,7},{6,4},{7,5},{8,10},{9,11},{10,... | collective-permute-start | bytes 4718600 | tf_op jit(solution)/shard_map/ppermute | solution.py:44
  323.4 194.2 %reduce-scatter.7.cloned.1.call-start = ((), (), s32[]{:S(2)}) async-start(), calls=%async_computation.5 | async-start | bytes 7208960 | tf_op jit(solution)/shard_map/reduce_scatter | solution.py:97
  355.5 18.1 %collective-permute-start.40 = (bf16[3,64,2048]{2,1,0:T(8,128)(2,1)S(1)}, bf16[3,64,2048]{2,1,0:T(8,128)(2,1)S(1)}, u32[]{:S(2)}, u32[]{:S(2)}) collective-permute-start(bf16[3,64,2048]{2,1,0:T(8,128)(2,1)S(1)} %slice.674), channel_id=1, source_target_pairs={{0,4},{1,5},{2,6},{3,7},{4,0},{5,1},{6,2},{7,3},{8,12},{9,13},{10,... | collective-permute-start | bytes 2359304 | tf_op jit(solution)/shard_map/ppermute | solution.py:44
  357.1 17.8 %collective-permute-start.39 = (bf16[3,64,2048]{2,1,0:T(8,128)(2,1)S(1)}, bf16[3,64,2048]{2,1,0:T(8,128)(2,1)S(1)}, u32[]{:S(2)}, u32[]{:S(2)}) collective-permute-start(bf16[3,64,2048]{2,1,0:T(8,128)(2,1)S(1)} %slice.673), channel_id=1, source_target_pairs={{0,2},{1,3},{2,0},{3,1},{4,6},{5,7},{6,4},{7,5},{8,10},{9,11},{10,... | collective-permute-start | bytes 2359304 | tf_op jit(solution)/shard_map/ppermute | solution.py:44
  380.4 36.5 %collective-permute-start.44 = (bf16[4,3,128,2048]{3,2,1,0:T(8,128)(2,1)}, bf16[4,3,128,2048]{3,2,1,0:T(8,128)(2,1)}, u32[]{:S(2)}, u32[]{:S(2)}) collective-permute-start(bf16[4,3,128,2048]{3,2,1,0:T(8,128)(2,1)} %pad_maximum_fusion.lower_ref), channel_id=1, source_target_pairs={{0,1},{1,0},{2,3},{3,2},{4,5},{5,4},{6,7},{7,6},{8,9},{9,8},{10,11... | collective-permute-start | bytes 18874376 | tf_op jit(solution)/shard_map/ppermute | solution.py:44
  380.5 36.4 %collective-permute-start.45 = (bf16[4,3,128,2048]{3,2,1,0:T(8,128)(2,1)}, bf16[4,3,128,2048]{3,2,1,0:T(8,128)(2,1)}, u32[]{:S(2)}, u32[]{:S(2)}) collective-permute-start(bf16[4,3,128,2048]{3,2,1,0:T(8,128)(2,1)} %bitcast.302), channel_id=1, source_target_pairs={{0,1},{1,0},{2,3},{3,2},{4,5},{5,4},{6,7},{7,6},{8,9},{9,8},{10,11... | collective-permute-start | bytes 18874376 | tf_op jit(solution)/shard_map/ppermute | solution.py:44
  405.8 179.9 %reduce-scatter.11.cloned.1.call-start = ((), (), s32[]{:S(2)}) async-start(), calls=%async_computation.7 | async-start | bytes 1310720 | tf_op jit(solution)/shard_map/reduce_scatter | solution.py:97
  414.8 23.6 %collective-permute-start.42 = (bf16[128,2048]{1,0:T(8,128)(2,1)S(1)}, bf16[128,2048]{1,0:T(8,128)(2,1)S(1)}, u32[]{:S(2)}, u32[]{:S(2)}) collective-permute-start(bf16[128,2048]{1,0:T(8,128)(2,1)S(1)} %pad_maximum_fusion.16), channel_id=1, source_target_pairs={{0,2},{1,3},{2,0},{3,1},{4,6},{5,7},{6,4},{7,5},{8,10},{9,11},{10,... | collective-permute-start | bytes 1572872 | tf_op jit(solution)/shard_map/ppermute | solution.py:44
  416.1 22.3 %collective-permute-start.43 = (bf16[128,2048]{1,0:T(8,128)(2,1)S(1)}, bf16[128,2048]{1,0:T(8,128)(2,1)}, u32[]{:S(2)}, u32[]{:S(2)}) collective-permute-start(bf16[128,2048]{1,0:T(8,128)(2,1)S(1)} %pad_maximum_fusion.17), channel_id=1, source_target_pairs={{0,4},{1,5},{2,6},{3,7},{4,0},{5,1},{6,2},{7,3},{8,12},{9,13},{10,... | collective-permute-start | bytes 1572872 | tf_op jit(solution)/shard_map/ppermute | solution.py:44
  500.4 134.0 %reduce-scatter.9.cloned.1.call-start = ((), (), s32[]{:S(2)}) async-start(), calls=%async_computation.6 | async-start | bytes 3932160 | tf_op jit(solution)/shard_map/reduce_scatter | solution.py:97
  518.6 45.3 %collective-permute-start.57 = (bf16[128,2048]{1,0:T(8,128)(2,1)S(1)}, bf16[128,2048]{1,0:T(8,128)(2,1)S(1)}, u32[]{:S(2)}, u32[]{:S(2)}) collective-permute-start(bf16[128,2048]{1,0:T(8,128)(2,1)S(1)} %pad_maximum_fusion.18), channel_id=1, source_target_pairs={{0,2},{1,3},{2,0},{3,1},{4,6},{5,7},{6,4},{7,5},{8,10},{9,11},{10,... | collective-permute-start | bytes 1572872 | tf_op jit(solution)/shard_map/ppermute | solution.py:44
  519.8 44.1 %collective-permute-start.58 = (bf16[128,2048]{1,0:T(8,128)(2,1)S(1)}, bf16[128,2048]{1,0:T(8,128)(2,1)S(1)}, u32[]{:S(2)}, u32[]{:S(2)}) collective-permute-start(bf16[128,2048]{1,0:T(8,128)(2,1)S(1)} %pad_maximum_fusion.19), channel_id=1, source_target_pairs={{0,4},{1,5},{2,6},{3,7},{4,0},{5,1},{6,2},{7,3},{8,12},{9,13},{10,... | collective-permute-start | bytes 1572872 | tf_op jit(solution)/shard_map/ppermute | solution.py:44
  588.3 25.7 %collective-permute-start.62 = (f32[3,4,704]{2,1,0:T(4,128)S(1)}, f32[3,4,704]{2,1,0:T(4,128)S(1)}, u32[]{:S(2)}, u32[]{:S(2)}) collective-permute-start(f32[3,4,704]{2,1,0:T(4,128)S(1)} %pad_maximum_fusion.24), channel_id=1, source_target_pairs={{0,4},{1,5},{2,6},{3,7},{4,0},{5,1},{6,2},{7,3},{8,12},{9,13},{10,... | collective-permute-start | bytes 101384 | tf_op jit(solution)/shard_map/ppermute | solution.py:44
  (152 other events, 1566.4 us)
Sparse Core Ops, SparseCore 0:
  214.0 86.2 all-gather.2
Sparse Core Ops, SparseCore 1:
  323.5 54.1 reduce-scatter.4
  405.9 99.2 reduce-scatter.6
  507.9 27.7 reduce-scatter.10
  566.4 57.7 reduce-scatter.8

commit v5 on v4

--- a/solution.py
+++ b/solution.py
@@ -153,7 +153,7 @@
     blocks, groups, count, width = lower.shape
     total = 2 * blocks * count
     capacity = scale.shape[1]
-    tile = 1024
+    tile = 2048
     rows = pl.BlockSpec((blocks, None, count, tile), lambda g, j: (0, g, 0, j))
     return local_call(
         pick_kernel,
@@ -579,8 +579,7 @@
     down_shared = sum_groups(down_term, 1)
     mid_shared = sum_groups(mid_term, 0)
     if wide:
-        (back_e,), (far_x, far_y, _) = after((back_e,), (far_x, far_y, mid_term))
-        far_diag = jnp.concatenate([swap(far_y[:, :far_half], 2), swap(far_x[:, far_half:], 4)], 1)
+        (back_e, far_own), _ = after((back_e, far_own), (mid_term,))
     switch_part = jnp.concatenate(
         [jnp.sum(a.astype(F32) * g, axis=1) for a, g in zip(acted_s, grad_act_s)], 0
     )
@@ -593,6 +592,9 @@
         ).astype(BF)
 
     back_upper = back_part(1)
+    if wide:
+        (back_e,), (far_x, far_y, _) = after((back_e,), (far_x, far_y, back_upper))
+        far_diag = jnp.concatenate([swap(far_y[:, :far_half], 2), swap(far_x[:, far_half:], 4)], 1)
     back_lower = back_part(0)
     gain_tokens = jnp.sum(pick.astype(F32) * gain_rows, axis=0)
     scalars = jnp.concatenate(

time: 658 us -> 641 us (0.974)
  waiting for transfers between devices: 162 us -> 148 us
  local copies, waits for them, and re-layouts: 51.7 us -> 59.5 us
    ppermute x55, waiting for transfers between devices: 133 us -> 124 us  [swap(): return lax.ppermute(values, 'sp', [(i, i ^ distance) for i in range(8)])]
    ppermute x9, starting transfers between devices: 26.1 us -> 17.6 us  [fetch_groups(): lax.ppermute(moved[0], 'dp', [((i + k) % size, i) for i in range(size)])]
    unnamed x228 -> x230, local copies, waits for them, and re-layouts: 29.8 us -> 35.1 us
  transfers between devices with their start and end apart: 72 -> 72, of which waited for: 35 -> 36; matrix products, arithmetic and copies ran while one was open for 30% -> 32% of each run, Pallas kernels for 22% -> 23%
where the time goes in v5:
time: 641 us; the launch traced here: 630 us
  waiting for transfers between devices  148 us (23%)
  Pallas kernels  146 us (23%)
  matrix products  112 us (17%)
  starting transfers between devices  71.7 us (11%)
  other arithmetic  69.7 us (11%)
  local copies, waits for them, and re-layouts  59.5 us (9%)
  between operations  22.2 us (3%)
    ppermute x55, waiting for transfers between devices, swap(): return lax.ppermute(values, 'sp', [(i, i ^ distance) for i in range(8)])  124 us
    dot_general x51, matrix products, dot(): lax.dot_general(left, right, (dims, ((), ())), preferred_element_type=F32)  111 us
    ppermute x55, starting transfers between devices, swap(): return lax.ppermute(values, 'sp', [(i, i ^ distance) for i in range(8)])  49.6 us
    pallas_call x1, Pallas kernels, expert_far(): local_call(expert_far_kernel, 'expert_far', 6 * count * width * hidden, g...  43.2 us
    pallas_call x4, Pallas kernels, pick_rows(): local_call(pick_kernel, 'pick_rows', 2 * groups * capacity * total * widt...  37.6 us
    unnamed x230, local copies, waits for them, and re-layouts  35.1 us
    pallas_call x1, Pallas kernels, expert_grads_of(): local_call(expert_grad_kernel, 'expert_grads', 6 * count * steps * share...  24.7 us
    ppermute x9, waiting for transfers between devices, fetch_groups(): lax.ppermute(moved[0], 'dp', [((i + k) % size, i) for i in range(size)])  23.7 us
  transfers between devices with their start and end apart: 72, of which 36 were waited for; matrix products, arithmetic and copies ran while one was open for 32% of the time, Pallas kernels for 23%

profile of v5, /device:TPU:0, one launch (start us, length us, event | category | flops | bytes accessed | tf_op | source)
XLA Modules:
  0.0 629.7 jit_solution(16546172601257026255)
XLA Ops:
  18.4 11.4 %copy.127 = bf16[1,2048,2,1408]{3,1,2,0:T(8,128)(2,1)} copy(bf16[1,2048,2,1408]{3,2,1,0:T(2,128)(2,1)} %param.38) | data formatting | bytes 23068672 | tf_op args[13]
  70.0 9.7 %collective-permute-done.6 = bf16[128,2048]{1,0:T(8,128)(2,1)S(1)} collective-permute-done((bf16[128,2048]{1,0:T(8,128)(2,1)S(1)}, bf16[128,2048]{1,0:T(8,128)(2,1)S(1)}, u32[]{:S(2)}, u32[]{:S(2)}) %collective-permute-start.6) | collective-permute-done | bytes 524320 | tf_op jit(solution)/shard_map/ppermute | solution.py:44
  81.9 5.6 collective-permute-done.16
  91.8 6.8 %collective-permute-done.9 = bf16[64,2048]{1,0:T(8,128)(2,1)} collective-permute-done((bf16[64,2048]{1,0:T(8,128)(2,1)}, bf16[64,2048]{1,0:T(8,128)(2,1)}, u32[]{:S(2)}, u32[]{:S(2)}) %collective-permute-start.9) | collective-permute-done | bytes 262176 | tf_op jit(solution)/shard_map/ppermute | solution.py:44
  104.3 10.3 %collective-permute-done.11 = bf16[128,2048]{1,0:T(8,128)(2,1)S(1)} collective-permute-done((bf16[128,2048]{1,0:T(8,128)(2,1)S(1)}, bf16[128,2048]{1,0:T(8,128)(2,1)S(1)}, u32[]{:S(2)}, u32[]{:S(2)}) %collective-permute-start.11) | collective-permute-done | bytes 524320 | tf_op jit(solution)/shard_map/ppermute | solution.py:44
  133.0 6.4 %pick_rows.4 = bf16[1,576,2048]{2,1,0:T(8,128)(2,1)} custom-call(s32[1,1,1024]{2,1,0:T(1,128)} %bitcast.349, f32[1,576,1]{2,1,0:T(8,128)} %broadcast_in_dim.78.scale_ref, bf16[4,1,128,2048]{3,2,1,0:T(8,128)(2,1)} %bitcast.316, bf16[4,1,128,2048]{3,2,1,0:T(8,128)(2,1)} %bitcast.323), custom_call_target="tpu_custom_call" | custom-call | flops 2415919104 | bytes 8053063 | tf_op jit(solution)/shard_map/pick_rows/pallas_call | solution.py:158
  139.4 19.0 %expert_forward.1 = (f32[576,1408]{1,0:T(8,128)}, f32[576,1408]{1,0:T(8,128)}, bf16[576,1408]{1,0:T(8,128)(2,1)}, bf16[576,2048]{1,0:T(8,128)(2,1)}) custom-call(bf16[576,2048]{1,0:T(8,128)(2,1)} %bitcast.319, bf16[2,2048,1408]{2,1,0:T(8,128)(2,1)} %bitcast.300, bf16[1408,2048]{1,0:T(8,128)(2,1)} %bitcast.359), custom_call_target="tpu_custom_call" | custom-call | flops 9965666304 | bytes 33218888 | tf_op jit(solution)/shard_map/expert_forward/pallas_call | solution.py:212
  166.0 5.2 multiply_convert_fusion.8
  188.4 11.7 %collective-permute-done.27 = bf16[128,2048]{1,0:T(8,128)(2,1)S(1)} collective-permute-done((bf16[128,2048]{1,0:T(8,128)(2,1)S(1)}, bf16[128,2048]{1,0:T(8,128)(2,1)S(1)}, u32[]{:S(2)}, u32[]{:S(2)}) %collective-permute-start.27) | collective-permute-done | bytes 524320 | tf_op jit(solution)/shard_map/ppermute | solution.py:44
  202.8 6.0 collective-permute-done.26
  219.2 13.7 %collective-permute-done.31 = bf16[128,2048]{1,0:T(8,128)(2,1)} collective-permute-done((bf16[128,2048]{1,0:T(8,128)(2,1)}, bf16[128,2048]{1,0:T(8,128)(2,1)}, u32[]{:S(2)}, u32[]{:S(2)}) %collective-permute-start.31) | collective-permute-done | bytes 524320 | tf_op jit(solution)/shard_map/ppermute | solution.py:119
  258.1 6.4 %pick_rows.5 = bf16[1,576,2048]{2,1,0:T(8,128)(2,1)} custom-call(s32[1,1,1024]{2,1,0:T(1,128)} %bitcast.350, f32[1,576,1]{2,1,0:T(8,128)} %broadcast_in_dim_broadcast_in_dim.4.scale_ref, bf16[4,1,128,2048]{3,2,1,0:T(8,128)(2,1)} %bitcast.317, bf16[4,1,128,2048]{3,2,1,0:T(8,128)(2,1)} %bitcast.324), custom_call_target="tpu_custom_call" | custom-call | flops 2415919104 | bytes 8053063 | tf_op jit(solution)/shard_map/pick_rows/pallas_call | solution.py:158
  264.4 21.6 %expert_back.1 = (bf16[576,1408]{1,0:T(8,128)(2,1)}, bf16[576,1408]{1,0:T(8,128)(2,1)}, bf16[576,2048]{1,0:T(8,128)(2,1)}, f32[576,1]{1,0:T(8,128)}) custom-call(bf16[576,2048]{1,0:T(8,128)(2,1)} %bitcast.321, f32[576,1408]{1,0:T(8,128)} %get-tuple-element.154.gate_ref, f32[576,1408]{1,0:T(8,128)} %get-tuple-element.155.up_ref, ...), custom_call_target="tpu_custom_call" | custom-call | flops 9965666304 | bytes 33218888 | tf_op jit(solution)/shard_map/expert_back/pallas_call | solution.py:242
  286.0 5.9 collective-permute-done.35
  309.2 10.9 %convolution_convert_fusion = bf16[2048,1408]{1,0:T(8,128)(2,1)} fusion(bf16[512,2048]{1,0:T(8,128)(2,1)} %copy-done.41, bf16[512,2048]{1,0:T(8,128)(2,1)} %copy-done.34, bf16[512,704]{0,1:T(8,128)(2,1)} %get-tuple-element.165, bf16[512,704]{0,1:T(8,128)(2,1)S(1)} %copy-done.55, bf16[512,704]{0,1:T(8,128)(2,1)} %get-tuple-element.276, ...), kind=kOutput, calls=%fused_computation.3 | convolution fusion | flops 5928386560 | bytes 12845056 | tf_op jit(solution)/shard_map/dot_general | solution.py:40
  320.1 5.9 fusion.31
  337.8 5.8 collective-permute-done.38
  354.2 10.5 %collective-permute-done.40 = bf16[3,64,2048]{2,1,0:T(8,128)(2,1)S(1)} collective-permute-done((bf16[3,64,2048]{2,1,0:T(8,128)(2,1)S(1)}, bf16[3,64,2048]{2,1,0:T(8,128)(2,1)S(1)}, u32[]{:S(2)}, u32[]{:S(2)}) %collective-permute-start.40) | collective-permute-done | bytes 786464 | tf_op jit(solution)/shard_map/ppermute | solution.py:44
  374.7 6.5 %collective-permute-done.48 = f32[5,16,128]{2,1,0:T(8,128)S(1)} collective-permute-done((f32[5,16,128]{2,1,0:T(8,128)S(1)}, f32[5,16,128]{2,1,0:T(8,128)S(1)}, u32[]{:S(2)}, u32[]{:S(2)}) %collective-permute-start.48) | collective-permute-done | bytes 40992 | tf_op jit(solution)/shard_map/ppermute | solution.py:44
  409.3 12.4 %pick_rows.6 = bf16[3,576,2048]{2,1,0:T(8,128)(2,1)} custom-call(s32[3,1,1024]{2,1,0:T(1,128)} %bitcast.334, f32[3,576,1]{2,1,0:T(8,128)} %copy.111.scale_ref, bf16[4,3,128,2048]{3,2,1,0:T(8,128)(2,1)} %pad_maximum_fusion.lower_ref, bf16[4,3,128,2048]{3,2,1,0:T(8,128)(2,1)} %collective-permute-done.44.upper_ref), custom_call_target="tpu_custom_call" | custom-call | flops 7247757312 | bytes 24159192 | tf_op jit(solution)/shard_map/pick_rows/pallas_call | solution.py:158
  425.2 5.7 collective-permute-done.46
  438.2 12.4 %pick_rows.7 = bf16[3,576,2048]{2,1,0:T(8,128)(2,1)} custom-call(s32[3,1,1024]{2,1,0:T(1,128)} %bitcast.342, f32[3,576,1]{2,1,0:T(8,128)} %broadcast_in_dim.91.scale_ref, bf16[4,3,128,2048]{3,2,1,0:T(8,128)(2,1)} %bitcast.304, bf16[4,3,128,2048]{3,2,1,0:T(8,128)(2,1)} %collective-permute-done.45.upper_ref), custom_call_target="tpu_custom_call" | custom-call | flops 7247757312 | bytes 24159192 | tf_op jit(solution)/shard_map/pick_rows/pallas_call | solution.py:158
  505.0 43.2 %expert_far.1 = (bf16[1728,1408]{1,0:T(8,128)(2,1)}, bf16[1728,1408]{1,0:T(8,128)(2,1)}, bf16[1728,1408]{1,0:T(8,128)(2,1)}) custom-call(bf16[1728,2048]{1,0:T(8,128)(2,1)} %bitcast.310, bf16[1728,2048]{1,0:T(8,128)(2,1)} %bitcast.308, bf16[2,2048,1408]{2,1,0:T(8,128)(2,1)} %bitcast.302, bf16[1408,2048]{1,0:T(8,128)(2,1)} %bitcast.361), custom_call_target="tpu_custom_call" | custom-call | flops 29896998912 | bytes 99656664 | tf_op jit(solution)/shard_map/expert_far/pallas_call | solution.py:266
  573.3 24.7 %expert_grads.1 = (f32[512,2,1408]{2,1,0:T(2,128)}, f32[1408,512]{1,0:T(8,128)}) custom-call(s32[1]{0:T(128)} %bitcast.104._, bf16[576,2048]{1,0:T(8,128)(2,1)} %bitcast.320, bf16[576,2048]{1,0:T(8,128)(2,1)} %bitcast.322, bf16[576,1408]{1,0:T(8,128)(2,1)} %get-tuple-element.156.act_ref.act, bf16[576,1408]{1,0:T(8,128)(2,1)} %get-tuple-element.204.gg, ...), custom_call_target="tpu_custom_call" | custom-call | flops 9965666304 | bytes 33218888 | tf_op jit(solution)/shard_map/expert_grads/pallas_call | solution.py:310
  (641 shorter events, 330.0 us)
Async XLA Ops:
  8.0 363.0 %all-gather.3.cloned.1.call-start = ((), (), s32[]{:S(2)}) async-start(), calls=%async_computation.8 | async-start | bytes 7864320 | tf_op jit(solution)/shard_map/all_gather | solution.py:58
  69.5 19.3 %collective-permute-start.8 = (bf16[128,2048]{1,0:T(8,128)(2,1)S(1)}, bf16[128,2048]{1,0:T(8,128)(2,1)S(1)}, u32[]{:S(2)}, u32[]{:S(2)}) collective-permute-start(bf16[128,2048]{1,0:T(8,128)(2,1)S(1)} %pad_maximum_fusion.13), channel_id=1, source_target_pairs={{0,4},{1,5},{2,6},{3,7},{4,0},{5,1},{6,2},{7,3},{8,12},{9,13},{10,... | collective-permute-start | bytes 1572872 | tf_op jit(solution)/shard_map/ppermute | solution.py:44
  122.9 48.2 %collective-permute-start.23 = (bf16[128,2048]{1,0:T(8,128)(2,1)S(1)}, bf16[128,2048]{1,0:T(8,128)(2,1)}, u32[]{:S(2)}, u32[]{:S(2)}) collective-permute-start(bf16[128,2048]{1,0:T(8,128)(2,1)S(1)} %get-tuple-element.250), channel_id=1, source_target_pairs={{16,0},{24,8},{0,16},{8,24},{17,1},{25,9},{1,17},{9,25},{18,2},{26... | collective-permute-start | bytes 1572872 | tf_op jit(solution)/shard_map/ppermute | solution.py:119
  125.6 59.1 %collective-permute-start.22 = (bf16[128,2048]{1,0:T(8,128)(2,1)S(1)}, bf16[128,2048]{1,0:T(8,128)(2,1)}, u32[]{:S(2)}, u32[]{:S(2)}) collective-permute-start(bf16[128,2048]{1,0:T(8,128)(2,1)S(1)} %get-tuple-element.250), channel_id=1, source_target_pairs={{24,0},{0,8},{8,16},{16,24},{25,1},{1,9},{9,17},{17,25},{26,2},{2,... | collective-permute-start | bytes 1572872 | tf_op jit(solution)/shard_map/ppermute | solution.py:119
  127.2 35.3 %collective-permute-start.21 = (bf16[128,2048]{1,0:T(8,128)(2,1)S(1)}, bf16[128,2048]{1,0:T(8,128)(2,1)}, u32[]{:S(2)}, u32[]{:S(2)}) collective-permute-start(bf16[128,2048]{1,0:T(8,128)(2,1)S(1)} %get-tuple-element.250), channel_id=1, source_target_pairs={{8,0},{16,8},{24,16},{0,24},{9,1},{17,9},{25,17},{1,25},{10,2},{18... | collective-permute-start | bytes 1572872 | tf_op jit(solution)/shard_map/ppermute | solution.py:119
  212.4 20.5 %collective-permute-start.31 = (bf16[128,2048]{1,0:T(8,128)(2,1)}, bf16[128,2048]{1,0:T(8,128)(2,1)}, u32[]{:S(2)}, u32[]{:S(2)}) collective-permute-start(bf16[128,2048]{1,0:T(8,128)(2,1)} %get-tuple-element.246), channel_id=1, source_target_pairs={{8,0},{16,8},{24,16},{0,24},{9,1},{17,9},{25,17},{1,25},{10,2},{18... | collective-permute-start | bytes 1572872 | tf_op jit(solution)/shard_map/ppermute | solution.py:119
  214.4 18.5 %collective-permute-start.30 = (bf16[128,2048]{1,0:T(8,128)(2,1)}, bf16[128,2048]{1,0:T(8,128)(2,1)}, u32[]{:S(2)}, u32[]{:S(2)}) collective-permute-start(bf16[128,2048]{1,0:T(8,128)(2,1)} %get-tuple-element.246), channel_id=1, source_target_pairs={{0,4},{1,5},{2,6},{3,7},{4,0},{5,1},{6,2},{7,3},{8,12},{9,13},{10,... | collective-permute-start | bytes 1572872 | tf_op jit(solution)/shard_map/ppermute | solution.py:44
  219.1 169.9 %reduce-scatter.5.cloned.1.call-start = ((), (), s32[]{:S(2)}) async-start(), calls=%async_computation.4 | async-start | bytes 3604480 | tf_op jit(solution)/shard_map/reduce_scatter | solution.py:97
  253.0 39.0 %collective-permute-start.35 = (bf16[128,2048]{1,0:T(8,128)(2,1)}, bf16[128,2048]{1,0:T(8,128)(2,1)S(1)}, u32[]{:S(2)}, u32[]{:S(2)}) collective-permute-start(bf16[128,2048]{1,0:T(8,128)(2,1)} %get-tuple-element.246), channel_id=1, source_target_pairs={{16,0},{24,8},{0,16},{8,24},{17,1},{25,9},{1,17},{9,25},{18,2},{26... | collective-permute-start | bytes 1572872 | tf_op jit(solution)/shard_map/ppermute | solution.py:119
  256.7 48.9 %collective-permute-start.36 = (bf16[128,2048]{1,0:T(8,128)(2,1)}, bf16[128,2048]{1,0:T(8,128)(2,1)}, u32[]{:S(2)}, u32[]{:S(2)}) collective-permute-start(bf16[128,2048]{1,0:T(8,128)(2,1)} %get-tuple-element.246), channel_id=1, source_target_pairs={{24,0},{0,8},{8,16},{16,24},{25,1},{1,9},{9,17},{17,25},{26,2},{2,... | collective-permute-start | bytes 1572872 | tf_op jit(solution)/shard_map/ppermute | solution.py:119
  307.2 36.4 %collective-permute-start.38 = (bf16[3,128,2048]{2,1,0:T(8,128)(2,1)S(1)}, bf16[3,128,2048]{2,1,0:T(8,128)(2,1)}, u32[]{:S(2)}, u32[]{:S(2)}) collective-permute-start(bf16[3,128,2048]{2,1,0:T(8,128)(2,1)S(1)} %pad_maximum_fusion.2), channel_id=1, source_target_pairs={{0,4},{1,5},{2,6},{3,7},{4,0},{5,1},{6,2},{7,3},{8,12},{9,13},{10,... | collective-permute-start | bytes 4718600 | tf_op jit(solution)/shard_map/ppermute | solution.py:44
  307.9 36.1 %collective-permute-start.37 = (bf16[3,128,2048]{2,1,0:T(8,128)(2,1)S(1)}, bf16[3,128,2048]{2,1,0:T(8,128)(2,1)}, u32[]{:S(2)}, u32[]{:S(2)}) collective-permute-start(bf16[3,128,2048]{2,1,0:T(8,128)(2,1)S(1)} %pad_maximum_fusion.2), channel_id=1, source_target_pairs={{0,2},{1,3},{2,0},{3,1},{4,6},{5,7},{6,4},{7,5},{8,10},{9,11},{10,... | collective-permute-start | bytes 4718600 | tf_op jit(solution)/shard_map/ppermute | solution.py:44
  326.0 175.6 %reduce-scatter.7.cloned.1.call-start = ((), (), s32[]{:S(2)}) async-start(), calls=%async_computation.5 | async-start | bytes 7208960 | tf_op jit(solution)/shard_map/reduce_scatter | solution.py:97
  346.4 18.3 %collective-permute-start.40 = (bf16[3,64,2048]{2,1,0:T(8,128)(2,1)S(1)}, bf16[3,64,2048]{2,1,0:T(8,128)(2,1)S(1)}, u32[]{:S(2)}, u32[]{:S(2)}) collective-permute-start(bf16[3,64,2048]{2,1,0:T(8,128)(2,1)S(1)} %slice.674), channel_id=1, source_target_pairs={{0,4},{1,5},{2,6},{3,7},{4,0},{5,1},{6,2},{7,3},{8,12},{9,13},{10,... | collective-permute-start | bytes 2359304 | tf_op jit(solution)/shard_map/ppermute | solution.py:44
  371.0 29.4 %collective-permute-start.44 = (bf16[4,3,128,2048]{3,2,1,0:T(8,128)(2,1)}, bf16[4,3,128,2048]{3,2,1,0:T(8,128)(2,1)}, u32[]{:S(2)}, u32[]{:S(2)}) collective-permute-start(bf16[4,3,128,2048]{3,2,1,0:T(8,128)(2,1)} %pad_maximum_fusion.lower_ref), channel_id=1, source_target_pairs={{0,1},{1,0},{2,3},{3,2},{4,5},{5,4},{6,7},{7,6},{8,9},{9,8},{10,11... | collective-permute-start | bytes 18874376 | tf_op jit(solution)/shard_map/ppermute | solution.py:44
  371.0 29.4 %collective-permute-start.45 = (bf16[4,3,128,2048]{3,2,1,0:T(8,128)(2,1)}, bf16[4,3,128,2048]{3,2,1,0:T(8,128)(2,1)}, u32[]{:S(2)}, u32[]{:S(2)}) collective-permute-start(bf16[4,3,128,2048]{3,2,1,0:T(8,128)(2,1)} %bitcast.303), channel_id=1, source_target_pairs={{0,1},{1,0},{2,3},{3,2},{4,5},{5,4},{6,7},{7,6},{8,9},{9,8},{10,11... | collective-permute-start | bytes 18874376 | tf_op jit(solution)/shard_map/ppermute | solution.py:44
  371.6 21.9 %collective-permute-start.41 = (bf16[512,2048]{1,0:T(8,128)(2,1)}, bf16[512,2048]{1,0:T(8,128)(2,1)}, u32[]{:S(2)}, u32[]{:S(2)}) collective-permute-start(bf16[512,2048]{1,0:T(8,128)(2,1)} %add_convert_fusion.3), channel_id=1, source_target_pairs={{0,1},{1,0},{2,3},{3,2},{4,5},{5,4},{6,7},{7,6},{8,9},{9,8},{10,11... | collective-permute-start | bytes 6291464 | tf_op jit(solution)/shard_map/ppermute | solution.py:44
  388.0 181.8 %reduce-scatter.11.cloned.1.call-start = ((), (), s32[]{:S(2)}) async-start(), calls=%async_computation.7 | async-start | bytes 1310720 | tf_op jit(solution)/shard_map/reduce_scatter | solution.py:97
  398.3 23.3 %collective-permute-start.42 = (bf16[128,2048]{1,0:T(8,128)(2,1)S(1)}, bf16[128,2048]{1,0:T(8,128)(2,1)S(1)}, u32[]{:S(2)}, u32[]{:S(2)}) collective-permute-start(bf16[128,2048]{1,0:T(8,128)(2,1)S(1)} %pad_maximum_fusion.16), channel_id=1, source_target_pairs={{0,2},{1,3},{2,0},{3,1},{4,6},{5,7},{6,4},{7,5},{8,10},{9,11},{10,... | collective-permute-start | bytes 1572872 | tf_op jit(solution)/shard_map/ppermute | solution.py:44
  399.8 21.9 %collective-permute-start.43 = (bf16[128,2048]{1,0:T(8,128)(2,1)S(1)}, bf16[128,2048]{1,0:T(8,128)(2,1)}, u32[]{:S(2)}, u32[]{:S(2)}) collective-permute-start(bf16[128,2048]{1,0:T(8,128)(2,1)S(1)} %pad_maximum_fusion.17), channel_id=1, source_target_pairs={{0,4},{1,5},{2,6},{3,7},{4,0},{5,1},{6,2},{7,3},{8,12},{9,13},{10,... | collective-permute-start | bytes 1572872 | tf_op jit(solution)/shard_map/ppermute | solution.py:44
  484.4 134.0 %reduce-scatter.9.cloned.1.call-start = ((), (), s32[]{:S(2)}) async-start(), calls=%async_computation.6 | async-start | bytes 3932160 | tf_op jit(solution)/shard_map/reduce_scatter | solution.py:97
  502.5 45.7 %collective-permute-start.57 = (bf16[128,2048]{1,0:T(8,128)(2,1)S(1)}, bf16[128,2048]{1,0:T(8,128)(2,1)S(1)}, u32[]{:S(2)}, u32[]{:S(2)}) collective-permute-start(bf16[128,2048]{1,0:T(8,128)(2,1)S(1)} %pad_maximum_fusion.18), channel_id=1, source_target_pairs={{0,2},{1,3},{2,0},{3,1},{4,6},{5,7},{6,4},{7,5},{8,10},{9,11},{10,... | collective-permute-start | bytes 1572872 | tf_op jit(solution)/shard_map/ppermute | solution.py:44
  503.7 44.5 %collective-permute-start.58 = (bf16[128,2048]{1,0:T(8,128)(2,1)S(1)}, bf16[128,2048]{1,0:T(8,128)(2,1)S(1)}, u32[]{:S(2)}, u32[]{:S(2)}) collective-permute-start(bf16[128,2048]{1,0:T(8,128)(2,1)S(1)} %pad_maximum_fusion.19), channel_id=1, source_target_pairs={{0,4},{1,5},{2,6},{3,7},{4,0},{5,1},{6,2},{7,3},{8,12},{9,13},{10,... | collective-permute-start | bytes 1572872 | tf_op jit(solution)/shard_map/ppermute | solution.py:44
  572.4 25.5 %collective-permute-start.62 = (f32[3,4,704]{2,1,0:T(4,128)S(1)}, f32[3,4,704]{2,1,0:T(4,128)S(1)}, u32[]{:S(2)}, u32[]{:S(2)}) collective-permute-start(f32[3,4,704]{2,1,0:T(4,128)S(1)} %pad_maximum_fusion.24), channel_id=1, source_target_pairs={{0,4},{1,5},{2,6},{3,7},{4,0},{5,1},{6,2},{7,3},{8,12},{9,13},{10,... | collective-permute-start | bytes 101384 | tf_op jit(solution)/shard_map/ppermute | solution.py:44
  (153 other events, 1563.0 us)
Sparse Core Ops, SparseCore 0:
  219.3 81.2 all-gather.2
Sparse Core Ops, SparseCore 1:
  326.1 53.5 reduce-scatter.4
  388.0 98.6 reduce-scatter.6
  489.5 27.7 reduce-scatter.10
  550.3 57.9 reduce-scatter.8

commit v6 on v5

--- a/solution.py
+++ b/solution.py
@@ -607,7 +607,6 @@
     grad_logits = gains - my_probs * jnp.sum(gains, axis=1, keepdims=True)
     steer = jnp.concatenate([grad_logits, grad_switch[:, None]], axis=1)
     if wide:
-        (back_lower,), (far_diag,) = after((back_lower,), (far_diag,))
         error_far = jnp.stack([far_own, far_x, far_y, far_diag], 0)
         error_far = (error_far, swap(error_far, 1))
         two_far = (two_side, swap(two_side, 1))

time: 641 us -> 653 us (1.019)
  matrix products: 112 us -> 121 us
    dot_general x51, matrix products: 111 us -> 120 us  [dot(): lax.dot_general(left, right, (dims, ((), ())), preferred_element_type=F32)]
    unnamed x230 -> x224, local copies, waits for them, and re-layouts: 35.1 us -> 34.9 us
  transfers between devices with their start and end apart: 72 -> 72, of which waited for: 36 -> 33; matrix products, arithmetic and copies ran while one was open for 32% -> 33% of each run, Pallas kernels for 23% -> 23%
where the time goes in v6:
time: 653 us; the launch traced here: 642 us
  waiting for transfers between devices  152 us (23%)
  Pallas kernels  146 us (22%)
  matrix products  121 us (19%)
  starting transfers between devices  70.9 us (11%)
  other arithmetic  70.2 us (11%)
  local copies, waits for them, and re-layouts  59.4 us (9%)
  between operations  22.2 us (3%)
    ppermute x55, waiting for transfers between devices, swap(): return lax.ppermute(values, 'sp', [(i, i ^ distance) for i in range(8)])  128 us
    dot_general x51, matrix products, dot(): lax.dot_general(left, right, (dims, ((), ())), preferred_element_type=F32)  120 us
    ppermute x55, starting transfers between devices, swap(): return lax.ppermute(values, 'sp', [(i, i ^ distance) for i in range(8)])  49 us
    pallas_call x1, Pallas kernels, expert_far(): local_call(expert_far_kernel, 'expert_far', 6 * count * width * hidden, g...  43.3 us
    pallas_call x4, Pallas kernels, pick_rows(): local_call(pick_kernel, 'pick_rows', 2 * groups * capacity * total * widt...  37.5 us
    unnamed x224, local copies, waits for them, and re-layouts  34.9 us
    pallas_call x1, Pallas kernels, expert_grads_of(): local_call(expert_grad_kernel, 'expert_grads', 6 * count * steps * share...  24.4 us
    ppermute x9, waiting for transfers between devices, fetch_groups(): lax.ppermute(moved[0], 'dp', [((i + k) % size, i) for i in range(size)])  23.7 us
  transfers between devices with their start and end apart: 72, of which 33 were waited for; matrix products, arithmetic and copies ran while one was open for 33% of the time, Pallas kernels for 23%

profile of v6, /device:TPU:0, one launch (start us, length us, event | category | flops | bytes accessed | tf_op | source)
XLA Modules:
  0.0 641.8 jit_solution(7312201163517188926)
XLA Ops:
  18.4 11.4 %copy.127 = bf16[1,2048,2,1408]{3,1,2,0:T(8,128)(2,1)} copy(bf16[1,2048,2,1408]{3,2,1,0:T(2,128)(2,1)} %param.38) | data formatting | bytes 23068672 | tf_op args[13]
  70.2 9.7 %collective-permute-done.6 = bf16[128,2048]{1,0:T(8,128)(2,1)S(1)} collective-permute-done((bf16[128,2048]{1,0:T(8,128)(2,1)S(1)}, bf16[128,2048]{1,0:T(8,128)(2,1)S(1)}, u32[]{:S(2)}, u32[]{:S(2)}) %collective-permute-start.6) | collective-permute-done | bytes 524320 | tf_op jit(solution)/shard_map/ppermute | solution.py:44
  82.0 5.6 collective-permute-done.16
  91.9 6.8 %collective-permute-done.9 = bf16[64,2048]{1,0:T(8,128)(2,1)} collective-permute-done((bf16[64,2048]{1,0:T(8,128)(2,1)}, bf16[64,2048]{1,0:T(8,128)(2,1)}, u32[]{:S(2)}, u32[]{:S(2)}) %collective-permute-start.9) | collective-permute-done | bytes 262176 | tf_op jit(solution)/shard_map/ppermute | solution.py:44
  104.5 10.3 %collective-permute-done.11 = bf16[128,2048]{1,0:T(8,128)(2,1)S(1)} collective-permute-done((bf16[128,2048]{1,0:T(8,128)(2,1)S(1)}, bf16[128,2048]{1,0:T(8,128)(2,1)S(1)}, u32[]{:S(2)}, u32[]{:S(2)}) %collective-permute-start.11) | collective-permute-done | bytes 524320 | tf_op jit(solution)/shard_map/ppermute | solution.py:44
  133.1 6.4 pick_rows.4
  139.5 19.0 %expert_forward.1 = (f32[576,1408]{1,0:T(8,128)}, f32[576,1408]{1,0:T(8,128)}, bf16[576,1408]{1,0:T(8,128)(2,1)}, bf16[576,2048]{1,0:T(8,128)(2,1)}) custom-call(bf16[576,2048]{1,0:T(8,128)(2,1)} %bitcast.317, bf16[2,2048,1408]{2,1,0:T(8,128)(2,1)} %bitcast.299, bf16[1408,2048]{1,0:T(8,128)(2,1)} %bitcast.357), custom_call_target="tpu_custom_call" | custom-call | flops 9965666304 | bytes 33218888 | tf_op jit(solution)/shard_map/expert_forward/pallas_call | solution.py:212
  188.5 11.7 %collective-permute-done.27 = bf16[128,2048]{1,0:T(8,128)(2,1)S(1)} collective-permute-done((bf16[128,2048]{1,0:T(8,128)(2,1)S(1)}, bf16[128,2048]{1,0:T(8,128)(2,1)S(1)}, u32[]{:S(2)}, u32[]{:S(2)}) %collective-permute-start.27) | collective-permute-done | bytes 524320 | tf_op jit(solution)/shard_map/ppermute | solution.py:44
  203.0 6.0 collective-permute-done.26
  219.3 13.7 %collective-permute-done.31 = bf16[128,2048]{1,0:T(8,128)(2,1)} collective-permute-done((bf16[128,2048]{1,0:T(8,128)(2,1)}, bf16[128,2048]{1,0:T(8,128)(2,1)}, u32[]{:S(2)}, u32[]{:S(2)}) %collective-permute-start.31) | collective-permute-done | bytes 524320 | tf_op jit(solution)/shard_map/ppermute | solution.py:119
  258.2 6.4 pick_rows.5
  264.5 21.6 %expert_back.1 = (bf16[576,1408]{1,0:T(8,128)(2,1)}, bf16[576,1408]{1,0:T(8,128)(2,1)}, bf16[576,2048]{1,0:T(8,128)(2,1)}, f32[576,1]{1,0:T(8,128)}) custom-call(bf16[576,2048]{1,0:T(8,128)(2,1)} %bitcast.319, f32[576,1408]{1,0:T(8,128)} %get-tuple-element.152.gate_ref, f32[576,1408]{1,0:T(8,128)} %get-tuple-element.153.up_ref, ...), custom_call_target="tpu_custom_call" | custom-call | flops 9965666304 | bytes 33218888 | tf_op jit(solution)/shard_map/expert_back/pallas_call | solution.py:242
  286.2 5.9 collective-permute-done.35
  309.3 10.9 %convolution_convert_fusion = bf16[2048,1408]{1,0:T(8,128)(2,1)} fusion(bf16[512,2048]{1,0:T(8,128)(2,1)} %copy-done.40, bf16[512,2048]{1,0:T(8,128)(2,1)} %copy-done.33, bf16[512,704]{0,1:T(8,128)(2,1)} %get-tuple-element.163, bf16[512,704]{0,1:T(8,128)(2,1)S(1)} %copy-done.54, bf16[512,704]{0,1:T(8,128)(2,1)} %get-tuple-element.272, ...), kind=kOutput, calls=%fused_computation.3 | convolution fusion | flops 5928386560 | bytes 12845056 | tf_op jit(solution)/shard_map/dot_general | solution.py:40
  332.1 11.6 %collective-permute-done.38 = bf16[3,128,2048]{2,1,0:T(8,128)(2,1)} collective-permute-done((bf16[3,128,2048]{2,1,0:T(8,128)(2,1)S(1)}, bf16[3,128,2048]{2,1,0:T(8,128)(2,1)}, u32[]{:S(2)}, u32[]{:S(2)}) %collective-permute-start.38) | collective-permute-done | bytes 1572896 | tf_op jit(solution)/shard_map/ppermute | solution.py:44
  349.4 15.5 %collective-permute-done.42 = bf16[3,64,2048]{2,1,0:T(8,128)(2,1)S(1)} collective-permute-done((bf16[3,64,2048]{2,1,0:T(8,128)(2,1)S(1)}, bf16[3,64,2048]{2,1,0:T(8,128)(2,1)S(1)}, u32[]{:S(2)}, u32[]{:S(2)}) %collective-permute-start.42) | collective-permute-done | bytes 786464 | tf_op jit(solution)/shard_map/ppermute | solution.py:44
  365.9 5.4 pad_maximum_fusion.lower_ref
  383.2 5.8 fusion.31
  389.8 5.5 fusion.23
  395.5 8.3 %add_convert_fusion.2 = bf16[512,2048]{1,0:T(8,128)(2,1)} fusion(f32[512,2048]{1,0:T(8,128)} %fusion.31, f32[512,2048]{1,0:T(8,128)} %fusion.23, bf16[576,2048]{1,0:T(8,128)(2,1)} %get-tuple-element.165, bf16[576,1024]{1,0:T(8,128)(2,1)S(1)} %copy-done.10), kind=kOutput, calls=%fused_computation.23 | convolution fusion | flops 1211105280 | bytes 13434880 | tf_op jit(solution)/shard_map/dot_general | solution.py:40
  421.0 12.5 %pick_rows.6 = bf16[3,576,2048]{2,1,0:T(8,128)(2,1)} custom-call(s32[3,1,1024]{2,1,0:T(1,128)} %bitcast.332, f32[3,576,1]{2,1,0:T(8,128)} %copy.111.scale_ref, bf16[4,3,128,2048]{3,2,1,0:T(8,128)(2,1)} %pad_maximum_fusion.lower_ref, bf16[4,3,128,2048]{3,2,1,0:T(8,128)(2,1)} %collective-permute-done.44.upper_ref), custom_call_target="tpu_custom_call" | custom-call | flops 7247757312 | bytes 24159192 | tf_op jit(solution)/shard_map/pick_rows/pallas_call | solution.py:158
  450.6 12.2 %pick_rows.7 = bf16[3,576,2048]{2,1,0:T(8,128)(2,1)} custom-call(s32[3,1,1024]{2,1,0:T(1,128)} %bitcast.340, f32[3,576,1]{2,1,0:T(8,128)} %broadcast_in_dim.91.scale_ref, bf16[4,3,128,2048]{3,2,1,0:T(8,128)(2,1)} %bitcast.303, bf16[4,3,128,2048]{3,2,1,0:T(8,128)(2,1)} %collective-permute-done.45.upper_ref), custom_call_target="tpu_custom_call" | custom-call | flops 7247757312 | bytes 24159192 | tf_op jit(solution)/shard_map/pick_rows/pallas_call | solution.py:158
  517.5 43.3 %expert_far.1 = (bf16[1728,1408]{1,0:T(8,128)(2,1)}, bf16[1728,1408]{1,0:T(8,128)(2,1)}, bf16[1728,1408]{1,0:T(8,128)(2,1)}) custom-call(bf16[1728,2048]{1,0:T(8,128)(2,1)} %bitcast.309, bf16[1728,2048]{1,0:T(8,128)(2,1)} %bitcast.307, bf16[2,2048,1408]{2,1,0:T(8,128)(2,1)} %bitcast.301, bf16[1408,2048]{1,0:T(8,128)(2,1)} %bitcast.359), custom_call_target="tpu_custom_call" | custom-call | flops 29896998912 | bytes 99656664 | tf_op jit(solution)/shard_map/expert_far/pallas_call | solution.py:266
  585.4 24.4 %expert_grads.1 = (f32[512,2,1408]{2,1,0:T(2,128)}, f32[1408,512]{1,0:T(8,128)}) custom-call(s32[1]{0:T(128)} %bitcast.104._, bf16[576,2048]{1,0:T(8,128)(2,1)} %bitcast.318, bf16[576,2048]{1,0:T(8,128)(2,1)} %bitcast.320, bf16[576,1408]{1,0:T(8,128)(2,1)} %get-tuple-element.154.act_ref.act, bf16[576,1408]{1,0:T(8,128)(2,1)} %get-tuple-element.200.gg, ...), custom_call_target="tpu_custom_call" | custom-call | flops 9965666304 | bytes 33218888 | tf_op jit(solution)/shard_map/expert_grads/pallas_call | solution.py:310
  (634 shorter events, 329.5 us)
Async XLA Ops:
  8.0 363.4 %all-gather.3.cloned.1.call-start = ((), (), s32[]{:S(2)}) async-start(), calls=%async_computation.8 | async-start | bytes 7864320 | tf_op jit(solution)/shard_map/all_gather | solution.py:58
  69.6 19.3 %collective-permute-start.8 = (bf16[128,2048]{1,0:T(8,128)(2,1)S(1)}, bf16[128,2048]{1,0:T(8,128)(2,1)S(1)}, u32[]{:S(2)}, u32[]{:S(2)}) collective-permute-start(bf16[128,2048]{1,0:T(8,128)(2,1)S(1)} %pad_maximum_fusion.12), channel_id=1, source_target_pairs={{0,4},{1,5},{2,6},{3,7},{4,0},{5,1},{6,2},{7,3},{8,12},{9,13},{10,... | collective-permute-start | bytes 1572872 | tf_op jit(solution)/shard_map/ppermute | solution.py:44
  123.1 48.2 %collective-permute-start.23 = (bf16[128,2048]{1,0:T(8,128)(2,1)S(1)}, bf16[128,2048]{1,0:T(8,128)(2,1)}, u32[]{:S(2)}, u32[]{:S(2)}) collective-permute-start(bf16[128,2048]{1,0:T(8,128)(2,1)S(1)} %get-tuple-element.246), channel_id=1, source_target_pairs={{16,0},{24,8},{0,16},{8,24},{17,1},{25,9},{1,17},{9,25},{18,2},{26... | collective-permute-start | bytes 1572872 | tf_op jit(solution)/shard_map/ppermute | solution.py:119
  125.7 59.1 %collective-permute-start.22 = (bf16[128,2048]{1,0:T(8,128)(2,1)S(1)}, bf16[128,2048]{1,0:T(8,128)(2,1)}, u32[]{:S(2)}, u32[]{:S(2)}) collective-permute-start(bf16[128,2048]{1,0:T(8,128)(2,1)S(1)} %get-tuple-element.246), channel_id=1, source_target_pairs={{24,0},{0,8},{8,16},{16,24},{25,1},{1,9},{9,17},{17,25},{26,2},{2,... | collective-permute-start | bytes 1572872 | tf_op jit(solution)/shard_map/ppermute | solution.py:119
  127.3 35.3 %collective-permute-start.21 = (bf16[128,2048]{1,0:T(8,128)(2,1)S(1)}, bf16[128,2048]{1,0:T(8,128)(2,1)}, u32[]{:S(2)}, u32[]{:S(2)}) collective-permute-start(bf16[128,2048]{1,0:T(8,128)(2,1)S(1)} %get-tuple-element.246), channel_id=1, source_target_pairs={{8,0},{16,8},{24,16},{0,24},{9,1},{17,9},{25,17},{1,25},{10,2},{18... | collective-permute-start | bytes 1572872 | tf_op jit(solution)/shard_map/ppermute | solution.py:119
  212.6 20.5 %collective-permute-start.31 = (bf16[128,2048]{1,0:T(8,128)(2,1)}, bf16[128,2048]{1,0:T(8,128)(2,1)}, u32[]{:S(2)}, u32[]{:S(2)}) collective-permute-start(bf16[128,2048]{1,0:T(8,128)(2,1)} %get-tuple-element.242), channel_id=1, source_target_pairs={{8,0},{16,8},{24,16},{0,24},{9,1},{17,9},{25,17},{1,25},{10,2},{18... | collective-permute-start | bytes 1572872 | tf_op jit(solution)/shard_map/ppermute | solution.py:119
  214.6 18.5 %collective-permute-start.30 = (bf16[128,2048]{1,0:T(8,128)(2,1)}, bf16[128,2048]{1,0:T(8,128)(2,1)}, u32[]{:S(2)}, u32[]{:S(2)}) collective-permute-start(bf16[128,2048]{1,0:T(8,128)(2,1)} %get-tuple-element.242), channel_id=1, source_target_pairs={{0,4},{1,5},{2,6},{3,7},{4,0},{5,1},{6,2},{7,3},{8,12},{9,13},{10,... | collective-permute-start | bytes 1572872 | tf_op jit(solution)/shard_map/ppermute | solution.py:44
  219.3 184.6 %reduce-scatter.5.cloned.1.call-start = ((), (), s32[]{:S(2)}) async-start(), calls=%async_computation.4 | async-start | bytes 3604480 | tf_op jit(solution)/shard_map/reduce_scatter | solution.py:97
  253.1 39.0 %collective-permute-start.35 = (bf16[128,2048]{1,0:T(8,128)(2,1)}, bf16[128,2048]{1,0:T(8,128)(2,1)S(1)}, u32[]{:S(2)}, u32[]{:S(2)}) collective-permute-start(bf16[128,2048]{1,0:T(8,128)(2,1)} %get-tuple-element.242), channel_id=1, source_target_pairs={{16,0},{24,8},{0,16},{8,24},{17,1},{25,9},{1,17},{9,25},{18,2},{26... | collective-permute-start | bytes 1572872 | tf_op jit(solution)/shard_map/ppermute | solution.py:119
  256.8 48.9 %collective-permute-start.36 = (bf16[128,2048]{1,0:T(8,128)(2,1)}, bf16[128,2048]{1,0:T(8,128)(2,1)}, u32[]{:S(2)}, u32[]{:S(2)}) collective-permute-start(bf16[128,2048]{1,0:T(8,128)(2,1)} %get-tuple-element.242), channel_id=1, source_target_pairs={{24,0},{0,8},{8,16},{16,24},{25,1},{1,9},{9,17},{17,25},{26,2},{2,... | collective-permute-start | bytes 1572872 | tf_op jit(solution)/shard_map/ppermute | solution.py:119
  307.3 36.4 %collective-permute-start.38 = (bf16[3,128,2048]{2,1,0:T(8,128)(2,1)S(1)}, bf16[3,128,2048]{2,1,0:T(8,128)(2,1)}, u32[]{:S(2)}, u32[]{:S(2)}) collective-permute-start(bf16[3,128,2048]{2,1,0:T(8,128)(2,1)S(1)} %pad_maximum_fusion.2), channel_id=1, source_target_pairs={{0,4},{1,5},{2,6},{3,7},{4,0},{5,1},{6,2},{7,3},{8,12},{9,13},{10,... | collective-permute-start | bytes 4718600 | tf_op jit(solution)/shard_map/ppermute | solution.py:44
  308.1 36.1 %collective-permute-start.37 = (bf16[3,128,2048]{2,1,0:T(8,128)(2,1)S(1)}, bf16[3,128,2048]{2,1,0:T(8,128)(2,1)}, u32[]{:S(2)}, u32[]{:S(2)}) collective-permute-start(bf16[3,128,2048]{2,1,0:T(8,128)(2,1)S(1)} %pad_maximum_fusion.2), channel_id=1, source_target_pairs={{0,2},{1,3},{2,0},{3,1},{4,6},{5,7},{6,4},{7,5},{8,10},{9,11},{10,... | collective-permute-start | bytes 4718600 | tf_op jit(solution)/shard_map/ppermute | solution.py:44
  320.2 193.4 %reduce-scatter.7.cloned.1.call-start = ((), (), s32[]{:S(2)}) async-start(), calls=%async_computation.5 | async-start | bytes 7208960 | tf_op jit(solution)/shard_map/reduce_scatter | solution.py:97
  346.5 18.3 %collective-permute-start.42 = (bf16[3,64,2048]{2,1,0:T(8,128)(2,1)S(1)}, bf16[3,64,2048]{2,1,0:T(8,128)(2,1)S(1)}, u32[]{:S(2)}, u32[]{:S(2)}) collective-permute-start(bf16[3,64,2048]{2,1,0:T(8,128)(2,1)S(1)} %slice.681), channel_id=1, source_target_pairs={{0,2},{1,3},{2,0},{3,1},{4,6},{5,7},{6,4},{7,5},{8,10},{9,11},{10,... | collective-permute-start | bytes 2359304 | tf_op jit(solution)/shard_map/ppermute | solution.py:44
  347.9 17.9 %collective-permute-start.43 = (bf16[3,64,2048]{2,1,0:T(8,128)(2,1)S(1)}, bf16[3,64,2048]{2,1,0:T(8,128)(2,1)S(1)}, u32[]{:S(2)}, u32[]{:S(2)}) collective-permute-start(bf16[3,64,2048]{2,1,0:T(8,128)(2,1)S(1)} %slice.682), channel_id=1, source_target_pairs={{0,4},{1,5},{2,6},{3,7},{4,0},{5,1},{6,2},{7,3},{8,12},{9,13},{10,... | collective-permute-start | bytes 2359304 | tf_op jit(solution)/shard_map/ppermute | solution.py:44
  371.4 40.9 %collective-permute-start.44 = (bf16[4,3,128,2048]{3,2,1,0:T(8,128)(2,1)}, bf16[4,3,128,2048]{3,2,1,0:T(8,128)(2,1)}, u32[]{:S(2)}, u32[]{:S(2)}) collective-permute-start(bf16[4,3,128,2048]{3,2,1,0:T(8,128)(2,1)} %pad_maximum_fusion.lower_ref), channel_id=1, source_target_pairs={{0,1},{1,0},{2,3},{3,2},{4,5},{5,4},{6,7},{7,6},{8,9},{9,8},{10,11... | collective-permute-start | bytes 18874376 | tf_op jit(solution)/shard_map/ppermute | solution.py:44
  371.4 40.9 %collective-permute-start.45 = (bf16[4,3,128,2048]{3,2,1,0:T(8,128)(2,1)}, bf16[4,3,128,2048]{3,2,1,0:T(8,128)(2,1)}, u32[]{:S(2)}, u32[]{:S(2)}) collective-permute-start(bf16[4,3,128,2048]{3,2,1,0:T(8,128)(2,1)} %bitcast.302), channel_id=1, source_target_pairs={{0,1},{1,0},{2,3},{3,2},{4,5},{5,4},{6,7},{7,6},{8,9},{9,8},{10,11... | collective-permute-start | bytes 18874376 | tf_op jit(solution)/shard_map/ppermute | solution.py:44
  395.4 186.8 %reduce-scatter.11.cloned.1.call-start = ((), (), s32[]{:S(2)}) async-start(), calls=%async_computation.7 | async-start | bytes 1310720 | tf_op jit(solution)/shard_map/reduce_scatter | solution.py:97
  411.2 22.3 %collective-permute-start.40 = (bf16[128,2048]{1,0:T(8,128)(2,1)S(1)}, bf16[128,2048]{1,0:T(8,128)(2,1)S(1)}, u32[]{:S(2)}, u32[]{:S(2)}) collective-permute-start(bf16[128,2048]{1,0:T(8,128)(2,1)S(1)} %pad_maximum_fusion.15), channel_id=1, source_target_pairs={{0,2},{1,3},{2,0},{3,1},{4,6},{5,7},{6,4},{7,5},{8,10},{9,11},{10,... | collective-permute-start | bytes 1572872 | tf_op jit(solution)/shard_map/ppermute | solution.py:44
  412.1 21.4 %collective-permute-start.41 = (bf16[128,2048]{1,0:T(8,128)(2,1)S(1)}, bf16[128,2048]{1,0:T(8,128)(2,1)}, u32[]{:S(2)}, u32[]{:S(2)}) collective-permute-start(bf16[128,2048]{1,0:T(8,128)(2,1)S(1)} %pad_maximum_fusion.16), channel_id=1, source_target_pairs={{0,4},{1,5},{2,6},{3,7},{4,0},{5,1},{6,2},{7,3},{8,12},{9,13},{10,... | collective-permute-start | bytes 1572872 | tf_op jit(solution)/shard_map/ppermute | solution.py:44
  496.5 133.9 %reduce-scatter.9.cloned.1.call-start = ((), (), s32[]{:S(2)}) async-start(), calls=%async_computation.6 | async-start | bytes 3932160 | tf_op jit(solution)/shard_map/reduce_scatter | solution.py:97
  514.7 46.1 %collective-permute-start.57 = (bf16[128,2048]{1,0:T(8,128)(2,1)S(1)}, bf16[128,2048]{1,0:T(8,128)(2,1)S(1)}, u32[]{:S(2)}, u32[]{:S(2)}) collective-permute-start(bf16[128,2048]{1,0:T(8,128)(2,1)S(1)} %pad_maximum_fusion.17), channel_id=1, source_target_pairs={{0,2},{1,3},{2,0},{3,1},{4,6},{5,7},{6,4},{7,5},{8,10},{9,11},{10,... | collective-permute-start | bytes 1572872 | tf_op jit(solution)/shard_map/ppermute | solution.py:44
  515.9 44.9 %collective-permute-start.58 = (bf16[128,2048]{1,0:T(8,128)(2,1)S(1)}, bf16[128,2048]{1,0:T(8,128)(2,1)S(1)}, u32[]{:S(2)}, u32[]{:S(2)}) collective-permute-start(bf16[128,2048]{1,0:T(8,128)(2,1)S(1)} %pad_maximum_fusion.18), channel_id=1, source_target_pairs={{0,4},{1,5},{2,6},{3,7},{4,0},{5,1},{6,2},{7,3},{8,12},{9,13},{10,... | collective-permute-start | bytes 1572872 | tf_op jit(solution)/shard_map/ppermute | solution.py:44
  584.9 25.0 %collective-permute-start.62 = (f32[3,4,704]{2,1,0:T(4,128)S(1)}, f32[3,4,704]{2,1,0:T(4,128)S(1)}, u32[]{:S(2)}, u32[]{:S(2)}) collective-permute-start(f32[3,4,704]{2,1,0:T(4,128)S(1)} %pad_maximum_fusion.23), channel_id=1, source_target_pairs={{0,4},{1,5},{2,6},{3,7},{4,0},{5,1},{6,2},{7,3},{8,12},{9,13},{10,... | collective-permute-start | bytes 101384 | tf_op jit(solution)/shard_map/ppermute | solution.py:44
  (150 other events, 1533.4 us)
Sparse Core Ops, SparseCore 0:
  219.4 81.2 all-gather.2
Sparse Core Ops, SparseCore 1:
  320.3 53.5 reduce-scatter.4
  395.5 99.3 reduce-scatter.6
  497.6 27.6 reduce-scatter.10
  562.6 57.9 reduce-scatter.8
